TPU v7x, 32 devices: a whole 2x2x4 slice. The times are simulated.
32 devices in a mesh: dp: 8 (over z, x), chan: 4 (over y, core).
Axes of the slice: x: 2, y: 2, z: 4, core: 2. Of those that a mesh axis runs over, the one named last changes fastest.
Arguments:
- tokens: bfloat16 [32768, 768], P('dp', 'chan'), may hold values from -6 to 6
- norm1_gain: bfloat16 [768], P('chan'), may hold values from 0.099609375 to 1.8984375
- norm1_bias: bfloat16 [768], P('chan'), may hold values from -3 to 3
- qkv_weight: bfloat16 [3, 768, 768], P(None, None, 'chan'), may hold values from -0.21875 to 0.21875
- qv_bias: bfloat16 [2, 768], P(None, 'chan'), may hold values from -3 to 3
- pair_bias: bfloat16 [1024, 1024], replicated, may hold values from 0 to 4
- out_weight: bfloat16 [768, 768], P('chan'), may hold values from -2.5 to 2.5
- out_bias: bfloat16 [768], P('chan'), may hold values from -2 to 2
- norm2_gain: bfloat16 [768], P('chan'), may hold values from 0.099609375 to 1.8984375
- norm2_bias: bfloat16 [768], P('chan'), may hold values from -3 to 3
- up_weight: bfloat16 [768, 3072], P(None, 'chan'), may hold values from -0.21875 to 0.21875
- up_bias: bfloat16 [3072], P('chan'), may hold values from -3 to 3
- down_weight: bfloat16 [3072, 768], P('chan'), may hold values from -0.109375 to 0.109375
- down_bias: bfloat16 [768], P('chan'), may hold values from -2 to 2
- lengths: int32 [16], P('dp'), may hold values from 64 to 2048, as said below
- cotangent: bfloat16 [32768, 768], P('dp', 'chan'), may hold values from -6 to 6
Outputs:
- layer_out: bfloat16 [32768, 768], P('dp', 'chan')
- input_grad: bfloat16 [32768, 768], P('dp', 'chan')
- norm1_gain_grad: float32 [768], P('chan')
- norm1_bias_grad: float32 [768], P('chan')
- qkv_weight_grad: float32 [3, 768, 768], P(None, None, 'chan')
- qv_bias_grad: float32 [2, 768], P(None, 'chan')
- pair_bias_grad: float32 [1024, 1024], replicated
- out_weight_grad: float32 [768, 768], P('chan')
- out_bias_grad: float32 [768], P('chan')
- norm2_gain_grad: float32 [768], P('chan')
- norm2_bias_grad: float32 [768], P('chan')
- up_weight_grad: float32 [768, 3072], P(None, 'chan')
- up_bias_grad: float32 [3072], P('chan')
- down_weight_grad: float32 [3072, 768], P('chan')
- down_bias_grad: float32 [768], P('chan')
Inputs may be any that keep to these rules, and one draw needn't show every extreme that they name: `lengths`: each index of dp holds 2 whole sequences in a row, padded to 2048 rows each; in every such group one sequence is exactly 2048 long.
All inputs are finite; a program needn't handle non-finite values.
Results may differ from a plain program's by a relative error of at most 0.0089.
Values may be sent and summed in bfloat16 or wider, within the bound.
No kernel may reach another device: no remote copies, remote signals or barrier semaphores. Data moves between devices by JAX's collectives and lax.ppermute only.
A program may use at most 256 MiB of HBM per device.

v0:
```python
import jax
import jax.numpy as jnp
from jax import lax
from jax.sharding import PartitionSpec as P

D = 768
PAIR = 1024
WIN = 256
BLOCK = 512
LEN = 2048


EPSILON = 1e-05


def gelu_tanh(values):
    return jax.nn.gelu(values, approximate=True)


def band_rows():
    row_ids = lax.broadcasted_iota(jnp.int32, (BLOCK, PAIR), 0)
    col_ids = lax.broadcasted_iota(jnp.int32, (BLOCK, PAIR), 1)
    return (jnp.abs(row_ids + WIN - col_ids) < WIN).astype(jnp.float32)


def row_totals(first_sum, second_sum):
    return lax.psum((first_sum, second_sum), "chan")


def back_totals(first_sum, second_sum):
    return (
        lax.psum(first_sum.astype(jnp.bfloat16), "chan").astype(jnp.float32),
        lax.psum(second_sum.astype(jnp.bfloat16), "chan").astype(jnp.float32),
    )


def spread_rows(values):
    return lax.all_gather(values, "chan", axis=1, tiled=True)


def gather_grads(values):
    return lax.all_gather(values, "chan", axis=1, tiled=True)


def fold_rows(values):
    return lax.psum_scatter(values, "chan", scatter_dimension=1, tiled=True)


def norm_forward(values, gain_vals, shift_vals, totals):
    plain_sum, squares = totals(jnp.sum(values, axis=1), jnp.sum(values * values, axis=1))
    row_mean = (plain_sum / D)[:, None]
    spread = (squares / D)[:, None] - row_mean * row_mean
    inv_scale = lax.rsqrt(spread + EPSILON)
    centred = (values - row_mean) * inv_scale
    return (centred, inv_scale, centred * gain_vals + shift_vals)


def norm_backward(grad_out, centred, inv_scale, gain_vals, totals):
    scaled = grad_out * gain_vals
    plain_sum, crossed = totals(jnp.sum(scaled, axis=1), jnp.sum(scaled * centred, axis=1))
    grad_in = inv_scale * (scaled - (plain_sum / D)[:, None] - centred * (crossed / D)[:, None])
    return (grad_in, jnp.sum(grad_out * centred, axis=0), jnp.sum(grad_out, axis=0))


def bias_rows(pair_vals, row_start):
    anchor = jnp.int32(0)
    rows_of = lax.dynamic_slice(pair_vals, (row_start % PAIR, anchor), (BLOCK, PAIR))
    return jnp.roll(rows_of, WIN - row_start, axis=1)


def window_products(stacked_pad, pair_vals, band_mask):
    per_seq = LEN // BLOCK
    seq_count = stacked_pad.shape[0]
    span = stacked_pad.shape[2]
    anchor = jnp.int32(0)

    def one_block(block_id):
        seq_id = block_id // per_seq
        row_start = block_id % per_seq * BLOCK

        def compute():
            extent = lax.dynamic_slice(stacked_pad, (seq_id, row_start, anchor), (1, PAIR, span))[0]
            weights = (band_mask * (jnp.exp(bias_rows(pair_vals, row_start)) - 1.0)).astype(
                jnp.bfloat16
            )
            return jnp.dot(weights, extent, preferred_element_type=jnp.float32)

        block_out = compute()
        return block_out

    blocks = lax.map(one_block, jnp.arange(seq_count * per_seq, dtype=jnp.int32))
    return blocks.reshape(seq_count, LEN, span)


def window_back(grads_pad, stacked_pad, pair_vals, band_mask):
    per_seq = LEN // BLOCK
    seq_count = stacked_pad.shape[0]
    span = stacked_pad.shape[2]
    anchor = jnp.int32(0)

    def one_block(pair_sum, block_id):
        seq_id = block_id // per_seq
        row_start = block_id % per_seq * BLOCK

        def compute():
            grad_ext = lax.dynamic_slice(grads_pad, (seq_id, row_start, anchor), (1, PAIR, span))[0]
            grad_own = lax.dynamic_slice(
                grads_pad, (seq_id, row_start + WIN, anchor), (1, BLOCK, span)
            )[0]
            data_ext = lax.dynamic_slice(stacked_pad, (seq_id, row_start, anchor), (1, PAIR, span))[
                0
            ]
            cols_of = lax.dynamic_slice(pair_vals, (anchor, row_start % PAIR), (PAIR, BLOCK))
            turned = jnp.roll(cols_of, WIN - row_start, axis=0)
            weights_t = (band_mask.T * (jnp.exp(turned) - 1.0)).astype(jnp.bfloat16)
            into_cols = jnp.einsum(
                "rb,rk->bk", weights_t, grad_ext, preferred_element_type=jnp.float32
            )
            shifted = bias_rows(pair_vals, row_start)
            pair_terms = jnp.einsum(
                "bk,rk->br", grad_own, data_ext, preferred_element_type=jnp.float32
            )
            pair_terms = pair_terms * band_mask * jnp.exp(shifted)
            return (into_cols, jnp.roll(pair_terms, row_start - WIN, axis=1))

        into_cols, placed = compute()
        row_base = row_start % PAIR
        current = lax.dynamic_slice(pair_sum, (row_base, anchor), (BLOCK, PAIR))
        pair_sum = lax.dynamic_update_slice(pair_sum, current + placed, (row_base, anchor))
        return (pair_sum, into_cols)

    pair_sum, columns = lax.scan(
        one_block,
        jnp.zeros((PAIR, PAIR), jnp.float32),
        jnp.arange(seq_count * per_seq, dtype=jnp.int32),
    )
    return (pair_sum, columns.reshape(seq_count, LEN, span))


def body(
    tokens,
    norm1_gain,
    norm1_bias,
    qkv_weight,
    qv_bias,
    pair_bias,
    out_weight,
    out_bias,
    norm2_gain,
    norm2_bias,
    up_weight,
    up_bias,
    down_weight,
    down_bias,
    lengths,
    cotangent,
):
    seq_count = lengths.shape[0]
    row_count = tokens.shape[0]
    chan_width = tokens.shape[1]
    band_mask = band_rows()
    pair_vals = pair_bias.astype(jnp.float32)
    positions = jnp.arange(LEN, dtype=jnp.int32)
    live_rows = (positions[None, :] < lengths[:, None]).astype(jnp.float32).reshape(row_count, 1)
    inputs = tokens.astype(jnp.float32)
    gain_one = norm1_gain.astype(jnp.float32)
    gain_two = norm2_gain.astype(jnp.float32)
    shift_two = norm2_bias.astype(jnp.float32)
    centred_one, scale_one, normed_one = norm_forward(
        inputs, gain_one, norm1_bias.astype(jnp.float32), row_totals
    )
    rows_one = spread_rows(normed_one.astype(jnp.bfloat16))
    projected = jnp.einsum("rd,kdc->krc", rows_one, qkv_weight, preferred_element_type=jnp.float32)
    queries = projected[0] + qv_bias[0].astype(jnp.float32)
    key_proj = projected[1]
    value_proj = projected[2] + qv_bias[1].astype(jnp.float32)
    exp_keys = live_rows * jnp.exp(key_proj)
    carried = exp_keys * value_proj
    joined = jnp.concatenate([carried, exp_keys], axis=1).reshape(seq_count, LEN, 2 * chan_width)
    stacked_pad = jnp.pad(joined.astype(jnp.bfloat16), ((0, 0), (WIN, WIN), (0, 0)))
    seq_totals = jnp.sum(joined, axis=1, keepdims=True)
    windowed = window_products(stacked_pad, pair_vals, band_mask)
    merged = (seq_totals + windowed).reshape(row_count, 2 * chan_width)
    numerator = merged[:, :chan_width]
    denominator = merged[:, chan_width:]
    mix_ratio = numerator / denominator
    gate_vals = jax.nn.sigmoid(queries)
    mixed_low = (live_rows * gate_vals * mix_ratio).astype(jnp.bfloat16)
    branch_part = jnp.dot(mixed_low, out_weight, preferred_element_type=jnp.float32)
    branch = lax.psum_scatter(
        branch_part, "chan", scatter_dimension=1, tiled=True
    ) + out_bias.astype(jnp.float32)
    residual = inputs + live_rows * branch
    centred_two, scale_two, normed_two = norm_forward(residual, gain_two, shift_two, row_totals)
    rows_two = spread_rows(normed_two.astype(jnp.bfloat16))
    hidden = jnp.dot(rows_two, up_weight, preferred_element_type=jnp.float32) + up_bias.astype(
        jnp.float32
    )
    activated, gelu_pull = jax.vjp(gelu_tanh, hidden)
    act_low = activated.astype(jnp.bfloat16)
    down_part = jnp.dot(act_low, down_weight, preferred_element_type=jnp.float32)
    down_out = lax.psum_scatter(
        down_part.astype(jnp.bfloat16), "chan", scatter_dimension=1, tiled=True
    ).astype(jnp.float32) + down_bias.astype(jnp.float32)
    layer_out = (residual + live_rows * down_out).astype(jnp.bfloat16)
    cot_local = cotangent.astype(jnp.float32)
    cot_full = gather_grads(cotangent).astype(jnp.float32)
    down_grad = (live_rows * cot_full).astype(jnp.bfloat16)
    down_bias_grad = jnp.sum(live_rows * cot_local, axis=0)
    down_weight_grad = jnp.einsum(
        "rf,rd->fd", act_low, down_grad, preferred_element_type=jnp.float32
    )
    act_grad = jnp.einsum("rd,fd->rf", down_grad, down_weight, preferred_element_type=jnp.float32)
    hidden_grad = gelu_pull(act_grad)[0].astype(jnp.bfloat16)
    up_bias_grad = jnp.sum(hidden_grad.astype(jnp.float32), axis=0)
    up_weight_grad = jnp.einsum(
        "rd,rf->df", rows_two, hidden_grad, preferred_element_type=jnp.float32
    )
    norm_two_part = jnp.einsum(
        "rf,df->rd", hidden_grad, up_weight, preferred_element_type=jnp.float32
    )
    norm_two_cols = fold_rows(norm_two_part)
    back_two, norm2_gain_grad, norm2_bias_grad = norm_backward(
        norm_two_cols, centred_two, scale_two, gain_two, back_totals
    )
    res_grad = cot_local + back_two
    branch_cols = (live_rows * res_grad).astype(jnp.bfloat16)
    branch_grad = gather_grads(branch_cols)
    out_bias_grad = jnp.sum(branch_cols.astype(jnp.float32), axis=0)
    out_weight_grad = jnp.einsum(
        "rc,rd->cd", mixed_low, branch_grad, preferred_element_type=jnp.float32
    )
    mixed_grad = live_rows * jnp.einsum(
        "rd,cd->rc", branch_grad, out_weight, preferred_element_type=jnp.float32
    )
    query_grad = (mixed_grad * mix_ratio * gate_vals * (1.0 - gate_vals)).astype(jnp.bfloat16)
    ratio_grad = mixed_grad * gate_vals
    numer_grad = ratio_grad / denominator
    denom_grad = -ratio_grad * mix_ratio / denominator
    joined_grad = jnp.concatenate([numer_grad, denom_grad], axis=1).reshape(
        seq_count, LEN, 2 * chan_width
    )
    grads_pad = jnp.pad(joined_grad.astype(jnp.bfloat16), ((0, 0), (WIN, WIN), (0, 0)))
    pair_local, into_cols = window_back(grads_pad, stacked_pad, pair_vals, band_mask)
    pulled = (into_cols + jnp.sum(joined_grad, axis=1, keepdims=True)).reshape(
        row_count, 2 * chan_width
    )
    carried_grad = pulled[:, :chan_width]
    exp_grad = pulled[:, chan_width:]
    value_grad = (carried_grad * exp_keys).astype(jnp.bfloat16)
    key_grad = ((exp_grad + carried_grad * value_proj) * exp_keys).astype(jnp.bfloat16)
    qkv_grad = jnp.stack([query_grad, key_grad, value_grad])
    qkv_weight_grad = jnp.einsum(
        "rd,krc->kdc", rows_one, qkv_grad, preferred_element_type=jnp.float32
    )
    qv_bias_grad = jnp.stack(
        [
            jnp.sum(query_grad.astype(jnp.float32), axis=0),
            jnp.sum(value_grad.astype(jnp.float32), axis=0),
        ]
    )
    norm_one_part = jnp.einsum(
        "krc,kdc->rd", qkv_grad, qkv_weight, preferred_element_type=jnp.float32
    )
    norm_one_cols = fold_rows(norm_one_part)
    back_one, norm1_gain_grad, norm1_bias_grad = norm_backward(
        norm_one_cols, centred_one, scale_one, gain_one, back_totals
    )
    input_grad = (res_grad + back_one).astype(jnp.bfloat16)
    summed = lax.psum(
        (
            norm1_gain_grad,
            norm1_bias_grad,
            qkv_weight_grad,
            qv_bias_grad,
            out_weight_grad,
            out_bias_grad,
            norm2_gain_grad,
            norm2_bias_grad,
            up_weight_grad,
            up_bias_grad,
            down_weight_grad,
            down_bias_grad,
        ),
        "dp",
    )
    pair_total = lax.psum(pair_local, ("dp", "chan"))
    return (
        layer_out,
        input_grad,
        summed[0],
        summed[1],
        summed[2],
        summed[3],
        pair_total,
        summed[4],
        summed[5],
        summed[6],
        summed[7],
        summed[8],
        summed[9],
        summed[10],
        summed[11],
    )


def solution(mesh):
    in_specs = (
        P("dp", "chan"),
        P("chan"),
        P("chan"),
        P(None, None, "chan"),
        P(None, "chan"),
        P(),
        P("chan", None),
        P("chan"),
        P("chan"),
        P("chan"),
        P(None, "chan"),
        P("chan"),
        P("chan", None),
        P("chan"),
        P("dp"),
        P("dp", "chan"),
    )
    out_specs = (
        P("dp", "chan"),
        P("dp", "chan"),
        P("chan"),
        P("chan"),
        P(None, None, "chan"),
        P(None, "chan"),
        P(),
        P("chan", None),
        P("chan"),
        P("chan"),
        P("chan"),
        P(None, "chan"),
        P("chan"),
        P("chan", None),
        P("chan"),
    )
    return jax.shard_map(body, mesh=mesh, in_specs=in_specs, out_specs=out_specs, check_vma=False)
```

profile of v0, /device:TPU:1, one launch (start us, length us, event | category | flops | bytes accessed | tf_op | source)
XLA Modules:
  0.0 1426.3 jit_solution(7288491797598815370)
XLA Ops:
  10.7 11.2 all-reduce.5
  28.5 45.7 %all-gather.5.cloned.1.call-done = bf16[4096,768]{0,1:T(8,128)(2,1)} async-done(((bf16[4096,192]{0,1:T(8,128)(2,1)}), bf16[4096,768]{0,1:T(8,128)(2,1)}) %all-gather.5.cloned.1.call-update) | async-done | bytes 6291472 | tf_op jit(solution)/shard_map/all_gather | solution.py:38
  74.2 6.1 fusion.99
  85.8 5.6 exp.37
  91.4 5.7 squeeze.55
  97.1 6.5 fusion.84
  106.1 4.6 copy.65
  110.9 4.2 pad.7.clone
  118.3 64.4 %while.31 = (s32[]{:T(128)}, f32[8,512,384]{2,1,0:T(8,128)}, s32[8]{0:T(128)S(1)}, f32[1024,1024]{1,0:T(8,128)}, bf16[2,2560,384]{2,1,0:T(8,128)(2,1)}, /*index=...) while((s32[]{:T(128)}, f32[8,512,384]{2,1,0:T(8,128)}, ...), condition=%wide.region_6.8_spmd.clone, body=%wide.region_5.7_spmd.clone.sunk | while | flops 406323264 | bytes 7867141 | solution.py:91
  182.7 6.9 copy.62
  191.3 8.6 copy.67
  199.9 3.8 add.368
  203.7 4.9 multiply_convert_fusion.7
  209.8 6.3 fusion.94
  216.8 98.1 %reduce-scatter.5.cloned.1.call-done = f32[4096,192]{0,1:T(8,128)} async-done(((f32[4096,768]{0,1:T(8,128)}), f32[4096,192]{0,1:T(8,128)}) %reduce-scatter.5.cloned.1.call-update) | async-done | bytes 3145744 | tf_op jit(solution)/shard_map/reduce_scatter | solution.py:190
  314.9 4.3 fusion.92
  319.2 10.6 all-reduce.4
  329.9 3.7 add_convert_fusion.1
  334.3 47.2 %all-gather.7.cloned.1.call-done = bf16[4096,768]{0,1:T(8,128)(2,1)} async-done(((bf16[4096,192]{0,1:T(8,128)(2,1)}), bf16[4096,768]{0,1:T(8,128)(2,1)}) %all-gather.7.cloned.1.call-update) | async-done | bytes 6291472 | tf_op jit(solution)/shard_map/all_gather | solution.py:38
  381.4 10.6 fusion.95
  392.0 37.3 %all-gather.9.cloned.1.call-done = bf16[4096,768]{0,1:T(8,128)(2,1)} async-done(((bf16[4096,192]{0,1:T(8,128)(2,1)}), bf16[4096,768]{0,1:T(8,128)(2,1)}) %all-gather.9.cloned.1.call-update) | async-done | bytes 6291472 | tf_op jit(solution)/shard_map/all_gather | solution.py:42
  429.3 18.3 %convert_reduce_fusion = (f32[768]{0:T(1024)}, bf16[4096,768]{1,0:T(8,128)(2,1)S(1)}) fusion(f32[4096,768]{1,0:T(8,128)} %fusion.95, f32[768]{0:T(1024)S(1)} %convert_element_type.173, bf16[768,768]{1,0:T(8,128)(2,1)S(1)} %copy-done, bf16[4096,768]{0,1:T(8,128)(2,1)} %all-gather.9.cloned.1.call-done, f32[4096]{0:T(1024)S(1)} %bitcast.157), kind=kOutput, calls=%fused_computation.68 | convolution fusion | flops 4913626112 | bytes 26368000 | tf_op jit(solution)/shard_map/rd,fd->rf/dot_general | solution.py:213
  450.2 7.9 fusion.96
  458.4 11.1 convolution_convert_fusion
  470.2 86.8 %reduce-scatter.9.cloned.1.call-done = f32[4096,192]{0,1:T(8,128)} async-done(((f32[4096,768]{0,1:T(8,128)}), f32[4096,192]{0,1:T(8,128)}) %reduce-scatter.9.cloned.1.call-update) | async-done | bytes 3145744 | tf_op jit(solution)/shard_map/reduce_scatter | solution.py:46
  557.0 5.6 multiply_reduce_fusion
  562.6 9.7 all-reduce.7
  572.3 45.4 %reduce-scatter.7.cloned.1.call-done = bf16[4096,192]{0,1:T(8,128)(2,1)} async-done(((bf16[4096,768]{0,1:T(8,128)(2,1)}), bf16[4096,192]{0,1:T(8,128)(2,1)}) %reduce-scatter.7.cloned.1.call-update) | async-done | bytes 1572880 | tf_op jit(solution)/shard_map/reduce_scatter | solution.py:202
  617.7 6.3 convert_reduce_fusion.2
  624.2 46.9 %all-gather.11.cloned.1.call-done = bf16[4096,768]{0,1:T(8,128)(2,1)} async-done(((bf16[4096,192]{0,1:T(8,128)(2,1)}), bf16[4096,768]{0,1:T(8,128)(2,1)}) %all-gather.11.cloned.1.call-update) | async-done | bytes 6291472 | tf_op jit(solution)/shard_map/all_gather | solution.py:42
  671.1 8.5 convert_reduce_fusion.4
  682.7 9.5 reshape.114
  692.2 9.2 copy.59
  701.5 5.0 fusion.47
  706.5 8.6 copy.68
  723.1 171.4 %while.32 = (s32[]{:T(128)}, f32[1024,1024]{1,0:T(8,128)}, f32[8,512,384]{2,1,0:T(8,128)}, s32[8]{0:T(128)S(1)}, bf16[2,2560,384]{2,1,0:T(8,128)(2,1)}, /*index=...) while((s32[]{:T(128)}, f32[1024,1024]{1,0:T(8,128)}, ...), condition=%wide.region_19.21_spmd.clone.clone, body=%wide.region_18.20_spmd.clone.clone.sunk | while | flops 813695040 | bytes 32120324 | solution.py:132
  730.8 3.7 fusion.136
  734.4 5.3 copy.75
  752.2 3.6 fusion.136
  755.8 5.3 copy.75
  773.6 3.7 fusion.136
  777.2 5.3 copy.75
  798.7 5.3 copy.75
  816.5 3.7 fusion.136
  820.1 5.3 copy.75
  841.5 5.3 copy.75
  859.2 3.7 fusion.136
  862.9 5.3 copy.75
  884.3 5.3 copy.75
  894.6 6.7 copy.63
  901.3 5.7 add.385
  911.7 8.0 convolution_bitcast_fusion.2
  919.8 10.0 fusion.98
  929.8 19.0 %fusion.57 = f32[768,768]{1,0:T(8,128)} fusion(bf16[4096,768]{0,1:T(8,128)(2,1)} %all-gather.9.cloned.1.call-done, f32[4096]{0:T(1024)S(1)} %bitcast.161, f32[4096,768]{1,0:T(8,128)} %fusion.95, f32[768]{0:T(1024)S(1)} %convert_element_type.173), kind=kOutput, calls=%fused_computation.77 | convolution fusion | flops 4872732672 | bytes 21253120 | tf_op jit(solution)/shard_map/rf,rd->fd/dot_general | solution.py:210
  948.8 6.0 fusion.97
  954.9 7.8 fusion.86
  962.9 55.7 %reduce-scatter.11.cloned.1.call-done = f32[4096,192]{0,1:T(8,128)} async-done(((f32[4096,768]{0,1:T(8,128)}), f32[4096,192]{0,1:T(8,128)}) %reduce-scatter.11.cloned.1.call-update) | async-done | bytes 3145744 | tf_op jit(solution)/shard_map/reduce_scatter | solution.py:46
  1018.6 4.2 fusion.74
  1022.8 30.4 %all-reduce.2 = (f32[192]{0:T(256)}, f32[192]{0:T(256)}, f32[2,192]{1,0:T(2,128)}, f32[192]{0:T(256)}, f32[192]{0:T(256)}, /*index=5*/f32[192]{0:T(256)}, f32[768]{0:T(1024)}, f32[192]{0:T(256)}) all-reduce(f32[192]{0:T(256)S(1)} %get-tuple-element.364, f32[192]{0:T(256)S(1)} %get-tuple-element.369, ...), channel_id=1, replica_groups=mesh['dp'=8,'chan'=4] {'dp'}, use_global_device_ids=true, to_apply=%region_27.29 | all-reduce | flops 2304 | bytes 18432 | tf_op jit(solution)/shard_map/psum | solution.py:270
  1053.2 16.5 %all-reduce.6 = (bf16[4096]{0:T(1024)(128)(2,1)S(1)}, bf16[4096]{0:T(1024)(128)(2,1)S(1)}) all-reduce(bf16[4096]{0:T(1024)(128)(2,1)S(1)} %get-tuple-element.365, bf16[4096]{0:T(1024)(128)(2,1)S(1)} %get-tuple-element.366), channel_id=1, replica_groups=mesh['dp'=8,'chan'=4] {'chan'}, use_global_device_ids=true, to_apply=%region_25.27 | all-reduce | flops 8192 | bytes 32768 | tf_op jit(solution)/shard_map/psum | solution.py:33
  1069.7 6.2 fusion.73
  1075.9 89.3 %all-reduce.11.cloned.1.call-done = f32[1024,1024]{1,0:T(8,128)} async-done(((f32[1024,1024]{1,0:T(8,128)}), f32[1024,1024]{1,0:T(8,128)}) %all-reduce.11.cloned.1.call-update) | async-done | bytes 4194320 | tf_op jit(solution)/shard_map/psum | solution.py:287
  1165.2 242.5 %all-reduce.13.cloned.1.call-done = (f32[3,768,192]{1,2,0:T(8,128)}, f32[192,768]{1,0:T(8,128)}, f32[768,768]{1,0:T(8,128)}, f32[768,768]{1,0:T(8,128)}) async-done(((f32[3,768,192]{1,2,0:T(8,128)}, f32[192,768]{1,0:T(8,128)}, f32[768,768]{1,0:T(8,128)}, f32[768,768]{1,0:T(8,128)}), (f32[3,768,192]{1,2,0:T(8,128)}, f32[192,768]{1,0:T(8,128)}, f32[768,768]{1,0:T(8,128)}, ...) | async-done | bytes 7077904 | tf_op jit(solution)/shard_map/psum | solution.py:270
  1410.5 4.9 copy.100
  (243 shorter events, 183.4 us)
Async XLA Ops:
  7.2 422.1 %copy-start = (bf16[768,768]{1,0:T(8,128)(2,1)S(1)}, bf16[768,768]{1,0:T(8,128)(2,1)}, u32[]{:S(2)}) copy-start(bf16[768,768]{1,0:T(8,128)(2,1)} %param.34) | copy-start | bytes 3538948
  7.2 67.0 %all-gather.5.cloned.1.call-start = ((), (), s32[]{:S(2)}) async-start(), calls=%async_computation.4 | async-start | bytes 7864320 | tf_op jit(solution)/shard_map/all_gather | solution.py:38
  8.0 17.8 %copy-start.36 = (f32[192]{0:T(256)}, f32[192]{0:T(256)S(1)}, u32[]{:S(2)}) copy-start(f32[192]{0:T(256)S(1)} %convert_element_type.161) | copy-start | bytes 2308
  8.6 17.2 %copy-start.47 = (s32[2]{0:T(128)S(1)}, s32[2]{0:T(128)}, u32[]{:S(2)}) copy-start(s32[2]{0:T(128)} %param.36) | copy-start | bytes 28
  8.7 17.3 %copy-start.13 = (bf16[1024,1024]{1,0:T(8,128)(2,1)S(1)}, bf16[1024,1024]{1,0:T(8,128)(2,1)}, u32[]{:S(2)}) copy-start(bf16[1024,1024]{1,0:T(8,128)(2,1)} %param.27) | copy-start | bytes 6291460
  25.8 289.1 %reduce-scatter.5.cloned.1.call-start = ((), (), s32[]{:S(2)}) async-start(), calls=%async_computation.5 | async-start | bytes 15728640 | tf_op jit(solution)/shard_map/reduce_scatter | solution.py:190
  26.0 2.5 copy-start.43
  28.5 68.6 %copy-start.34 = (f32[1,192]{1,0:T(1,128)}, f32[1,192]{1,0:T(1,128)S(1)}, u32[]{:S(2)}) copy-start(f32[1,192]{1,0:T(1,128)S(1)} %get-tuple-element.445) | copy-start | bytes 2308
  80.3 5.5 copy-start.4
  182.7 6.9 copy-start.45
  189.6 10.3 slice-start
  191.3 8.7 slice-start.1
  203.7 4.9 copy-start.6
  203.7 6.0 copy-start.23
  208.6 1.1 copy-start.9
  216.1 0.7 copy-start.52
  216.1 98.8 %copy-start.2 = (bf16[4096,192]{0,1:T(8,128)(2,1)S(1)}, bf16[4096,192]{0,1:T(8,128)(2,1)}, u32[]{:S(2)}) copy-start(bf16[4096,192]{0,1:T(8,128)(2,1)} %param.22) | copy-start | bytes 4718596
  216.1 165.3 %all-gather.7.cloned.1.call-start = ((), (), s32[]{:S(2)}) async-start(), calls=%async_computation.6 | async-start | bytes 7864320 | tf_op jit(solution)/shard_map/all_gather | solution.py:38
  216.8 401.0 %copy-start.32 = (f32[192]{0:T(256)}, f32[192]{0:T(256)S(1)}, u32[]{:S(2)}) copy-start(f32[192]{0:T(256)S(1)} %convert_element_type.170) | copy-start | bytes 2308
  329.8 287.9 %copy-start.19 = (f32[4096]{0:T(1024)}, f32[4096]{0:T(1024)S(1)}, u32[]{:S(2)}) copy-start(f32[4096]{0:T(1024)S(1)} %get-tuple-element.440) | copy-start | bytes 49156
  329.8 287.9 %copy-start.21 = (f32[4096]{0:T(1024)}, f32[4096]{0:T(1024)S(1)}, u32[]{:S(2)}) copy-start(f32[4096]{0:T(1024)S(1)} %get-tuple-element.441) | copy-start | bytes 49156
  329.9 4.4 copy-start.44
  329.9 51.6 %copy-start.48 = (bf16[768,768]{1,0:T(8,128)(2,1)S(1)}, bf16[768,768]{1,0:T(8,128)(2,1)}, u32[]{:S(2)}) copy-start(bf16[768,768]{1,0:T(8,128)(2,1)} %param.32) | copy-start | bytes 3538948
  333.6 95.7 %all-gather.9.cloned.1.call-start = ((), (), s32[]{:S(2)}) async-start(), calls=%async_computation.8 | async-start | bytes 7864320 | tf_op jit(solution)/shard_map/all_gather | solution.py:42
  334.2 222.8 %reduce-scatter.9.cloned.1.call-start = ((), (), s32[]{:S(2)}) async-start(), calls=%async_computation.9 | async-start | bytes 15728640 | tf_op jit(solution)/shard_map/reduce_scatter | solution.py:46
  447.6 2.6 copy-start.56
  458.1 159.6 %reduce-scatter.7.cloned.1.call-start = ((), (), s32[]{:S(2)}) async-start(), calls=%async_computation.7 | async-start | bytes 7864320 | tf_op jit(solution)/shard_map/reduce_scatter | solution.py:202
  469.5 201.6 %all-gather.11.cloned.1.call-start = ((), (), s32[]{:S(2)}) async-start(), calls=%async_computation.10 | async-start | bytes 7864320 | tf_op jit(solution)/shard_map/all_gather | solution.py:42
  470.1 147.6 %copy-start.7 = (bf16[4096,192]{0,1:T(8,128)(2,1)S(1)}, bf16[4096,192]{0,1:T(8,128)(2,1)}, u32[]{:S(2)}) copy-start(bf16[4096,192]{0,1:T(8,128)(2,1)} %param.37) | copy-start | bytes 4718596
  572.3 51.8 %copy-start.28 = (f32[4096]{0:T(1024)}, f32[4096]{0:T(1024)S(1)}, u32[]{:S(2)}) copy-start(f32[4096]{0:T(1024)S(1)} %get-tuple-element.448) | copy-start | bytes 49156
  572.3 51.8 %copy-start.30 = (f32[4096]{0:T(1024)}, f32[4096]{0:T(1024)S(1)}, u32[]{:S(2)}) copy-start(f32[4096]{0:T(1024)S(1)} %get-tuple-element.449) | copy-start | bytes 49156
  624.1 394.4 %reduce-scatter.11.cloned.1.call-start = ((), (), s32[]{:S(2)}) async-start(), calls=%async_computation.11 | async-start | bytes 15728640 | tf_op jit(solution)/shard_map/reduce_scatter | solution.py:46
  679.6 230.5 %copy-start.54 = (bf16[4096,192]{0,1:T(8,128)(2,1)}, bf16[4096,192]{0,1:T(8,128)(2,1)S(1)}, u32[]{:S(2)}) copy-start(bf16[4096,192]{0,1:T(8,128)(2,1)S(1)} %get-tuple-element.427) | copy-start | bytes 4718596
  706.5 8.7 copy-start.8
  719.9 3.2 copy-start.46
  901.2 7.3 copy-start.5
  901.2 7.3 copy-start.35
  908.5 3.2 copy-start.49
  910.1 1.1 copy-start.14
  910.1 1.7 copy-start.16
  919.7 245.4 %all-reduce.11.cloned.1.call-start = ((), (), s32[]{:S(2)}) async-start(), calls=%async_computation.12 | async-start | bytes 8388608 | tf_op jit(solution)/shard_map/psum | solution.py:287
  929.8 19.0 %copy-start.10 = (bf16[4096,192]{0,1:T(8,128)(2,1)S(1)}, bf16[4096,192]{0,1:T(8,128)(2,1)}, u32[]{:S(2)}) copy-start(bf16[4096,192]{0,1:T(8,128)(2,1)} %copy-done.9) | copy-start | bytes 4718596
  929.8 477.9 %all-reduce.13.cloned.1.call-start = ((), (), s32[]{:S(2)}) async-start(), calls=%async_computation.13 | async-start | bytes 14155776 | tf_op jit(solution)/shard_map/psum | solution.py:270
  948.8 6.1 copy-start.15
  948.8 6.1 copy-start.17
  948.8 6.1 copy-start.55
  962.7 55.8 %copy-start.3 = (bf16[4096,192]{0,1:T(8,128)(2,1)S(1)}, bf16[4096,192]{0,1:T(8,128)(2,1)}, u32[]{:S(2)}) copy-start(bf16[4096,192]{0,1:T(8,128)(2,1)} %param.22) | copy-start | bytes 4718596
  962.7 55.8 %copy-start.25 = (f32[4096]{0:T(1024)S(1)}, f32[4096]{0:T(1024)}, u32[]{:S(2)}) copy-start(f32[4096]{0:T(1024)} %copy-done.24) | copy-start | bytes 49156
  962.7 55.8 %copy-start.27 = (f32[4096]{0:T(1024)S(1)}, f32[4096]{0:T(1024)}, u32[]{:S(2)}) copy-start(f32[4096]{0:T(1024)} %copy-done.26) | copy-start | bytes 49156
  962.7 55.8 %copy-start.37 = (f32[192]{0:T(256)S(1)}, f32[192]{0:T(256)}, u32[]{:S(2)}) copy-start(f32[192]{0:T(256)} %copy-done.36) | copy-start | bytes 2308
  962.8 60.0 %copy-start.38 = (f32[192]{0:T(256)S(1)}, f32[192]{0:T(256)}, u32[]{:S(2)}) copy-start(f32[192]{0:T(256)} %get-tuple-element.362) | copy-start | bytes 2308
  962.8 60.0 %copy-start.39 = (f32[192]{0:T(256)S(1)}, f32[192]{0:T(256)}, u32[]{:S(2)}) copy-start(f32[192]{0:T(256)} %get-tuple-element.368) | copy-start | bytes 2308
  962.8 60.0 %copy-start.40 = (f32[192]{0:T(256)S(1)}, f32[192]{0:T(256)}, u32[]{:S(2)}) copy-start(f32[192]{0:T(256)} %get-tuple-element.424) | copy-start | bytes 2308
  962.8 60.0 %copy-start.41 = (f32[192]{0:T(256)S(1)}, f32[192]{0:T(256)}, u32[]{:S(2)}) copy-start(f32[192]{0:T(256)} %get-tuple-element.439) | copy-start | bytes 2308
  962.8 60.0 %copy-start.42 = (f32[768]{0:T(1024)S(1)}, f32[768]{0:T(1024)}, u32[]{:S(2)}) copy-start(f32[768]{0:T(1024)} %get-tuple-element.422) | copy-start | bytes 9220
  962.8 106.9 %copy-start.20 = (f32[4096]{0:T(1024)S(1)}, f32[4096]{0:T(1024)}, u32[]{:S(2)}) copy-start(f32[4096]{0:T(1024)} %copy-done.19) | copy-start | bytes 49156
  962.8 106.9 %copy-start.22 = (f32[4096]{0:T(1024)S(1)}, f32[4096]{0:T(1024)}, u32[]{:S(2)}) copy-start(f32[4096]{0:T(1024)} %copy-done.21) | copy-start | bytes 49156
  962.8 106.9 %copy-start.29 = (f32[4096]{0:T(1024)S(1)}, f32[4096]{0:T(1024)}, u32[]{:S(2)}) copy-start(f32[4096]{0:T(1024)} %copy-done.28) | copy-start | bytes 49156
  962.8 106.9 %copy-start.31 = (f32[4096]{0:T(1024)S(1)}, f32[4096]{0:T(1024)}, u32[]{:S(2)}) copy-start(f32[4096]{0:T(1024)} %copy-done.30) | copy-start | bytes 49156
  962.9 106.9 %copy-start.33 = (f32[192]{0:T(256)S(1)}, f32[192]{0:T(256)}, u32[]{:S(2)}) copy-start(f32[192]{0:T(256)} %copy-done.32) | copy-start | bytes 2308
  1410.5 4.9 copy-start.18
  1410.5 5.8 copy-start.12
  1415.4 2.2 copy-start.11
  1416.3 2.8 copy-start.1
  (5 other events, 3.2 us)
Sparse Core Ops, SparseCore 0:
  25.9 48.1 all-gather.4
  216.2 98.6 reduce-scatter.4
  333.7 47.6 all-gather.6
  382.8 46.3 all-gather.8
  458.3 98.6 reduce-scatter.8
  559.3 58.3 reduce-scatter.6
  624.2 46.8 all-gather.10
  919.9 98.6 reduce-scatter.10
  1025.0 140.1 all-reduce.10
  1171.2 236.4 all-reduce.12
where the time goes:
time: 1440 us; the launch traced here: 1430 us
  waiting for transfers between devices  795 us (55%)
  local copies, waits for them, and re-layouts  202 us (14%)
  matrix products  190 us (13%)
  other arithmetic  102 us (7%)
  blocking collectives  78.4 us (5%)
  loops' own time  43.1 us (3%)
  between operations  15.2 us (1%)
    psum x1, waiting for transfers between devices, body(): lax.psum((norm1_gain_grad, norm1_bias_grad, qkv_weight_grad, qv_bias_grad...  243 us
    reduce_scatter x2, waiting for transfers between devices, fold_rows(): return lax.psum_scatter(values, 'chan', scatter_dimension=1, tiled=True)  142 us
    reduce_scatter x1, waiting for transfers between devices, body(): lax.psum_scatter(branch_part, 'chan', scatter_dimension=1, tiled=True)  98.1 us
    all_gather x2, waiting for transfers between devices, spread_rows(): return lax.all_gather(values, 'chan', axis=1, tiled=True)  92.8 us
    psum x1, waiting for transfers between devices, body(): pair_total = lax.psum(pair_local, ('dp', 'chan'))  89.3 us
    all_gather x2, waiting for transfers between devices, gather_grads(): return lax.all_gather(values, 'chan', axis=1, tiled=True)  84.2 us
    reduce_scatter x1, waiting for transfers between devices, body(): lax.psum_scatter(down_part.astype(jnp.bfloat16), 'chan', scatter_dimensio...  45.4 us
    unnamed x127, local copies, waits for them, and re-layouts  44.1 us
  transfers between devices with their start and end apart: 10, of which 10 were waited for; matrix products, arithmetic and copies ran while one was open for 6% of the time, Pallas kernels for 0%

commit v1 on v0

v1 whole, which is shorter than its diff:
```python
import jax
import jax.numpy as jnp
from jax import lax
from jax.sharding import PartitionSpec as P

D = 768
PAIR = 1024
WIN = 256
LEN = 2048
CHAN = 4
EPSILON = 1e-05
BF = jnp.bfloat16
F32 = jnp.float32


def flip(values, axis, mask):
    size = lax.axis_size(axis)
    return lax.ppermute(values, axis, [(i, i ^ mask) for i in range(size)])


def dot_f32(left, right, dims):
    return lax.dot_general(left, right, (dims, ((), ())), preferred_element_type=F32)


def mm(left, right):
    return dot_f32(left, right, ((1,), (0,)))


def mm_t(left, right):
    return dot_f32(left, right, ((1,), (1,)))


def t_mm(left, right):
    return dot_f32(left, right, ((0,), (0,)))


def pick(pieces, index):
    low, high = index % 2 == 1, index // 2 == 1
    a, b, c, d = pieces
    a, b = jnp.where(low, b, a), jnp.where(low, a, b)
    c, d = jnp.where(low, d, c), jnp.where(low, c, d)
    a, c = jnp.where(high, c, a), jnp.where(high, a, c)
    b, d = jnp.where(high, d, b), jnp.where(high, b, d)
    return [a, b, c, d]


def rows_in(values, me):
    rows = values.shape[0] // CHAN
    pieces = [lax.dynamic_slice_in_dim(values, (me ^ r) * rows, rows, 0) for r in range(CHAN)]
    pieces = pieces[:1] + [flip(pieces[r], "chan", r) for r in range(1, CHAN)]
    return jnp.concatenate(pick(pieces, me), axis=1)


def rows_out(values, me):
    cols = values.shape[1] // CHAN
    rows = values.shape[0]
    pieces = pick([values[:, r * cols : (r + 1) * cols] for r in range(CHAN)], me)
    pieces = pieces[:1] + [flip(pieces[r], "chan", r) for r in range(1, CHAN)]
    out = jnp.zeros((CHAN * rows, cols), values.dtype)
    for r in range(CHAN):
        out = lax.dynamic_update_slice_in_dim(out, pieces[r], (me ^ r) * rows, 0)
    return out


def shards(weight):
    near = flip(weight, "chan", 1)
    far = flip(weight, "chan", 2)
    return [weight, near, far, flip(far, "chan", 1)]


def dp_stages():
    size = lax.axis_size("dp")
    stages, mask = [[1]], 2
    while mask < size:
        if mask * 2 < size:
            stages.append([mask, mask * 2, mask * 3])
            mask *= 4
        else:
            stages.append([mask])
            mask *= 2
    return stages


def group_index(index, masks):
    return (index // masks[0]) % (len(masks) + 1)


def dp_sum(values):
    me = lax.axis_index("dp")
    stages = dp_stages()
    for masks in stages:
        own = group_index(me, masks)
        parts = len(masks) + 1
        rows = values.shape[0] // parts
        got = [
            flip(
                lax.dynamic_slice_in_dim(values, (own ^ k) * rows, rows, 0), "dp", masks[0] * k
            )
            for k in range(1, parts)
        ]
        total = lax.dynamic_slice_in_dim(values, own * rows, rows, 0).astype(F32)
        for g in got:
            total = total + g.astype(F32)
        values = total.astype(BF)
    for masks in reversed(stages):
        own = group_index(me, masks)
        parts = len(masks) + 1
        rows = values.shape[0]
        out = jnp.zeros((parts * rows, values.shape[1]), values.dtype)
        out = lax.dynamic_update_slice_in_dim(out, values, own * rows, 0)
        for k in range(1, parts):
            got = flip(values, "dp", masks[0] * k)
            out = lax.dynamic_update_slice_in_dim(out, got, (own ^ k) * rows, 0)
        values = out
    return values


def weight_sum(grads):
    far = grads[2] + flip(grads[3].astype(BF), "chan", 1).astype(F32)
    near = grads[0] + flip(grads[1].astype(BF), "chan", 1).astype(F32)
    own = near + flip(far.astype(BF), "chan", 2).astype(F32)
    return dp_sum(own.astype(BF)).astype(F32)


def all_sum(values):
    for k in (1, 2):
        values = values + flip(values, "chan", k)
    for masks in dp_stages():
        got = [flip(values, "dp", m) for m in masks]
        for g in got:
            values = values + g
    return values


def pair_sum_all(values):
    me = lax.axis_index("chan")
    for bit in (1, 2):
        rows = values.shape[0] // 2
        own = (me // bit) % 2
        got = flip(lax.dynamic_slice_in_dim(values, (1 - own) * rows, rows, 0), "chan", bit)
        kept = lax.dynamic_slice_in_dim(values, own * rows, rows, 0)
        values = (kept.astype(F32) + got.astype(F32)).astype(BF)
    values = dp_sum(values)
    for bit in (2, 1):
        own = (me // bit) % 2
        got = flip(values, "chan", bit)
        first = jnp.where(own == 0, values, got)
        second = jnp.where(own == 0, got, values)
        values = jnp.concatenate([first, second], axis=0)
    return values


def norm_forward(values, gain_vals, shift_vals):
    row_mean = jnp.mean(values, axis=1, keepdims=True)
    spread = jnp.mean(values * values, axis=1, keepdims=True) - row_mean * row_mean
    inv_scale = lax.rsqrt(spread + EPSILON)
    centred = (values - row_mean) * inv_scale
    return centred, inv_scale, (centred * gain_vals + shift_vals).astype(BF)


def norm_backward(grad_out, centred, inv_scale, gain_vals):
    scaled = grad_out * gain_vals
    plain = jnp.mean(scaled, axis=1, keepdims=True)
    crossed = jnp.mean(scaled * centred, axis=1, keepdims=True)
    grad_in = inv_scale * (scaled - plain - centred * crossed)
    return grad_in, jnp.sum(grad_out * centred, axis=0), jnp.sum(grad_out, axis=0)


def gelu_pair(u):
    c0, c1 = 0.7978845608, 0.044715
    sq = u * u
    t = jnp.tanh(c0 * u * (1.0 + c1 * sq))
    half = 0.5 * (1.0 + t)
    slope = half + 0.5 * u * (1.0 - t * t) * (c0 * (1.0 + 3.0 * c1 * sq))
    return u * half, slope


def body(
    tokens,
    norm1_gain,
    norm1_bias,
    qkv_weight,
    qv_bias,
    pair_bias,
    out_weight,
    out_bias,
    norm2_gain,
    norm2_bias,
    up_weight,
    up_bias,
    down_weight,
    down_bias,
    lengths,
    cotangent,
):
    me = lax.axis_index("chan")
    half = me % 2
    rows = tokens.shape[0] // CHAN
    blocks = rows // WIN
    width = D // CHAN
    length = lax.dynamic_index_in_dim(lengths, me // 2, 0, keepdims=False)
    place = lax.broadcasted_iota(jnp.int32, (rows, 1), 0) + half * rows
    live = (place < length).astype(F32)

    small = jnp.stack(
        [norm1_gain, norm1_bias, qv_bias[0], qv_bias[1], out_bias, norm2_gain, norm2_bias, down_bias]
    )
    small = jnp.concatenate([small, up_bias.reshape(CHAN, width)], axis=0)
    small_rel = [small] + [flip(small, "chan", r) for r in range(1, CHAN)]
    small_abs = jnp.concatenate(pick(small_rel, me), axis=1).astype(F32)
    gain_one, shift_one = small_abs[0], small_abs[1]
    out_shift, gain_two, shift_two, down_shift = (
        small_abs[4],
        small_abs[5],
        small_abs[6],
        small_abs[7],
    )
    q_shift = jnp.concatenate(pick([s[2] for s in small_rel], half)).astype(F32)
    v_shift = jnp.concatenate(pick([s[3] for s in small_rel], half)).astype(F32)
    up_shift = [s[8:].reshape(-1).astype(F32) for s in small_rel]

    x_rows = rows_in(tokens, me).astype(F32)
    qkv_t = jnp.concatenate(pick(shards(jnp.swapaxes(qkv_weight, 1, 2)), half), axis=1)
    out_w = jnp.concatenate(pick(shards(out_weight), half), axis=0)
    up_w = shards(up_weight)
    down_w = shards(down_weight)
    cot = rows_in(cotangent, me).astype(F32)

    pair = pair_bias.astype(F32)
    row_ids = lax.broadcasted_iota(jnp.int32, (WIN, WIN), 0)
    col_ids = lax.broadcasted_iota(jnp.int32, (WIN, WIN), 1)
    masks = [col_ids > row_ids, col_ids >= 0, col_ids < row_ids]

    def pair_block(b, k):
        col = (b - 1 + k) % blocks
        return jnp.exp(pair[b * WIN : (b + 1) * WIN, col * WIN : (col + 1) * WIN])

    terms = [
        jnp.concatenate(
            [jnp.where(masks[k], pair_block(b, k) - 1.0, 0.0).astype(BF) for k in range(3)], axis=1
        )
        for b in range(blocks)
    ]
    terms_t = [
        jnp.concatenate(
            [terms[(s - 1 + k) % blocks][:, (2 - k) * WIN : (3 - k) * WIN] for k in range(3)], axis=0
        )
        for s in range(blocks)
    ]

    def extend(values):
        edge = lax.dynamic_slice_in_dim(values, (1 - half) * (rows - WIN), WIN, 0)
        halo = flip(edge, "chan", 1)
        none = jnp.zeros_like(halo)
        return jnp.concatenate(
            [jnp.where(half == 1, halo, none), values, jnp.where(half == 1, none, halo)], axis=0
        )

    def both_halves(values):
        return values + flip(values, "chan", 1)

    cent_one, inv_one, normed_one = norm_forward(x_rows, gain_one, shift_one)
    queries = mm_t(normed_one, qkv_t[0]) + q_shift
    key_proj = mm_t(normed_one, qkv_t[1])
    value_proj = mm_t(normed_one, qkv_t[2]) + v_shift
    exp_keys = live * jnp.exp(key_proj)
    carried = exp_keys * value_proj
    joined = jnp.concatenate([carried, exp_keys], axis=1)
    totals = both_halves(jnp.sum(joined, axis=0, keepdims=True))
    data_ext = extend(joined.astype(BF))
    windowed = jnp.concatenate(
        [mm(terms[b], data_ext[b * WIN : (b + 3) * WIN]) for b in range(blocks)], axis=0
    )
    merged = totals + windowed
    denominator = merged[:, D:]
    mix_ratio = merged[:, :D] / denominator
    gate = jax.nn.sigmoid(queries)
    mixed = (live * gate * mix_ratio).astype(BF)
    residual = x_rows + live * (mm(mixed, out_w) + out_shift)
    cent_two, inv_two, normed_two = norm_forward(residual, gain_two, shift_two)

    down_grad = (live * cot).astype(BF)
    down_out = jnp.zeros((rows, D), F32)
    norm_two_in = jnp.zeros((rows, D), F32)
    up_grads, down_grads, up_shift_grads = [None] * CHAN, [None] * CHAN, [None] * CHAN
    for r in (0, 1, 3, 2):
        hidden = mm(normed_two, up_w[r]) + up_shift[r]
        act, slope = gelu_pair(hidden)
        act = act.astype(BF)
        down_out = down_out + mm(act, down_w[r])
        hidden_grad = (mm_t(down_grad, down_w[r]) * slope).astype(BF)
        down_grads[r] = t_mm(act, down_grad)
        up_grads[r] = t_mm(normed_two, hidden_grad)
        up_shift_grads[r] = jnp.sum(hidden_grad.astype(F32), axis=0)
        norm_two_in = norm_two_in + mm_t(hidden_grad, up_w[r])
    layer_out = (residual + live * (down_out + down_shift)).astype(BF)
    layer_out = rows_out(layer_out, me)
    down_weight_grad = weight_sum(down_grads)
    up_weight_grad = weight_sum(up_grads)

    back_two, gain_two_grad, shift_two_grad = norm_backward(
        norm_two_in, cent_two, inv_two, gain_two
    )
    res_grad = cot + back_two
    branch_grad = (live * res_grad).astype(BF)
    out_grad = t_mm(mixed, branch_grad)
    out_weight_grad = weight_sum(
        pick([out_grad[r * width : (r + 1) * width] for r in range(CHAN)], half)
    )
    mixed_grad = live * mm_t(branch_grad, out_w)
    query_grad = (mixed_grad * mix_ratio * gate * (1.0 - gate)).astype(BF)
    num_grad = mixed_grad * gate / denominator
    den_grad = -num_grad * mix_ratio
    joined_grad = jnp.concatenate([num_grad, den_grad], axis=1)
    grad_totals = both_halves(jnp.sum(joined_grad, axis=0, keepdims=True))
    grad_low = joined_grad.astype(BF)
    grad_ext = extend(grad_low)
    tri = []
    for b in range(blocks):
        prod = mm_t(grad_low[b * WIN : (b + 1) * WIN], data_ext[b * WIN : (b + 3) * WIN])
        side = jnp.where(masks[0], prod[:, :WIN], 0.0) + jnp.where(
            masks[2], prod[:, 2 * WIN :], 0.0
        )
        tri.append(jnp.concatenate([prod[:, WIN : 2 * WIN], side], axis=1))
    packed = pair_sum_all(jnp.concatenate(tri, axis=0).astype(BF)).astype(F32)
    lines = []
    for b in range(blocks):
        own, side = packed[b * WIN : (b + 1) * WIN, :WIN], packed[b * WIN : (b + 1) * WIN, WIN:]
        squares = [jnp.zeros((WIN, WIN), F32)] * blocks
        squares[b] = own * pair_block(b, 1)
        squares[(b - 1) % blocks] = jnp.where(masks[0], side * pair_block(b, 0), 0.0)
        squares[(b + 1) % blocks] = jnp.where(masks[2], side * pair_block(b, 2), 0.0)
        lines.append(jnp.concatenate(squares, axis=1))
    pair_bias_grad = jnp.concatenate(lines, axis=0)

    pulled = grad_totals + jnp.concatenate(
        [t_mm(terms_t[s], grad_ext[s * WIN : (s + 3) * WIN]) for s in range(blocks)], axis=0
    )
    carried_grad, exp_grad = pulled[:, :D], pulled[:, D:]
    value_grad = (carried_grad * exp_keys).astype(BF)
    key_grad = ((exp_grad + carried_grad * value_proj) * exp_keys).astype(BF)
    qkv_grads = [query_grad, key_grad, value_grad]
    qkv_full = jnp.stack([t_mm(g, normed_one) for g in qkv_grads])
    qkv_sum = weight_sum(
        pick([qkv_full[:, r * width : (r + 1) * width].reshape(-1, D) for r in range(CHAN)], half)
    )
    qkv_weight_grad = jnp.swapaxes(qkv_sum.reshape(3, width, D), 1, 2)
    norm_one_in = mm(query_grad, qkv_t[0]) + mm(key_grad, qkv_t[1]) + mm(value_grad, qkv_t[2])
    back_one, gain_one_grad, shift_one_grad = norm_backward(
        norm_one_in, cent_one, inv_one, gain_one
    )
    input_grad = rows_out((res_grad + back_one).astype(BF), me)

    def rel(vector):
        pieces = pick([vector[r * width : (r + 1) * width] for r in range(CHAN)], half)
        return jnp.stack(pick(pieces, me))

    def col_sum(values):
        return jnp.sum(values.astype(F32), axis=0)

    def absolute(vector):
        return vector.reshape(CHAN, width)

    pieces = jnp.stack(
        [
            absolute(gain_one_grad),
            absolute(shift_one_grad),
            rel(col_sum(query_grad)),
            rel(col_sum(value_grad)),
            absolute(col_sum(branch_grad)),
            absolute(gain_two_grad),
            absolute(shift_two_grad),
            absolute(jnp.sum(live * cot, axis=0)),
        ],
        axis=1,
    )
    ups = jnp.stack(pick([g.reshape(CHAN, width) for g in up_shift_grads], me))
    pieces = all_sum(jnp.concatenate([pieces, ups], axis=1))
    mine = lax.dynamic_index_in_dim(pieces, me, 0, keepdims=False)
    return (
        layer_out,
        input_grad,
        mine[0],
        mine[1],
        qkv_weight_grad,
        mine[2:4],
        pair_bias_grad,
        out_weight_grad,
        mine[4],
        mine[5],
        mine[6],
        up_weight_grad,
        mine[8:].reshape(-1),
        down_weight_grad,
        mine[7],
    )


def solution(mesh):
    in_specs = (
        P("dp", "chan"),
        P("chan"),
        P("chan"),
        P(None, None, "chan"),
        P(None, "chan"),
        P(),
        P("chan", None),
        P("chan"),
        P("chan"),
        P("chan"),
        P(None, "chan"),
        P("chan"),
        P("chan", None),
        P("chan"),
        P("dp"),
        P("dp", "chan"),
    )
    out_specs = (
        P("dp", "chan"),
        P("dp", "chan"),
        P("chan"),
        P("chan"),
        P(None, None, "chan"),
        P(None, "chan"),
        P(),
        P("chan", None),
        P("chan"),
        P("chan"),
        P("chan"),
        P(None, "chan"),
        P("chan"),
        P("chan", None),
        P("chan"),
    )
    return jax.shard_map(body, mesh=mesh, in_specs=in_specs, out_specs=out_specs, check_vma=False)
```

time: 1440 us -> 632 us (0.44)
  the two profiles are of different devices: /device:TPU:1 before, /device:TPU:0 now
where the time goes in v1:
time: 632 us; the launch traced here: 624 us
  waiting for transfers between devices  220 us (35%)
  matrix products  136 us (22%)
  local copies, waits for them, and re-layouts  95.5 us (15%)
  starting transfers between devices  87.8 us (14%)
  other arithmetic  80.9 us (13%)
    ppermute x93, waiting for transfers between devices, flip(): return lax.ppermute(values, axis, [(i, i ^ mask) for i in range(size)])  220 us
    dot_general x48, matrix products, dot_f32(): lax.dot_general(left, right, (dims, ((), ())), preferred_element_type=F32)  136 us
    ppermute x93, starting transfers between devices, flip(): return lax.ppermute(values, axis, [(i, i ^ mask) for i in range(size)])  87.8 us
    unnamed x280, local copies, waits for them, and re-layouts  23.7 us
  transfers between devices with their start and end apart: 93, of which 33 were waited for; matrix products, arithmetic and copies ran while one was open for 34% of the time, Pallas kernels for 0%

profile of v1, /device:TPU:0, one launch (start us, length us, event | category | flops | bytes accessed | tf_op | source)
XLA Modules:
  0.0 623.7 jit_solution(973369871526883989)
XLA Ops:
  6.1 2.5 collective-permute-start.3
  37.5 6.8 %collective-permute-done = bf16[1024,192]{1,0:T(8,128)(2,1)S(1)} collective-permute-done((bf16[1024,192]{1,0:T(8,128)(2,1)}, bf16[1024,192]{1,0:T(8,128)(2,1)S(1)}, u32[]{:S(2)}, u32[]{:S(2)}) %collective-permute-start) | collective-permute-done | bytes 393248 | tf_op jit(solution)/shard_map/ppermute | solution.py:18
  45.3 11.6 %collective-permute-done.1 = bf16[1024,192]{1,0:T(8,128)(2,1)S(1)} collective-permute-done((bf16[1024,192]{1,0:T(8,128)(2,1)}, bf16[1024,192]{1,0:T(8,128)(2,1)S(1)}, u32[]{:S(2)}, u32[]{:S(2)}) %collective-permute-start.1) | collective-permute-done | bytes 393248 | tf_op jit(solution)/shard_map/ppermute | solution.py:18
  57.5 5.7 collective-permute-done.11
  65.1 8.0 %collective-permute-done.23 = bf16[1024,192]{1,0:T(8,128)(2,1)S(1)} collective-permute-done((bf16[1024,192]{1,0:T(8,128)(2,1)}, bf16[1024,192]{1,0:T(8,128)(2,1)S(1)}, u32[]{:S(2)}, u32[]{:S(2)}) %collective-permute-start.23) | collective-permute-done | bytes 393248 | tf_op jit(solution)/shard_map/ppermute | solution.py:18
  74.3 10.8 %collective-permute-done.24 = bf16[1024,192]{1,0:T(8,128)(2,1)S(1)} collective-permute-done((bf16[1024,192]{1,0:T(8,128)(2,1)}, bf16[1024,192]{1,0:T(8,128)(2,1)S(1)}, u32[]{:S(2)}, u32[]{:S(2)}) %collective-permute-start.24) | collective-permute-done | bytes 393248 | tf_op jit(solution)/shard_map/ppermute | solution.py:18
  99.4 14.8 %collective-permute-done.18 = bf16[768,768]{1,0:T(8,128)(2,1)} collective-permute-done((bf16[768,768]{1,0:T(8,128)(2,1)}, bf16[768,768]{1,0:T(8,128)(2,1)}, u32[]{:S(2)}, u32[]{:S(2)}) %collective-permute-start.18) | collective-permute-done | bytes 1179680 | tf_op jit(solution)/shard_map/ppermute | solution.py:18
  114.2 23.6 %collective-permute-done.16 = bf16[768,768]{1,0:T(8,128)(2,1)S(1)} collective-permute-done((bf16[768,768]{1,0:T(8,128)(2,1)}, bf16[768,768]{1,0:T(8,128)(2,1)S(1)}, u32[]{:S(2)}, u32[]{:S(2)}) %collective-permute-start.16) | collective-permute-done | bytes 1179680 | tf_op jit(solution)/shard_map/ppermute | solution.py:18
  142.1 3.8 multiply_convert_fusion.11
  148.3 3.2 fusion.148
  151.6 6.5 %convert_reduce_fusion.1 = (f32[768]{0:T(1024)}, bf16[1024,768]{1,0:T(8,128)(2,1)S(1)}) fusion(f32[1024,768]{1,0:T(8,128)S(1)} %fusion.148, f32[768]{0:T(1024)S(1)} %copy-done.100, bf16[768,768]{1,0:T(8,128)(2,1)} %param.28, f32[1024]{0:T(1024)S(1)} %fusion.104, bf16[1024,192]{1,0:T(8,128)(2,1)S(1)} %get-tuple-element.112, ...), kind=kOutput, calls=%fused_computation.37 | convolution fusion | flops 1232338176 | bytes 7481344 | tf_op jit(solution)/shard_map/dot_general | solution.py:22
  158.1 3.3 fusion.152
  162.8 3.1 fusion.149
  167.4 7.2 %convert_reduce_fusion.3 = (f32[768]{0:T(1024)}, bf16[1024,768]{1,0:T(8,128)(2,1)}) fusion(f32[1024,768]{1,0:T(8,128)S(1)} %fusion.151, f32[768]{0:T(1024)S(1)} %reshape.350, bf16[768,768]{1,0:T(8,128)(2,1)} %collective-permute-done.18, f32[1024]{0:T(1024)S(1)} %fusion.104, bf16[1024,192]{1,0:T(8,128)(2,1)S(1)} %get-tuple-element.112, ...), kind=kOutput, calls=%fused_computation.39 | convolution fusion | flops 1232338176 | bytes 7481344 | tf_op jit(solution)/shard_map/dot_general | solution.py:22
  174.6 6.2 convert_reduce_fusion.2
  184.5 5.1 fusion.129
  189.6 6.1 convert_reduce_fusion.4
  195.7 4.8 multiply_reduce_fusion
  200.5 4.8 convert_reduce_fusion.5
  205.4 5.3 negate_multiply_fusion
  216.3 3.1 fusion.41
  219.4 3.1 convolution_bitcast_fusion.2
  229.9 2.9 fusion.155
  232.8 3.7 convolution_convert_fusion
  236.5 3.9 fusion.128
  240.4 3.4 convolution_convert_fusion.1
  243.8 2.5 convolution_convert_fusion.2
  246.3 3.0 fusion.156
  249.3 2.5 convolution_convert_fusion.3
  251.8 3.4 fusion.131
  255.2 3.9 fusion.127
  259.1 4.1 add_convert_fusion
  276.2 2.6 select_convert_fusion.3
  291.3 2.6 add_convert_fusion.11
  301.1 2.4 collective-permute-done.62
  308.4 2.8 collective-permute-done.63
  311.2 3.7 collective-permute-start.66
  317.0 2.7 collective-permute-done.65
  332.1 3.1 fusion.42
  342.9 3.0 fusion.18
  355.3 2.3 collective-permute-start.69
  384.0 2.8 collective-permute-start.35
  390.2 2.8 collective-permute-start.51
  404.0 3.2 collective-permute-done.55
  409.5 3.6 collective-permute-done.56
  423.2 6.5 %add_convert_fusion.3 = bf16[768,768]{1,0:T(8,128)(2,1)} fusion(bf16[768,768]{1,0:T(8,128)(2,1)} %collective-permute-done.83, f32[1024,768]{1,0:T(8,128)} %copy-done.121, f32[768]{0:T(1024)S(1)} %copy-done.102, f32[1024]{0:T(1024)S(1)} %copy-done.83, bf16[1024,192]{1,0:T(8,128)(2,1)} %copy-done.24, bf16[1024,192]{1,0:T(8,128)(2,1)} %copy-done.22, ...), kind=kOutput, calls=%fused_computation.92 | convolution fusion | flops 1225457664 | bytes 7085056 | tf_op jit(solution)/shard_map/dot_general | solution.py:22
  430.9 3.7 add_convert_fusion.5
  452.6 22.6 %collective-permute-done.84 = bf16[768,768]{1,0:T(8,128)(2,1)S(1)} collective-permute-done((bf16[768,768]{1,0:T(8,128)(2,1)S(1)}, bf16[768,768]{1,0:T(8,128)(2,1)S(1)}, u32[]{:S(2)}, u32[]{:S(2)}) %collective-permute-start.84) | collective-permute-done | bytes 1179680 | tf_op jit(solution)/shard_map/ppermute | solution.py:18
  477.4 23.1 %collective-permute-done.73 = bf16[768,768]{1,0:T(8,128)(2,1)S(1)} collective-permute-done((bf16[768,768]{1,0:T(8,128)(2,1)S(1)}, bf16[768,768]{1,0:T(8,128)(2,1)S(1)}, u32[]{:S(2)}, u32[]{:S(2)}) %collective-permute-start.73) | collective-permute-done | bytes 1179680 | tf_op jit(solution)/shard_map/ppermute | solution.py:18
  502.7 9.9 %maximum_maximum_fusion = f32[1024,1024]{1,0:T(8,128)} fusion(f32[256,256]{1,0:T(8,128)S(1)} %get-tuple-element.83, f32[256,256]{1,0:T(8,128)S(1)} %get-tuple-element.82, f32[256,256]{1,0:T(8,128)S(1)} %broadcast_in_dim.70, f32[256,256]{1,0:T(8,128)S(1)} %get-tuple-element.84, f32[256,256]{1,0:T(8,128)S(1)} %get-tuple-element.81, ...), kind=kLoop, calls=%fused_computation.13 | loop fusion | flops 15728640 | bytes 7602176 | tf_op jit(solution)/shard_map/concatenate | solution.py:334
  512.6 5.9 collective-permute-done.39
  520.9 2.4 collective-permute-start.77
  525.4 2.4 collective-permute-start.88
  527.8 3.6 collective-permute-done.40
  533.6 11.0 %collective-permute-done.76 = bf16[96,768]{1,0:T(8,128)(2,1)S(1)} collective-permute-done((bf16[96,768]{1,0:T(8,128)(2,1)S(1)}, bf16[96,768]{1,0:T(8,128)(2,1)S(1)}, u32[]{:S(2)}, u32[]{:S(2)}) %collective-permute-start.76) | collective-permute-done | bytes 147488 | tf_op jit(solution)/shard_map/ppermute | solution.py:18
  545.6 9.4 %collective-permute-start.86 = (bf16[96,768]{1,0:T(8,128)(2,1)S(1)}, bf16[96,768]{1,0:T(8,128)(2,1)S(1)}, u32[]{:S(2)}, u32[]{:S(2)}) collective-permute-start(bf16[96,768]{1,0:T(8,128)(2,1)S(1)} %get-tuple-element.143), channel_id=1, source_target_pairs={{0,8},{4,12},{8,0},{12,4},{16,24},{20,28},{24,16},{28,20},{1,9},{5... | collective-permute-start | bytes 442376 | tf_op jit(solution)/shard_map/ppermute | solution.py:18
  556.6 2.3 collective-permute-start.79
  563.4 8.3 %collective-permute-done.44 = bf16[72,768]{1,0:T(8,128)(2,1)S(1)} collective-permute-done((bf16[72,768]{1,0:T(8,128)(2,1)S(1)}, bf16[72,768]{1,0:T(8,128)(2,1)S(1)}, u32[]{:S(2)}, u32[]{:S(2)}) %collective-permute-start.44) | collective-permute-done | bytes 110624 | tf_op jit(solution)/shard_map/ppermute | solution.py:18
  573.7 5.8 collective-permute-done.45
  581.2 5.7 collective-permute-done.46
  590.2 6.6 %collective-permute-done.90 = bf16[96,768]{1,0:T(8,128)(2,1)S(1)} collective-permute-done((bf16[96,768]{1,0:T(8,128)(2,1)S(1)}, bf16[96,768]{1,0:T(8,128)(2,1)S(1)}, u32[]{:S(2)}, u32[]{:S(2)}) %collective-permute-start.90) | collective-permute-done | bytes 147488 | tf_op jit(solution)/shard_map/ppermute | solution.py:18
  597.8 3.4 collective-permute-done.47
  602.5 11.3 %collective-permute-done.81 = bf16[384,768]{1,0:T(8,128)(2,1)S(1)} collective-permute-done((bf16[384,768]{1,0:T(8,128)(2,1)S(1)}, bf16[384,768]{1,0:T(8,128)(2,1)S(1)}, u32[]{:S(2)}, u32[]{:S(2)}) %collective-permute-start.81) | collective-permute-done | bytes 589856 | tf_op jit(solution)/shard_map/ppermute | solution.py:18
  615.4 6.4 %collective-permute-done.92 = bf16[384,768]{1,0:T(8,128)(2,1)S(1)} collective-permute-done((bf16[384,768]{1,0:T(8,128)(2,1)S(1)}, bf16[384,768]{1,0:T(8,128)(2,1)S(1)}, u32[]{:S(2)}, u32[]{:S(2)}) %collective-permute-start.92) | collective-permute-done | bytes 589856 | tf_op jit(solution)/shard_map/ppermute | solution.py:18
  (641 shorter events, 250.2 us)
Async XLA Ops:
  6.1 28.0 %collective-permute-start.3 = (bf16[12,192]{1,0:T(8,128)(2,1)S(1)}, bf16[12,192]{1,0:T(8,128)(2,1)}, u32[]{:S(2)}, u32[]{:S(2)}) collective-permute-start(bf16[12,192]{1,0:T(8,128)(2,1)S(1)} %concatenate.144), channel_id=1, source_target_pairs={{0,3},{1,2},{2,1},{3,0},{4,7},{5,6},{6,5},{7,4},{8,11},{9,10},{10,... | collective-permute-start | bytes 13832 | tf_op jit(solution)/shard_map/ppermute | solution.py:18
  8.5 22.0 %collective-permute-start.4 = (bf16[12,192]{1,0:T(8,128)(2,1)S(1)}, bf16[12,192]{1,0:T(8,128)(2,1)}, u32[]{:S(2)}, u32[]{:S(2)}) collective-permute-start(bf16[12,192]{1,0:T(8,128)(2,1)S(1)} %concatenate.144), channel_id=1, source_target_pairs={{0,2},{1,3},{2,0},{3,1},{4,6},{5,7},{6,4},{7,5},{8,10},{9,11},{10,... | collective-permute-start | bytes 13832 | tf_op jit(solution)/shard_map/ppermute | solution.py:18
  9.2 22.5 %collective-permute-start.5 = (bf16[12,192]{1,0:T(8,128)(2,1)S(1)}, bf16[12,192]{1,0:T(8,128)(2,1)}, u32[]{:S(2)}, u32[]{:S(2)}) collective-permute-start(bf16[12,192]{1,0:T(8,128)(2,1)S(1)} %concatenate.144), channel_id=1, source_target_pairs={{0,1},{1,0},{2,3},{3,2},{4,5},{5,4},{6,7},{7,6},{8,9},{9,8},{10,11... | collective-permute-start | bytes 13832 | tf_op jit(solution)/shard_map/ppermute | solution.py:18
  9.2 54.0 %collective-permute-start.6 = (bf16[3,192,768]{2,1,0:T(8,128)(2,1)}, bf16[3,192,768]{2,1,0:T(8,128)(2,1)}, u32[]{:S(2)}, u32[]{:S(2)}) collective-permute-start(bf16[3,192,768]{2,1,0:T(8,128)(2,1)} %bitcast.107), channel_id=1, source_target_pairs={{0,2},{1,3},{2,0},{3,1},{4,6},{5,7},{6,4},{7,5},{8,10},{9,11},{10,... | collective-permute-start | bytes 2654216 | tf_op jit(solution)/shard_map/ppermute | solution.py:18
  11.0 78.6 %collective-permute-start.8 = (bf16[3,192,768]{2,1,0:T(8,128)(2,1)}, bf16[3,192,768]{2,1,0:T(8,128)(2,1)}, u32[]{:S(2)}, u32[]{:S(2)}) collective-permute-start(bf16[3,192,768]{2,1,0:T(8,128)(2,1)} %bitcast.108), channel_id=1, source_target_pairs={{0,1},{1,0},{2,3},{3,2},{4,5},{5,4},{6,7},{7,6},{8,9},{9,8},{10,11... | collective-permute-start | bytes 2654216 | tf_op jit(solution)/shard_map/ppermute | solution.py:18
  30.5 13.9 %collective-permute-start = (bf16[1024,192]{1,0:T(8,128)(2,1)}, bf16[1024,192]{1,0:T(8,128)(2,1)S(1)}, u32[]{:S(2)}, u32[]{:S(2)}) collective-permute-start(bf16[1024,192]{1,0:T(8,128)(2,1)} %copy.73), channel_id=1, source_target_pairs={{0,3},{1,2},{2,1},{3,0},{4,7},{5,6},{6,5},{7,4},{8,11},{9,10},{10,... | collective-permute-start | bytes 1179656 | tf_op jit(solution)/shard_map/ppermute | solution.py:18
  31.6 25.2 %collective-permute-start.1 = (bf16[1024,192]{1,0:T(8,128)(2,1)}, bf16[1024,192]{1,0:T(8,128)(2,1)S(1)}, u32[]{:S(2)}, u32[]{:S(2)}) collective-permute-start(bf16[1024,192]{1,0:T(8,128)(2,1)} %copy.74), channel_id=1, source_target_pairs={{0,2},{1,3},{2,0},{3,1},{4,6},{5,7},{6,4},{7,5},{8,10},{9,11},{10,... | collective-permute-start | bytes 1179656 | tf_op jit(solution)/shard_map/ppermute | solution.py:18
  34.1 22.8 %collective-permute-start.2 = (bf16[1024,192]{1,0:T(8,128)(2,1)}, bf16[1024,192]{1,0:T(8,128)(2,1)S(1)}, u32[]{:S(2)}, u32[]{:S(2)}) collective-permute-start(bf16[1024,192]{1,0:T(8,128)(2,1)} %copy.75), channel_id=1, source_target_pairs={{0,1},{1,0},{2,3},{3,2},{4,5},{5,4},{6,7},{7,6},{8,9},{9,8},{10,11... | collective-permute-start | bytes 1179656 | tf_op jit(solution)/shard_map/ppermute | solution.py:18
  44.4 18.8 %collective-permute-start.11 = (bf16[192,768]{1,0:T(8,128)(2,1)}, bf16[192,768]{1,0:T(8,128)(2,1)S(1)}, u32[]{:S(2)}, u32[]{:S(2)}) collective-permute-start(bf16[192,768]{1,0:T(8,128)(2,1)} %param.22), channel_id=1, source_target_pairs={{0,2},{1,3},{2,0},{3,1},{4,6},{5,7},{6,4},{7,5},{8,10},{9,11},{10,... | collective-permute-start | bytes 884744 | tf_op jit(solution)/shard_map/ppermute | solution.py:18
  56.9 16.3 %collective-permute-start.23 = (bf16[1024,192]{1,0:T(8,128)(2,1)}, bf16[1024,192]{1,0:T(8,128)(2,1)S(1)}, u32[]{:S(2)}, u32[]{:S(2)}) collective-permute-start(bf16[1024,192]{1,0:T(8,128)(2,1)} %copy.77), channel_id=1, source_target_pairs={{0,3},{1,2},{2,1},{3,0},{4,7},{5,6},{6,5},{7,4},{8,11},{9,10},{10,... | collective-permute-start | bytes 1179656 | tf_op jit(solution)/shard_map/ppermute | solution.py:18
  56.9 28.1 %collective-permute-start.24 = (bf16[1024,192]{1,0:T(8,128)(2,1)}, bf16[1024,192]{1,0:T(8,128)(2,1)S(1)}, u32[]{:S(2)}, u32[]{:S(2)}) collective-permute-start(bf16[1024,192]{1,0:T(8,128)(2,1)} %copy.78), channel_id=1, source_target_pairs={{0,2},{1,3},{2,0},{3,1},{4,6},{5,7},{6,4},{7,5},{8,10},{9,11},{10,... | collective-permute-start | bytes 1179656 | tf_op jit(solution)/shard_map/ppermute | solution.py:18
  63.2 22.3 %collective-permute-start.25 = (bf16[1024,192]{1,0:T(8,128)(2,1)S(1)}, bf16[1024,192]{1,0:T(8,128)(2,1)S(1)}, u32[]{:S(2)}, u32[]{:S(2)}) collective-permute-start(bf16[1024,192]{1,0:T(8,128)(2,1)S(1)} %copy.79), channel_id=1, source_target_pairs={{0,1},{1,0},{2,3},{3,2},{4,5},{5,4},{6,7},{7,6},{8,9},{9,8},{10,11... | collective-permute-start | bytes 1179656 | tf_op jit(solution)/shard_map/ppermute | solution.py:18
  63.2 26.4 %collective-permute-start.7 = (bf16[3,192,768]{2,1,0:T(8,128)(2,1)}, bf16[3,192,768]{2,1,0:T(8,128)(2,1)S(1)}, u32[]{:S(2)}, u32[]{:S(2)}) collective-permute-start(bf16[3,192,768]{2,1,0:T(8,128)(2,1)} %collective-permute-done.6), channel_id=1, source_target_pairs={{0,1},{1,0},{2,3},{3,2},{4,5},{5,4},{6,7},{7,6},{8,9},{9,8},{10,11... | collective-permute-start | bytes 2654216 | tf_op jit(solution)/shard_map/ppermute | solution.py:18
  73.1 12.6 %collective-permute-start.13 = (bf16[192,768]{1,0:T(8,128)(2,1)S(1)}, bf16[192,768]{1,0:T(8,128)(2,1)S(1)}, u32[]{:S(2)}, u32[]{:S(2)}) collective-permute-start(bf16[192,768]{1,0:T(8,128)(2,1)S(1)} %copy-done.60), channel_id=1, source_target_pairs={{0,1},{1,0},{2,3},{3,2},{4,5},{5,4},{6,7},{7,6},{8,9},{9,8},{10,11... | collective-permute-start | bytes 884744 | tf_op jit(solution)/shard_map/ppermute | solution.py:18
  85.0 29.2 %collective-permute-start.18 = (bf16[768,768]{1,0:T(8,128)(2,1)}, bf16[768,768]{1,0:T(8,128)(2,1)}, u32[]{:S(2)}, u32[]{:S(2)}) collective-permute-start(bf16[768,768]{1,0:T(8,128)(2,1)} %param.28), channel_id=1, source_target_pairs={{0,2},{1,3},{2,0},{3,1},{4,6},{5,7},{6,4},{7,5},{8,10},{9,11},{10,... | collective-permute-start | bytes 3538952 | tf_op jit(solution)/shard_map/ppermute | solution.py:18
  85.7 88.8 %collective-permute-start.15 = (bf16[768,768]{1,0:T(8,128)(2,1)}, bf16[768,768]{1,0:T(8,128)(2,1)}, u32[]{:S(2)}, u32[]{:S(2)}) collective-permute-start(bf16[768,768]{1,0:T(8,128)(2,1)} %param.28), channel_id=1, source_target_pairs={{0,1},{1,0},{2,3},{3,2},{4,5},{5,4},{6,7},{7,6},{8,9},{9,8},{10,11... | collective-permute-start | bytes 3538952 | tf_op jit(solution)/shard_map/ppermute | solution.py:18
  87.1 50.8 %collective-permute-start.16 = (bf16[768,768]{1,0:T(8,128)(2,1)}, bf16[768,768]{1,0:T(8,128)(2,1)S(1)}, u32[]{:S(2)}, u32[]{:S(2)}) collective-permute-start(bf16[768,768]{1,0:T(8,128)(2,1)} %param.26), channel_id=1, source_target_pairs={{0,2},{1,3},{2,0},{3,1},{4,6},{5,7},{6,4},{7,5},{8,10},{9,11},{10,... | collective-permute-start | bytes 3538952 | tf_op jit(solution)/shard_map/ppermute | solution.py:18
  96.1 42.9 %collective-permute-start.10 = (bf16[256,1536]{1,0:T(8,128)(2,1)S(1)}, bf16[256,1536]{1,0:T(8,128)(2,1)S(1)}, u32[]{:S(2)}, u32[]{:S(2)}) collective-permute-start(bf16[256,1536]{1,0:T(8,128)(2,1)S(1)} %constant_dynamic-slice_fusion.31), channel_id=1, source_target_pairs={{0,1},{1,0},{2,3},{3,2},{4,5},{5,4},{6,7},{7,6},{8,9},{9,8},{10,11... | collective-permute-start | bytes 2359304 | tf_op jit(solution)/shard_map/ppermute | solution.py:18
  97.7 41.2 %collective-permute-start.9 = (f32[1,1536]{1,0:T(1,128)S(1)}, f32[1,1536]{1,0:T(1,128)S(1)}, u32[]{:S(2)}, u32[]{:S(2)}) collective-permute-start(f32[1,1536]{1,0:T(1,128)S(1)} %broadcast_in_dim.69), channel_id=1, source_target_pairs={{0,1},{1,0},{2,3},{3,2},{4,5},{5,4},{6,7},{7,6},{8,9},{9,8},{10,11... | collective-permute-start | bytes 18440 | tf_op jit(solution)/shard_map/ppermute | solution.py:18
  114.2 48.5 %collective-permute-start.14 = (bf16[768,768]{1,0:T(8,128)(2,1)}, bf16[768,768]{1,0:T(8,128)(2,1)S(1)}, u32[]{:S(2)}, u32[]{:S(2)}) collective-permute-start(bf16[768,768]{1,0:T(8,128)(2,1)} %param.26), channel_id=1, source_target_pairs={{0,1},{1,0},{2,3},{3,2},{4,5},{5,4},{6,7},{7,6},{8,9},{9,8},{10,11... | collective-permute-start | bytes 3538952 | tf_op jit(solution)/shard_map/ppermute | solution.py:18
  137.9 51.7 %collective-permute-start.19 = (bf16[768,768]{1,0:T(8,128)(2,1)}, bf16[768,768]{1,0:T(8,128)(2,1)}, u32[]{:S(2)}, u32[]{:S(2)}) collective-permute-start(bf16[768,768]{1,0:T(8,128)(2,1)} %collective-permute-done.18), channel_id=1, source_target_pairs={{0,1},{1,0},{2,3},{3,2},{4,5},{5,4},{6,7},{7,6},{8,9},{9,8},{10,11... | collective-permute-start | bytes 3538952 | tf_op jit(solution)/shard_map/ppermute | solution.py:18
  138.9 27.1 %collective-permute-start.17 = (bf16[768,768]{1,0:T(8,128)(2,1)}, bf16[768,768]{1,0:T(8,128)(2,1)S(1)}, u32[]{:S(2)}, u32[]{:S(2)}) collective-permute-start(bf16[768,768]{1,0:T(8,128)(2,1)} %copy-done.109), channel_id=1, source_target_pairs={{0,1},{1,0},{2,3},{3,2},{4,5},{5,4},{6,7},{7,6},{8,9},{9,8},{10,11... | collective-permute-start | bytes 3538952 | tf_op jit(solution)/shard_map/ppermute | solution.py:18
  266.2 27.6 %collective-permute-start.20 = (bf16[1024,192]{1,0:T(8,128)(2,1)}, bf16[1024,192]{1,0:T(8,128)(2,1)}, u32[]{:S(2)}, u32[]{:S(2)}) collective-permute-start(bf16[1024,192]{1,0:T(8,128)(2,1)} %get-tuple-element.127), channel_id=1, source_target_pairs={{0,1},{1,0},{2,3},{3,2},{4,5},{5,4},{6,7},{7,6},{8,9},{9,8},{10,11... | collective-permute-start | bytes 1179656 | tf_op jit(solution)/shard_map/ppermute | solution.py:18
  266.8 29.8 %collective-permute-start.21 = (bf16[1024,192]{1,0:T(8,128)(2,1)}, bf16[1024,192]{1,0:T(8,128)(2,1)}, u32[]{:S(2)}, u32[]{:S(2)}) collective-permute-start(bf16[1024,192]{1,0:T(8,128)(2,1)} %get-tuple-element.128), channel_id=1, source_target_pairs={{0,2},{1,3},{2,0},{3,1},{4,6},{5,7},{6,4},{7,5},{8,10},{9,11},{10,... | collective-permute-start | bytes 1179656 | tf_op jit(solution)/shard_map/ppermute | solution.py:18
  267.5 31.3 %collective-permute-start.22 = (bf16[1024,192]{1,0:T(8,128)(2,1)}, bf16[1024,192]{1,0:T(8,128)(2,1)}, u32[]{:S(2)}, u32[]{:S(2)}) collective-permute-start(bf16[1024,192]{1,0:T(8,128)(2,1)} %get-tuple-element.125), channel_id=1, source_target_pairs={{0,3},{1,2},{2,1},{3,0},{4,7},{5,6},{6,5},{7,4},{8,11},{9,10},{10,... | collective-permute-start | bytes 1179656 | tf_op jit(solution)/shard_map/ppermute | solution.py:18
  268.8 20.6 %collective-permute-start.26 = (f32[1,1536]{1,0:T(1,128)}, f32[1,1536]{1,0:T(1,128)}, u32[]{:S(2)}, u32[]{:S(2)}) collective-permute-start(f32[1,1536]{1,0:T(1,128)} %broadcast_in_dim.71), channel_id=1, source_target_pairs={{0,1},{1,0},{2,3},{3,2},{4,5},{5,4},{6,7},{7,6},{8,9},{9,8},{10,11... | collective-permute-start | bytes 18440 | tf_op jit(solution)/shard_map/ppermute | solution.py:18
  278.8 12.5 %collective-permute-start.61 = (bf16[192,768]{1,0:T(8,128)(2,1)}, bf16[192,768]{1,0:T(8,128)(2,1)}, u32[]{:S(2)}, u32[]{:S(2)}) collective-permute-start(bf16[192,768]{1,0:T(8,128)(2,1)} %get-tuple-element.107), channel_id=1, source_target_pairs={{0,1},{1,0},{2,3},{3,2},{4,5},{5,4},{6,7},{7,6},{8,9},{9,8},{10,11... | collective-permute-start | bytes 884744 | tf_op jit(solution)/shard_map/ppermute | solution.py:18
  289.5 31.4 %collective-permute-start.27 = (bf16[256,1536]{1,0:T(8,128)(2,1)}, bf16[256,1536]{1,0:T(8,128)(2,1)}, u32[]{:S(2)}, u32[]{:S(2)}) collective-permute-start(bf16[256,1536]{1,0:T(8,128)(2,1)} %constant_dynamic-slice_fusion.26), channel_id=1, source_target_pairs={{0,1},{1,0},{2,3},{3,2},{4,5},{5,4},{6,7},{7,6},{8,9},{9,8},{10,11... | collective-permute-start | bytes 2359304 | tf_op jit(solution)/shard_map/ppermute | solution.py:18
  298.8 123.7 %collective-permute-start.83 = (bf16[768,768]{1,0:T(8,128)(2,1)}, bf16[768,768]{1,0:T(8,128)(2,1)}, u32[]{:S(2)}, u32[]{:S(2)}) collective-permute-start(bf16[768,768]{1,0:T(8,128)(2,1)} %convolution_convert_fusion), channel_id=1, source_target_pairs={{0,1},{1,0},{2,3},{3,2},{4,5},{5,4},{6,7},{7,6},{8,9},{9,8},{10,11... | collective-permute-start | bytes 3538952 | tf_op jit(solution)/shard_map/ppermute | solution.py:18
  317.0 112.7 %collective-permute-start.72 = (bf16[768,768]{1,0:T(8,128)(2,1)}, bf16[768,768]{1,0:T(8,128)(2,1)}, u32[]{:S(2)}, u32[]{:S(2)}) collective-permute-start(bf16[768,768]{1,0:T(8,128)(2,1)} %convolution_convert_fusion.2), channel_id=1, source_target_pairs={{0,1},{1,0},{2,3},{3,2},{4,5},{5,4},{6,7},{7,6},{8,9},{9,8},{10,11... | collective-permute-start | bytes 3538952 | tf_op jit(solution)/shard_map/ppermute | solution.py:18
  319.7 35.6 %collective-permute-start.49 = (bf16[256,512]{1,0:T(8,128)(2,1)}, bf16[256,512]{1,0:T(8,128)(2,1)}, u32[]{:S(2)}, u32[]{:S(2)}) collective-permute-start(bf16[256,512]{1,0:T(8,128)(2,1)} %constant_dynamic-slice_fusion.19), channel_id=1, source_target_pairs={{0,2},{1,3},{2,0},{3,1},{4,6},{5,7},{6,4},{7,5},{8,10},{9,11},{10,... | collective-permute-start | bytes 786440 | tf_op jit(solution)/shard_map/ppermute | solution.py:18
  320.9 47.6 %collective-permute-start.67 = (bf16[24,768]{1,0:T(8,128)(2,1)}, bf16[24,768]{1,0:T(8,128)(2,1)}, u32[]{:S(2)}, u32[]{:S(2)}) collective-permute-start(bf16[24,768]{1,0:T(8,128)(2,1)} %get-tuple-element.46), channel_id=1, source_target_pairs={{0,8},{4,12},{8,0},{12,4},{16,24},{20,28},{24,16},{28,20},{1,9},{5... | collective-permute-start | bytes 110600 | tf_op jit(solution)/shard_map/ppermute | solution.py:18
  321.6 48.4 %collective-permute-start.68 = (bf16[24,768]{1,0:T(8,128)(2,1)}, bf16[24,768]{1,0:T(8,128)(2,1)}, u32[]{:S(2)}, u32[]{:S(2)}) collective-permute-start(bf16[24,768]{1,0:T(8,128)(2,1)} %get-tuple-element.46), channel_id=1, source_target_pairs={{0,16},{4,20},{8,24},{12,28},{16,0},{20,4},{24,8},{28,12},{1,17},{... | collective-permute-start | bytes 110600 | tf_op jit(solution)/shard_map/ppermute | solution.py:18
  355.3 19.9 %collective-permute-start.69 = (bf16[24,768]{1,0:T(8,128)(2,1)}, bf16[24,768]{1,0:T(8,128)(2,1)}, u32[]{:S(2)}, u32[]{:S(2)}) collective-permute-start(bf16[24,768]{1,0:T(8,128)(2,1)} %get-tuple-element.46), channel_id=1, source_target_pairs={{0,24},{4,28},{8,16},{12,20},{16,8},{20,12},{24,0},{28,4},{1,25},{... | collective-permute-start | bytes 110600 | tf_op jit(solution)/shard_map/ppermute | solution.py:18
  369.9 14.1 %collective-permute-start.50 = (bf16[128,512]{1,0:T(8,128)(2,1)}, bf16[128,512]{1,0:T(8,128)(2,1)S(1)}, u32[]{:S(2)}, u32[]{:S(2)}) collective-permute-start(bf16[128,512]{1,0:T(8,128)(2,1)} %constant_dynamic-slice_fusion.18), channel_id=1, source_target_pairs={{0,4},{4,0},{8,12},{12,8},{16,20},{20,16},{24,28},{28,24},{1,5},{5... | collective-permute-start | bytes 393224 | tf_op jit(solution)/shard_map/ppermute | solution.py:18
  394.4 40.3 %collective-permute-start.28 = (bf16[1024,192]{1,0:T(8,128)(2,1)}, bf16[1024,192]{1,0:T(8,128)(2,1)}, u32[]{:S(2)}, u32[]{:S(2)}) collective-permute-start(bf16[1024,192]{1,0:T(8,128)(2,1)} %get-tuple-element.119), channel_id=1, source_target_pairs={{0,1},{1,0},{2,3},{3,2},{4,5},{5,4},{6,7},{7,6},{8,9},{9,8},{10,11... | collective-permute-start | bytes 1179656 | tf_op jit(solution)/shard_map/ppermute | solution.py:18
  395.2 19.0 %collective-permute-start.70 = (bf16[96,768]{1,0:T(8,128)(2,1)}, bf16[96,768]{1,0:T(8,128)(2,1)}, u32[]{:S(2)}, u32[]{:S(2)}) collective-permute-start(bf16[96,768]{1,0:T(8,128)(2,1)} %constant_dynamic-update-slice_fusion.14), channel_id=1, source_target_pairs={{0,4},{4,0},{8,12},{12,8},{16,20},{20,16},{24,28},{28,24},{1,5},{5... | collective-permute-start | bytes 442376 | tf_op jit(solution)/shard_map/ppermute | solution.py:18
  413.1 23.6 %collective-permute-start.29 = (bf16[1024,192]{1,0:T(8,128)(2,1)}, bf16[1024,192]{1,0:T(8,128)(2,1)}, u32[]{:S(2)}, u32[]{:S(2)}) collective-permute-start(bf16[1024,192]{1,0:T(8,128)(2,1)} %get-tuple-element.120), channel_id=1, source_target_pairs={{0,2},{1,3},{2,0},{3,1},{4,6},{5,7},{6,4},{7,5},{8,10},{9,11},{10,... | collective-permute-start | bytes 1179656 | tf_op jit(solution)/shard_map/ppermute | solution.py:18
  421.9 17.3 %collective-permute-start.30 = (bf16[1024,192]{1,0:T(8,128)(2,1)}, bf16[1024,192]{1,0:T(8,128)(2,1)}, u32[]{:S(2)}, u32[]{:S(2)}) collective-permute-start(bf16[1024,192]{1,0:T(8,128)(2,1)} %get-tuple-element.117), channel_id=1, source_target_pairs={{0,3},{1,2},{2,1},{3,0},{4,7},{5,6},{6,5},{7,4},{8,11},{9,10},{10,... | collective-permute-start | bytes 1179656 | tf_op jit(solution)/shard_map/ppermute | solution.py:18
  422.5 23.8 %collective-permute-start.38 = (bf16[576,768]{1,0:T(8,128)(2,1)}, bf16[576,768]{1,0:T(8,128)(2,1)}, u32[]{:S(2)}, u32[]{:S(2)}) collective-permute-start(bf16[576,768]{1,0:T(8,128)(2,1)} %bitcast.106), channel_id=1, source_target_pairs={{0,1},{1,0},{2,3},{3,2},{4,5},{5,4},{6,7},{7,6},{8,9},{9,8},{10,11... | collective-permute-start | bytes 2654216 | tf_op jit(solution)/shard_map/ppermute | solution.py:18
  429.7 13.4 %collective-permute-start.58 = (bf16[256,512]{1,0:T(8,128)(2,1)}, bf16[256,512]{1,0:T(8,128)(2,1)}, u32[]{:S(2)}, u32[]{:S(2)}) collective-permute-start(bf16[256,512]{1,0:T(8,128)(2,1)} %constant_dynamic-update-slice_fusion.18), channel_id=1, source_target_pairs={{0,2},{1,3},{2,0},{3,1},{4,6},{5,7},{6,4},{7,5},{8,10},{9,11},{10,... | collective-permute-start | bytes 786440 | tf_op jit(solution)/shard_map/ppermute | solution.py:18
  434.7 16.6 %collective-permute-start.82 = (bf16[768,768]{1,0:T(8,128)(2,1)}, bf16[768,768]{1,0:T(8,128)(2,1)}, u32[]{:S(2)}, u32[]{:S(2)}) collective-permute-start(bf16[768,768]{1,0:T(8,128)(2,1)} %convolution_convert_fusion.1), channel_id=1, source_target_pairs={{0,1},{1,0},{2,3},{3,2},{4,5},{5,4},{6,7},{7,6},{8,9},{9,8},{10,11... | collective-permute-start | bytes 3538952 | tf_op jit(solution)/shard_map/ppermute | solution.py:18
  436.7 40.7 %collective-permute-start.71 = (bf16[768,768]{1,0:T(8,128)(2,1)}, bf16[768,768]{1,0:T(8,128)(2,1)}, u32[]{:S(2)}, u32[]{:S(2)}) collective-permute-start(bf16[768,768]{1,0:T(8,128)(2,1)} %convolution_convert_fusion.3), channel_id=1, source_target_pairs={{0,1},{1,0},{2,3},{3,2},{4,5},{5,4},{6,7},{7,6},{8,9},{9,8},{10,11... | collective-permute-start | bytes 3538952 | tf_op jit(solution)/shard_map/ppermute | solution.py:18
  439.2 73.4 %collective-permute-start.37 = (bf16[576,768]{1,0:T(8,128)(2,1)}, bf16[576,768]{1,0:T(8,128)(2,1)}, u32[]{:S(2)}, u32[]{:S(2)}) collective-permute-start(bf16[576,768]{1,0:T(8,128)(2,1)} %bitcast.105), channel_id=1, source_target_pairs={{0,1},{1,0},{2,3},{3,2},{4,5},{5,4},{6,7},{7,6},{8,9},{9,8},{10,11... | collective-permute-start | bytes 2654216 | tf_op jit(solution)/shard_map/ppermute | solution.py:18
  446.3 28.8 %collective-permute-start.84 = (bf16[768,768]{1,0:T(8,128)(2,1)S(1)}, bf16[768,768]{1,0:T(8,128)(2,1)S(1)}, u32[]{:S(2)}, u32[]{:S(2)}) collective-permute-start(bf16[768,768]{1,0:T(8,128)(2,1)S(1)} %copy-done.111), channel_id=1, source_target_pairs={{0,2},{1,3},{2,0},{3,1},{4,6},{5,7},{6,4},{7,5},{8,10},{9,11},{10,... | collective-permute-start | bytes 3538952 | tf_op jit(solution)/shard_map/ppermute | solution.py:18
  448.7 51.8 %collective-permute-start.73 = (bf16[768,768]{1,0:T(8,128)(2,1)S(1)}, bf16[768,768]{1,0:T(8,128)(2,1)S(1)}, u32[]{:S(2)}, u32[]{:S(2)}) collective-permute-start(bf16[768,768]{1,0:T(8,128)(2,1)S(1)} %copy-done.112), channel_id=1, source_target_pairs={{0,2},{1,3},{2,0},{3,1},{4,6},{5,7},{6,4},{7,5},{8,10},{9,11},{10,... | collective-permute-start | bytes 3538952 | tf_op jit(solution)/shard_map/ppermute | solution.py:18
  451.3 67.2 %collective-permute-start.39 = (bf16[576,768]{1,0:T(8,128)(2,1)S(1)}, bf16[576,768]{1,0:T(8,128)(2,1)S(1)}, u32[]{:S(2)}, u32[]{:S(2)}) collective-permute-start(bf16[576,768]{1,0:T(8,128)(2,1)S(1)} %fusion.38), channel_id=1, source_target_pairs={{0,2},{1,3},{2,0},{3,1},{4,6},{5,7},{6,4},{7,5},{8,10},{9,11},{10,... | collective-permute-start | bytes 2654216 | tf_op jit(solution)/shard_map/ppermute | solution.py:18
  477.0 43.6 %collective-permute-start.85 = (bf16[384,768]{1,0:T(8,128)(2,1)S(1)}, bf16[384,768]{1,0:T(8,128)(2,1)S(1)}, u32[]{:S(2)}, u32[]{:S(2)}) collective-permute-start(bf16[384,768]{1,0:T(8,128)(2,1)S(1)} %constant_dynamic-slice_fusion.6), channel_id=1, source_target_pairs={{0,4},{4,0},{8,12},{12,8},{16,20},{20,16},{24,28},{28,24},{1,5},{5... | collective-permute-start | bytes 1769480 | tf_op jit(solution)/shard_map/ppermute | solution.py:18
  502.2 18.3 %collective-permute-start.74 = (bf16[384,768]{1,0:T(8,128)(2,1)S(1)}, bf16[384,768]{1,0:T(8,128)(2,1)S(1)}, u32[]{:S(2)}, u32[]{:S(2)}) collective-permute-start(bf16[384,768]{1,0:T(8,128)(2,1)S(1)} %constant_dynamic-slice_fusion.10), channel_id=1, source_target_pairs={{0,4},{4,0},{8,12},{12,8},{16,20},{20,16},{24,28},{28,24},{1,5},{5... | collective-permute-start | bytes 1769480 | tf_op jit(solution)/shard_map/ppermute | solution.py:18
  523.4 21.2 %collective-permute-start.76 = (bf16[96,768]{1,0:T(8,128)(2,1)S(1)}, bf16[96,768]{1,0:T(8,128)(2,1)S(1)}, u32[]{:S(2)}, u32[]{:S(2)}) collective-permute-start(bf16[96,768]{1,0:T(8,128)(2,1)S(1)} %get-tuple-element.148), channel_id=1, source_target_pairs={{0,16},{4,20},{8,24},{12,28},{16,0},{20,4},{24,8},{28,12},{1,17},{... | collective-permute-start | bytes 442376 | tf_op jit(solution)/shard_map/ppermute | solution.py:18
  523.4 21.2 %collective-permute-start.75 = (bf16[96,768]{1,0:T(8,128)(2,1)S(1)}, bf16[96,768]{1,0:T(8,128)(2,1)S(1)}, u32[]{:S(2)}, u32[]{:S(2)}) collective-permute-start(bf16[96,768]{1,0:T(8,128)(2,1)S(1)} %get-tuple-element.146), channel_id=1, source_target_pairs={{0,8},{4,12},{8,0},{12,4},{16,24},{20,28},{24,16},{28,20},{1,9},{5... | collective-permute-start | bytes 442376 | tf_op jit(solution)/shard_map/ppermute | solution.py:18
  525.4 33.6 %collective-permute-start.88 = (bf16[96,768]{1,0:T(8,128)(2,1)S(1)}, bf16[96,768]{1,0:T(8,128)(2,1)S(1)}, u32[]{:S(2)}, u32[]{:S(2)}) collective-permute-start(bf16[96,768]{1,0:T(8,128)(2,1)S(1)} %get-tuple-element.144), channel_id=1, source_target_pairs={{0,24},{4,28},{8,16},{12,20},{16,8},{20,12},{24,0},{28,4},{1,25},{... | collective-permute-start | bytes 442376 | tf_op jit(solution)/shard_map/ppermute | solution.py:18
  531.5 29.7 %collective-permute-start.87 = (bf16[96,768]{1,0:T(8,128)(2,1)S(1)}, bf16[96,768]{1,0:T(8,128)(2,1)S(1)}, u32[]{:S(2)}, u32[]{:S(2)}) collective-permute-start(bf16[96,768]{1,0:T(8,128)(2,1)S(1)} %get-tuple-element.145), channel_id=1, source_target_pairs={{0,16},{4,20},{8,24},{12,28},{16,0},{20,4},{24,8},{28,12},{1,17},{... | collective-permute-start | bytes 442376 | tf_op jit(solution)/shard_map/ppermute | solution.py:18
  531.7 14.0 %collective-permute-start.43 = (bf16[72,768]{1,0:T(8,128)(2,1)S(1)}, bf16[72,768]{1,0:T(8,128)(2,1)S(1)}, u32[]{:S(2)}, u32[]{:S(2)}) collective-permute-start(bf16[72,768]{1,0:T(8,128)(2,1)S(1)} %get-tuple-element.152), channel_id=1, source_target_pairs={{0,24},{4,28},{8,16},{12,20},{16,8},{20,12},{24,0},{28,4},{1,25},{... | collective-permute-start | bytes 331784 | tf_op jit(solution)/shard_map/ppermute | solution.py:18
  544.6 12.0 %collective-permute-start.42 = (bf16[72,768]{1,0:T(8,128)(2,1)S(1)}, bf16[72,768]{1,0:T(8,128)(2,1)S(1)}, u32[]{:S(2)}, u32[]{:S(2)}) collective-permute-start(bf16[72,768]{1,0:T(8,128)(2,1)S(1)} %get-tuple-element.153), channel_id=1, source_target_pairs={{0,16},{4,20},{8,24},{12,28},{16,0},{20,4},{24,8},{28,12},{1,17},{... | collective-permute-start | bytes 331784 | tf_op jit(solution)/shard_map/ppermute | solution.py:18
  544.6 12.0 %collective-permute-start.41 = (bf16[72,768]{1,0:T(8,128)(2,1)S(1)}, bf16[72,768]{1,0:T(8,128)(2,1)S(1)}, u32[]{:S(2)}, u32[]{:S(2)}) collective-permute-start(bf16[72,768]{1,0:T(8,128)(2,1)S(1)} %get-tuple-element.151), channel_id=1, source_target_pairs={{0,8},{4,12},{8,0},{12,4},{16,24},{20,28},{24,16},{28,20},{1,9},{5... | collective-permute-start | bytes 331784 | tf_op jit(solution)/shard_map/ppermute | solution.py:18
  545.6 15.5 %collective-permute-start.86 = (bf16[96,768]{1,0:T(8,128)(2,1)S(1)}, bf16[96,768]{1,0:T(8,128)(2,1)S(1)}, u32[]{:S(2)}, u32[]{:S(2)}) collective-permute-start(bf16[96,768]{1,0:T(8,128)(2,1)S(1)} %get-tuple-element.143), channel_id=1, source_target_pairs={{0,8},{4,12},{8,0},{12,4},{16,24},{20,28},{24,16},{28,20},{1,9},{5... | collective-permute-start | bytes 442376 | tf_op jit(solution)/shard_map/ppermute | solution.py:18
  556.6 30.4 %collective-permute-start.78 = (bf16[96,768]{1,0:T(8,128)(2,1)S(1)}, bf16[96,768]{1,0:T(8,128)(2,1)S(1)}, u32[]{:S(2)}, u32[]{:S(2)}) collective-permute-start(bf16[96,768]{1,0:T(8,128)(2,1)S(1)} %get-tuple-element.44), channel_id=1, source_target_pairs={{0,8},{4,12},{8,0},{12,4},{16,24},{20,28},{24,16},{28,20},{1,9},{5... | collective-permute-start | bytes 442376 | tf_op jit(solution)/shard_map/ppermute | solution.py:18
  556.6 31.4 %collective-permute-start.79 = (bf16[96,768]{1,0:T(8,128)(2,1)S(1)}, bf16[96,768]{1,0:T(8,128)(2,1)S(1)}, u32[]{:S(2)}, u32[]{:S(2)}) collective-permute-start(bf16[96,768]{1,0:T(8,128)(2,1)S(1)} %get-tuple-element.44), channel_id=1, source_target_pairs={{0,16},{4,20},{8,24},{12,28},{16,0},{20,4},{24,8},{28,12},{1,17},{... | collective-permute-start | bytes 442376 | tf_op jit(solution)/shard_map/ppermute | solution.py:18
  559.0 30.6 %collective-permute-start.80 = (bf16[96,768]{1,0:T(8,128)(2,1)S(1)}, bf16[96,768]{1,0:T(8,128)(2,1)S(1)}, u32[]{:S(2)}, u32[]{:S(2)}) collective-permute-start(bf16[96,768]{1,0:T(8,128)(2,1)S(1)} %get-tuple-element.44), channel_id=1, source_target_pairs={{0,24},{4,28},{8,16},{12,20},{16,8},{20,12},{24,0},{28,4},{1,25},{... | collective-permute-start | bytes 442376 | tf_op jit(solution)/shard_map/ppermute | solution.py:18
  561.3 28.9 %collective-permute-start.89 = (bf16[96,768]{1,0:T(8,128)(2,1)S(1)}, bf16[96,768]{1,0:T(8,128)(2,1)S(1)}, u32[]{:S(2)}, u32[]{:S(2)}) collective-permute-start(bf16[96,768]{1,0:T(8,128)(2,1)S(1)} %get-tuple-element.42), channel_id=1, source_target_pairs={{0,8},{4,12},{8,0},{12,4},{16,24},{20,28},{24,16},{28,20},{1,9},{5... | collective-permute-start | bytes 442376 | tf_op jit(solution)/shard_map/ppermute | solution.py:18
  588.0 13.2 %collective-permute-start.47 = (bf16[288,768]{1,0:T(8,128)(2,1)S(1)}, bf16[288,768]{1,0:T(8,128)(2,1)S(1)}, u32[]{:S(2)}, u32[]{:S(2)}) collective-permute-start(bf16[288,768]{1,0:T(8,128)(2,1)S(1)} %constant_dynamic-update-slice_fusion.26), channel_id=1, source_target_pairs={{0,4},{4,0},{8,12},{12,8},{16,20},{20,16},{24,28},{28,24},{1,5},{5... | collective-permute-start | bytes 1327112 | tf_op jit(solution)/shard_map/ppermute | solution.py:18
  589.7 24.1 %collective-permute-start.81 = (bf16[384,768]{1,0:T(8,128)(2,1)S(1)}, bf16[384,768]{1,0:T(8,128)(2,1)S(1)}, u32[]{:S(2)}, u32[]{:S(2)}) collective-permute-start(bf16[384,768]{1,0:T(8,128)(2,1)S(1)} %constant_dynamic-update-slice_fusion.8), channel_id=1, source_target_pairs={{0,4},{4,0},{8,12},{12,8},{16,20},{20,16},{24,28},{28,24},{1,5},{5... | collective-permute-start | bytes 1769480 | tf_op jit(solution)/shard_map/ppermute | solution.py:18
  597.0 24.8 %collective-permute-start.92 = (bf16[384,768]{1,0:T(8,128)(2,1)S(1)}, bf16[384,768]{1,0:T(8,128)(2,1)S(1)}, u32[]{:S(2)}, u32[]{:S(2)}) collective-permute-start(bf16[384,768]{1,0:T(8,128)(2,1)S(1)} %constant_dynamic-update-slice_fusion.2), channel_id=1, source_target_pairs={{0,4},{4,0},{8,12},{12,8},{16,20},{20,16},{24,28},{28,24},{1,5},{5... | collective-permute-start | bytes 1769480 | tf_op jit(solution)/shard_map/ppermute | solution.py:18
  (165 other events, 2895.9 us)

commit v2 on v0

v2 whole, which is shorter than its diff:
```python
import functools

import jax
import jax.numpy as jnp
from jax import lax
from jax.experimental import pallas as pl
from jax.experimental.pallas import tpu as pltpu
from jax.sharding import PartitionSpec as P

D = 768
PAIR = 1024
WIN = 256
LEN = 2048
CHAN = 4
EPSILON = 1e-05
BF = jnp.bfloat16
F32 = jnp.float32
SMEM = pltpu.SMEM
MIB = 1024 * 1024
RB = 512
INPUT_COST = 72


def flip(values, axis, mask):
    size = lax.axis_size(axis)
    return lax.ppermute(values, axis, [(i, i ^ mask) for i in range(size)])


def dot_f32(left, right, dims):
    return lax.dot_general(left, right, (dims, ((), ())), preferred_element_type=F32)


def mm(left, right):
    return dot_f32(left, right, ((1,), (0,)))


def mm_t(left, right):
    return dot_f32(left, right, ((1,), (1,)))


def t_mm(left, right):
    return dot_f32(left, right, ((0,), (0,)))


def pick(pieces, index):
    low, high = index % 2 == 1, index // 2 == 1
    a, b, c, d = pieces
    a, b = jnp.where(low, b, a), jnp.where(low, a, b)
    c, d = jnp.where(low, d, c), jnp.where(low, c, d)
    a, c = jnp.where(high, c, a), jnp.where(high, a, c)
    b, d = jnp.where(high, d, b), jnp.where(high, b, d)
    return [a, b, c, d]


def call(
    kernel, steps, views, out_views, out_shape, scratch=(), flops=0, heavy=0, mem=18, tokens=()
):
    vm = pl.BlockSpec(memory_space=pltpu.VMEM)
    specs = [pl.BlockSpec(memory_space=SMEM) if v is None else vm for v in views]
    every = list(views) + list(out_views)
    first_out, count = len(views) + len(tokens), len(out_views)

    def unrolled(*refs):
        used = refs[: len(views)] + refs[first_out : first_out + count]
        refs[first_out + count][...] = jnp.zeros((8, 128), F32)
        for step in range(steps):
            parts = [r if v is None else v(r, step) for v, r in zip(every, used)]
            kernel(step, steps, *parts, *refs[first_out + count + 1 :])

    run = pl.pallas_call(
        unrolled,
        in_specs=specs + [vm] * len(tokens),
        out_specs=[vm] * (count + 1),
        out_shape=list(out_shape) + [shape_of((8, 128), F32)],
        scratch_shapes=list(scratch),
        compiler_params=pltpu.CompilerParams(vmem_limit_bytes=mem * MIB),
        cost_estimate=pl.CostEstimate(
            flops=flops, bytes_accessed=flops // 300, transcendentals=heavy
        ),
    )
    return lambda *operands: run(*operands, *tokens)


def whole(ref, step):
    return ref


def rows_of(size):
    return lambda ref, step: ref.at[step * size : (step + 1) * size]


def cols_of(size):
    return lambda ref, step: ref.at[:, step * size : (step + 1) * size]


def shape_of(shape, dtype):
    return jax.ShapeDtypeStruct(shape, dtype)


def live_block(info_ref, step, size):
    ids = lax.broadcasted_iota(jnp.int32, (size, 1), 0) + step * size
    return (ids < info_ref[0]).astype(F32)


def normalize(values):
    row_mean = jnp.mean(values, axis=1, keepdims=True)
    spread = jnp.mean(values * values, axis=1, keepdims=True) - row_mean * row_mean
    inv_scale = lax.rsqrt(spread + EPSILON)
    return (values - row_mean) * inv_scale, inv_scale


def norm_back(grad_out, centred, inv_scale, gain_vals):
    scaled = grad_out * gain_vals
    plain = jnp.mean(scaled, axis=1, keepdims=True)
    crossed = jnp.mean(scaled * centred, axis=1, keepdims=True)
    return inv_scale * (scaled - plain - centred * crossed)


def col_sum(values):
    return jnp.sum(values, axis=0, keepdims=True)


def gelu_pair(u):
    c0, c1 = 0.7978845608, 0.044715
    sq = u * u
    half = 0.5 + 0.5 * jnp.tanh(u * (c0 + c0 * c1 * sq))
    slope = half * (1.0 + (1.0 - half) * (u * (2.0 * c0 + 6.0 * c0 * c1 * sq)))
    return u * half, slope


def add_into(ref, step, values):
    ref[...] = values if step == 0 else ref[...] + values


def vector_kernel(step, count, info, small_ref, vec_ref, up_ref):
    width, me = D // CHAN, info[2]
    for k in range(CHAN):
        cols = slice(k * width, (k + 1) * width)
        own = small_ref[me ^ k].astype(F32)
        pair = small_ref[k - k % 2 + (k % 2 + info[1]) % 2].astype(F32)
        vec_ref[0:2, cols] = own[0:2]
        vec_ref[2:4, cols] = pair[2:4]
        vec_ref[4:8, cols] = own[4:8]
        ups = small_ref[k].astype(F32)
        for t in range(CHAN):
            up_ref[k : k + 1, t * width : (t + 1) * width] = ups[8 + t : 9 + t]


def vectors(info, small, tokens=()):
    return call(
        vector_kernel,
        1,
        [None, whole],
        [whole, whole],
        [shape_of((8, D), F32), shape_of((CHAN, D), F32)],
        mem=16,
        tokens=tokens,
    )(info, small)


def chan_row(info, r):
    return (r - r % 2) + (r % 2 + info[1]) % 2


def project_kernel(
    step, count, info, x_ref, vec, w_0, w_1, w_2, w_3, n_ref, gate_ref, v_ref, s_ref, tot_ref, w_ref
):
    width = D // CHAN
    if step == 0:
        for r, ref in enumerate((w_0, w_1, w_2, w_3)):
            row = pl.multiple_of(chan_row(info, r) * width, width)
            for k in range(3):
                w_ref[k, pl.ds(row, width)] = ref[k * width : (k + 1) * width]
    live = live_block(info, step, RB)
    centred, _ = normalize(x_ref[...].astype(F32).T)
    normed = (centred * vec[0:1] + vec[1:2]).astype(BF)
    n_ref[...] = normed
    gate_ref[...] = jax.nn.sigmoid(mm_t(normed, w_ref[0]) + vec[2:3]).astype(BF)
    keys = live * jnp.exp(mm_t(normed, w_ref[1]))
    vals = mm_t(normed, w_ref[2]) + vec[3:4]
    carried = keys * vals
    v_ref[...] = vals.astype(BF)
    s_ref[:, :D] = carried.astype(BF)
    s_ref[:, D:] = keys.astype(BF)
    add_into(tot_ref, step, jnp.concatenate([col_sum(carried), col_sum(keys)], axis=1))


def project(info, x_t, vec, weights, tokens=()):
    rows = x_t.shape[1]
    return call(
        project_kernel,
        rows // RB,
        [None, cols_of(RB)] + [whole] * 5,
        [rows_of(RB)] * 4 + [whole] * 2,
        [shape_of((rows, D), BF)] * 3
        + [shape_of((rows, 2 * D), BF), shape_of((1, 2 * D), F32), shape_of((3, D, D), BF)],
        flops=6 * rows * D * D,
        heavy=rows * D * 2,
        tokens=tokens,
    )(info, x_t, vec, *weights)


def side_masks():
    row_ids = lax.broadcasted_iota(jnp.int32, (WIN, WIN), 0)
    col_ids = lax.broadcasted_iota(jnp.int32, (WIN, WIN), 1)
    return col_ids > row_ids, col_ids < row_ids


def neighbours(info, step, count, ref, halo_ref):
    half = info[1]
    if step == 0:
        left = jnp.where(half == 1, halo_ref[:WIN], jnp.zeros_like(halo_ref[:WIN]))
    else:
        left = ref[(step - 1) * WIN : step * WIN]
    if step == count - 1:
        right = jnp.where(half == 0, halo_ref[:WIN], jnp.zeros_like(halo_ref[:WIN]))
    else:
        right = ref[(step + 1) * WIN : (step + 2) * WIN]
    return left, ref[step * WIN : (step + 1) * WIN], right


def pair_total(tot_ref, far_ref):
    far = far_ref[WIN : WIN + 16].astype(F32)
    return tot_ref[...] + (far[0:1] + far[1:2])


def pair_cols(ref, step, count, side):
    col = (step + side) % count
    return ref[step * WIN : (step + 1) * WIN, col * WIN : (col + 1) * WIN]


def mix_kernel(
    step, count, info, pair_ref, s_ref, far_ref, tot_ref, gate_ref, x_ref, vec,
    w_0, w_1, w_2, w_3, term_ref, ratio_ref, inv_ref, mixed_ref, res_ref, n_ref, w_ref,
):
    width = D // CHAN
    if step == 0:
        for r, ref in enumerate((w_0, w_1, w_2, w_3)):
            row = pl.multiple_of(chan_row(info, r) * width, width)
            w_ref[pl.ds(row, width)] = ref[3 * width :]
    live = live_block(info, step, WIN)
    before, after_own = side_masks()
    left, own, right = neighbours(info, step, count, s_ref, far_ref)
    grow = [jnp.exp(pair_cols(pair_ref, step, count, k).astype(F32)) - 1.0 for k in (-1, 0, 1)]
    term_l = jnp.where(before, grow[0], 0.0).astype(BF)
    term_o = grow[1].astype(BF)
    term_r = jnp.where(after_own, grow[2], 0.0).astype(BF)
    term_ref[:, :WIN] = term_l
    term_ref[:, WIN : 2 * WIN] = term_o
    term_ref[:, 2 * WIN :] = term_r
    merged = mm(term_l, left) + mm(term_o, own) + mm(term_r, right)
    merged = merged + pair_total(tot_ref, far_ref)
    inverse = 1.0 / merged[:, D:]
    ratio = merged[:, :D] * inverse
    mixed = (live * gate_ref[...].astype(F32) * ratio).astype(BF)
    ratio_ref[...] = ratio.astype(BF)
    inv_ref[...] = inverse
    mixed_ref[...] = mixed
    residual = x_ref[...].astype(F32).T + live * (mm(mixed, w_ref[...]) + vec[4:5])
    res_ref[...] = residual
    centred, _ = normalize(residual)
    n_ref[...] = (centred * vec[5:6] + vec[6:7]).astype(BF)


def mix(info, pair_bias, stacked, message, totals, gate, x_t, vec, weights, tokens=()):
    rows = x_t.shape[1]
    return call(
        mix_kernel,
        rows // WIN,
        [None, whole, whole, whole, whole, rows_of(WIN), cols_of(WIN)] + [whole] * 5,
        [rows_of(WIN)] * 6 + [whole],
        [
            shape_of((rows, 3 * WIN), BF),
            shape_of((rows, D), BF),
            shape_of((rows, D), F32),
            shape_of((rows, D), BF),
            shape_of((rows, D), F32),
            shape_of((rows, D), BF),
            shape_of((D, D), BF),
        ],
        flops=2 * rows * D * (6 * WIN + D),
        heavy=rows * D * 2,
        tokens=tokens,
    )(info, pair_bias, stacked, message, totals, gate, x_t, vec, *weights)


def feed_kernel(first, final, extra, step, count, info, n_ref, cot_ref, shift_ref, w_ref, *rest):
    rest = list(rest)
    state = [rest.pop(0), rest.pop(0)] if not first else None
    final_refs = [rest.pop(0), rest.pop(0)] if final else None
    extra_ref = rest.pop(0) if extra else None
    sum_ref, into_ref, ups_ref = rest.pop(0), rest.pop(0), rest.pop(0)
    weight_grad = rest.pop(0)
    if first:
        rest.pop(0)[...] = (cot := cot_ref[...].T)
    else:
        cot = cot_ref[...]
    grad_sc, act_sc, hidden_sc = rest
    live = lax.broadcasted_iota(jnp.int32, (n_ref.shape[0], 1), 0) < info[0]
    grad_sc[...] = jnp.where(live, cot, jnp.zeros_like(cot))
    grad = grad_sc[...]
    for f in range(0, D, WIN):
        cols, low = slice(f, f + WIN), slice(D + f, D + f + WIN)
        hidden = mm(n_ref[...], w_ref[:D, cols]) + shift_ref[:, cols]
        act, slope = gelu_pair(hidden)
        act = act.astype(BF)
        hidden_grad = (mm_t(grad, w_ref[low]) * slope).astype(BF)
        act_sc[:, cols] = act
        hidden_sc[:, cols] = hidden_grad
        ups_ref[:, cols] = col_sum(hidden_grad.astype(F32))
        of_up = t_mm(n_ref[...], hidden_grad)
        of_down = t_mm(act, grad)
        if extra:
            of_up = of_up + extra_ref[:D, cols].astype(F32)
            of_down = of_down + extra_ref[low].astype(F32)
        weight_grad[:D, cols] = of_up.astype(BF)
        weight_grad[low] = of_down.astype(BF)
    total = mm(act_sc[...], w_ref[D:])
    into = mm_t(hidden_sc[...], w_ref[:D])
    if not first:
        total, into = total + state[0][...], into + state[1][...]
    into_ref[...] = into
    if final:
        res_ref, vec = final_refs
        out = res_ref[...] + jnp.where(live, total + vec[7:8], 0.0)
        sum_ref[...] = out.T.astype(BF)
    else:
        sum_ref[...] = total


def feed(info, normed, cot, shift, weights, state=None, final=None, extra=None, tokens=()):
    rows = normed.shape[0]
    operands = [info, normed, cot, shift, weights]
    operands += list(state or ()) + list(final or ()) + ([] if extra is None else [extra])
    out_shape = [
        shape_of((rows, D), F32) if final is None else shape_of((D, rows), BF),
        shape_of((rows, D), F32),
        shape_of((1, D), F32),
    ]
    out_shape.append(shape_of((2 * D, D), BF))
    if state is None:
        out_shape.append(shape_of((rows, D), BF))
    flags = (state is None, final is not None, extra is not None)
    return call(
        functools.partial(feed_kernel, *flags),
        1,
        [None] + [whole] * (len(operands) - 1),
        [whole] * len(out_shape),
        out_shape,
        scratch=[pltpu.VMEM((rows, D), BF)] * 3,
        flops=12 * rows * D * D,
        heavy=rows * D,
        mem=18,
        tokens=tokens,
    )(*operands)


def branch_kernel(
    step, count, info, into_ref, res_ref, cot_ref, vec, w_ref, ratio_ref, inv_ref, gate_ref,
    resg_ref, branch_ref, qg_ref, g_ref, tot_ref, cols_ref,
):
    live = live_block(info, step, RB)
    upstream = into_ref[...]
    centred, inv_scale = normalize(res_ref[...])
    cot = cot_ref[...].astype(F32)
    res_grad = cot + norm_back(upstream, centred, inv_scale, vec[5:6])
    resg_ref[...] = res_grad
    branch = (live * res_grad).astype(BF)
    branch_ref[...] = branch
    mixed_grad = live * mm_t(branch, w_ref[...])
    gate, ratio = gate_ref[...].astype(F32), ratio_ref[...].astype(F32)
    pulled = mixed_grad * gate
    qg_ref[...] = (pulled * ratio * (1.0 - gate)).astype(BF)
    num = pulled * inv_ref[...]
    den = -num * ratio
    g_ref[:, :D] = num.astype(BF)
    g_ref[:, D:] = den.astype(BF)
    add_into(tot_ref, step, jnp.concatenate([col_sum(num), col_sum(den)], axis=1))
    cols = [
        col_sum(upstream * centred),
        col_sum(upstream),
        col_sum(branch.astype(F32)),
        col_sum(live * cot),
        jnp.zeros((4, D), F32),
    ]
    add_into(cols_ref, step, jnp.concatenate(cols, axis=0))


def branch_back(info, into, residual, cot, vec, out_w, ratio, inverse, gate, tokens=()):
    rows = cot.shape[0]
    wide = rows_of(RB)
    return call(
        branch_kernel,
        rows // RB,
        [None, wide, wide, wide, whole, whole, wide, wide, wide],
        [wide, wide, wide, wide, whole, whole],
        [
            shape_of((rows, D), F32),
            shape_of((rows, D), BF),
            shape_of((rows, D), BF),
            shape_of((rows, 2 * D), BF),
            shape_of((1, 2 * D), F32),
            shape_of((8, D), F32),
        ],
        flops=2 * rows * D * D,
        tokens=tokens,
    )(info, into, residual, cot, vec, out_w, ratio, inverse, gate)


def window_kernel(
    step, count, info, t_ref, g_ref, gfar_ref, tot_ref, s_ref, sfar_ref, v_ref,
    kg_ref, vg_ref, pair_ref,
):
    before, after_own = side_masks()
    left, own, right = neighbours(info, step, count, g_ref, gfar_ref)

    def term(block, part):
        block = block % count
        return t_ref[block * WIN : (block + 1) * WIN, part * WIN : (part + 1) * WIN]

    pulled = t_mm(term(step - 1, 2), left) + t_mm(term(step, 1), own)
    pulled = pulled + t_mm(term(step + 1, 0), right) + pair_total(tot_ref, gfar_ref)
    carried_grad, exp_grad = pulled[:, :D], pulled[:, D:]
    left, data, right = neighbours(info, step, count, s_ref, sfar_ref)
    keys = data[:, D:].astype(F32)
    vg_ref[...] = (carried_grad * keys).astype(BF)
    kg_ref[...] = ((exp_grad + carried_grad * v_ref[...].astype(F32)) * keys).astype(BF)
    pair_ref[:, :WIN] = mm_t(own, data).astype(BF)
    side = jnp.where(before, mm_t(own, left), 0.0) + jnp.where(after_own, mm_t(own, right), 0.0)
    pair_ref[:, WIN:] = side.astype(BF)


def window_back(info, terms, grads, grad_message, grad_totals, stacked, message, vals, tokens=()):
    rows = vals.shape[0]
    return call(
        window_kernel,
        rows // WIN,
        [None, whole, whole, whole, whole, whole, whole, rows_of(WIN)],
        [rows_of(WIN)] * 3,
        [shape_of((rows, D), BF), shape_of((rows, D), BF), shape_of((rows, 2 * WIN), BF)],
        flops=8 * rows * D * 3 * WIN,
        tokens=tokens,
    )(info, terms, grads, grad_message, grad_totals, stacked, message, vals)


def mixing_grads_kernel(
    step, count, info, q_ref, k_ref, v_ref, m_ref, n_ref, b_ref, pair_ref, two_ref, ups_ref,
    keep_near, keep_far, send_ref, pack_ref,
):
    half, me = info[1], info[2]
    width = D // CHAN
    keep_refs = (keep_near, keep_far)
    products = [t_mm(ref[...], n_ref[...]).astype(BF) for ref in (q_ref, k_ref, v_ref)]
    products.append(t_mm(m_ref[...], b_ref[...]).astype(BF))

    def store(core, far, rows, values):
        @pl.when(half == core)
        def _():
            keep_refs[far][rows] = values

        @pl.when(half != core)
        def _():
            send_ref[far, rows] = values

    for k, product in enumerate(products):
        for far in range(2):
            for core in range(2):
                b = 2 * far + core
                rows = slice(k * width, (k + 1) * width)
                store(core, far, rows, product[b * width : (b + 1) * width])

    sums = [col_sum(q_ref[...].astype(F32)), col_sum(v_ref[...].astype(F32))]
    turned = [jnp.concatenate([t[:, D // 2 :], t[:, : D // 2]], axis=1) for t in sums]
    pack_ref[0:2] = jnp.zeros((2, D), F32)
    pack_ref[2:6] = two_ref[0:4]
    for k in range(2):
        pack_ref[6 + k : 7 + k] = jnp.where(me // 2 == 1, turned[k], sums[k])
    for r in range(CHAN):
        pack_ref[pl.ds(8 + (me ^ r), 1)] = ups_ref[r : r + 1]
    pack_ref[12:16] = jnp.zeros((4, D), F32)

    for r in range(CHAN):
        target = keep_refs[r // 2] if r % 2 == 0 else send_ref.at[r // 2]
        block = me ^ r
        rows = slice(D, D + WIN)
        target[rows, : 2 * WIN] = pair_ref[pl.ds(pl.multiple_of(block * WIN, WIN), WIN)]
        lines = [pack_ref[pl.ds(3 * block + i, 1)] for i in range(3)]
        lines = [line[:, t * WIN : (t + 1) * WIN] for line in lines for t in range(3)]
        lines = jnp.concatenate(lines + [jnp.zeros((WIN - 9, WIN), F32)], axis=0)
        target[rows, 2 * WIN :] = lines.astype(BF)


def mixing_grads(info, q_grad, k_grad, v_grad, mixed, normed, branch, pair_grad, two, ups, tokens=()):
    rows = normed.shape[0]
    return call(
        mixing_grads_kernel,
        1,
        [None] + [whole] * 9,
        [whole] * 3,
        [shape_of((D + WIN, D), BF)] * 2 + [shape_of((2, D + WIN, D), BF)],
        scratch=[pltpu.VMEM((16, D), F32)],
        flops=8 * rows * D * D,
        mem=18,
        tokens=tokens,
    )(info, q_grad, k_grad, v_grad, mixed, normed, branch, pair_grad, two, ups)


def input_kernel(step, count, q_ref, k_ref, v_ref, w_ref, x_ref, vec, resg_ref, out_ref, cols_ref):
    upstream = mm(q_ref[...], w_ref[0]) + mm(k_ref[...], w_ref[1]) + mm(v_ref[...], w_ref[2])
    centred, inv_scale = normalize(x_ref[...].astype(F32).T)
    grad = resg_ref[...] + norm_back(upstream, centred, inv_scale, vec[0:1])
    out_ref[...] = grad.T.astype(BF)
    cols = [col_sum(upstream * centred), col_sum(upstream), jnp.zeros((6, D), F32)]
    add_into(cols_ref, step, jnp.concatenate(cols, axis=0))


def input_back(q_grad, k_grad, v_grad, weights, x_t, vec, res_grad, tokens=()):
    rows = res_grad.shape[0]
    wide = rows_of(RB)
    return call(
        input_kernel,
        rows // RB,
        [wide, wide, wide, whole, cols_of(RB), whole, wide],
        [cols_of(RB), whole],
        [shape_of((D, rows), BF), shape_of((8, D), F32)],
        flops=INPUT_COST * rows * D * D,
        tokens=tokens,
    )(q_grad, k_grad, v_grad, weights, x_t, vec, res_grad)


def sync(*arrays):
    return lax.optimization_barrier(arrays)


def row_pieces(values, rows):
    return values.reshape(-1, CHAN, rows).swapaxes(0, 1)


def to_rows(pieces):
    pieces = lax.all_to_all(pieces, "chan", 0, 0, tiled=True)
    return pieces.reshape(-1, pieces.shape[2])


def exchange_near(pieces):
    return flip(jnp.stack([pieces[1], pieces[3]]), "chan", 1)


def exchange_far(pieces, near):
    return flip(jnp.stack([pieces[2], near[1]]), "chan", 2)


def columns(pieces, near, far, me):
    return jnp.concatenate(pick([pieces[0], near[0], far[0], far[1]], me), axis=1).T


def split_rows(values, count):
    size = values.shape[0] // count
    return [values[k * size : (k + 1) * size] for k in range(count)]


def take(values, index, size, axis=0):
    return lax.dynamic_slice_in_dim(values, index * size, size, axis)


def unpack_kernel(step, count, info, packed_ref, pair_ref, out_ref, small_ref, *vectors):
    before, after_own = side_masks()
    grow = [jnp.exp(pair_cols(pair_ref, step, count, k).astype(F32)) for k in (-1, 0, 1)]
    own = packed_ref[step, :, :WIN].astype(F32)
    side = packed_ref[step, :, WIN : 2 * WIN].astype(F32)
    squares = [jnp.zeros((WIN, WIN), F32)] * count
    squares[step] = own * grow[1]
    squares[(step - 1) % count] = jnp.where(before, side * grow[0], 0.0)
    squares[(step + 1) % count] = jnp.where(after_own, side * grow[2], 0.0)
    for k in range(count):
        out_ref[:, k * WIN : (k + 1) * WIN] = squares[k]
    if step == count - 1:
        me, width = info[2], D // CHAN
        lines = []
        for b in range(CHAN):
            part = packed_ref[b, :16, 2 * WIN :].astype(F32)
            for i in range(3):
                lines.append(
                    jnp.concatenate([part[3 * i + t : 3 * i + t + 1] for t in range(3)], axis=1)
                )
        every = jnp.concatenate(lines, axis=0)
        mine = every[:8, :width]
        for k in range(1, CHAN):
            mine = jnp.where(me == k, every[:8, k * width : (k + 1) * width], mine)
        ups = every[8:9]
        for k in range(1, CHAN):
            ups = jnp.where(me == k, every[8 + k : 9 + k], ups)
        small_ref[:, :width] = mine
        small_ref[:, width:] = jnp.zeros((8, D - width), F32)
        vectors[0][...] = ups


def unpack_pairs(info, packed, pair_bias, tokens=()):
    size = pair_bias.shape[0]
    return call(
        unpack_kernel,
        size // WIN,
        [None, whole, whole],
        [rows_of(WIN), whole, whole],
        [shape_of((size, size), F32), shape_of((8, D), F32), shape_of((1, D), F32)],
        heavy=size * WIN * 3,
        tokens=tokens,
    )(info, packed, pair_bias)


def dp_stages():
    size = lax.axis_size("dp")
    stages, mask = [[1]], 2
    while mask < size:
        if mask * 2 < size:
            stages.append([mask, mask * 2, mask * 3])
            mask *= 4
        else:
            stages.append([mask])
            mask *= 2
    return stages


def add(first, second):
    return first.astype(F32) + second.astype(F32)


def dp_groups(masks):
    size = lax.axis_size("dp")
    low, count = masks[0], len(masks) + 1
    starts = [i for i in range(size) if (i // low) % count == 0]
    return [[i + low * k for k in range(count)] for i in starts]


def own_share(masks):
    return (lax.axis_index("dp") // masks[0]) % (len(masks) + 1)


def scatter_start(values, masks):
    count = len(masks) + 1
    n, rows, cols = values.shape[0], values.shape[1] // count, values.shape[2]
    if count == 2:
        return flip(take(values, 1 - own_share(masks), rows, 1), "dp", masks[0])
    parts = values.reshape(n, count, rows, cols).swapaxes(0, 1)
    return lax.all_to_all(parts, "dp", 0, 0, axis_index_groups=dp_groups(masks), tiled=True)


def scatter_end(values, got, masks):
    count = len(masks) + 1
    if count == 2:
        return add(take(values, own_share(masks), values.shape[1] // 2, 1), got).astype(BF)
    total = got[0].astype(F32)
    for k in range(1, count):
        total = total + got[k].astype(F32)
    return total.astype(BF)


def gather_start(values, masks):
    count = len(masks) + 1
    if count == 2:
        return flip(values, "dp", masks[0])
    parts = jnp.broadcast_to(values[None], (count, *values.shape))
    return lax.all_to_all(parts, "dp", 0, 0, axis_index_groups=dp_groups(masks), tiled=True)


def gather_end(values, got, masks):
    if len(masks) == 1:
        own = own_share(masks)
        pieces = [jnp.where(own == 1, got, values), jnp.where(own == 1, values, got)]
        return jnp.concatenate(pieces, axis=1)
    return got.swapaxes(0, 1).reshape(values.shape[0], -1, values.shape[2])


def scatter_rest(values, stages):
    for masks in stages:
        values = scatter_end(values, scatter_start(values, masks), masks)
    return values


def gather_rest(values, stages):
    for masks in reversed(stages):
        values = gather_end(values, gather_start(values, masks), masks)
    return values


def body(
    tokens,
    norm1_gain,
    norm1_bias,
    qkv_weight,
    qv_bias,
    pair_bias,
    out_weight,
    out_bias,
    norm2_gain,
    norm2_bias,
    up_weight,
    up_bias,
    down_weight,
    down_bias,
    lengths,
    cotangent,
):
    me = lax.axis_index("chan")
    place = lax.axis_index("dp") % 4
    half = me % 2
    rows = tokens.shape[0] // CHAN
    width = D // CHAN
    length = lax.dynamic_index_in_dim(lengths, me // 2, 0, keepdims=False)
    info = jnp.stack([jnp.clip(length - half * rows, 0, rows), half, me]).astype(jnp.int32)
    along, across, *others = dp_stages()

    mixing = jnp.concatenate([jnp.swapaxes(qkv_weight, 1, 2).reshape(-1, D), out_weight], axis=0)
    mix_q0 = flip(take(mixing, place, D // 4), "chan", 2)
    mix_near = flip(mixing, "chan", 1)
    feeding = jnp.concatenate([up_weight, down_weight], axis=0)
    feed_near = flip(feeding, "chan", 1)
    token_pieces = row_pieces(tokens.T, rows)
    mix_q0, token_pieces = sync(mix_q0, token_pieces)
    x_t = to_rows(token_pieces)
    mix_q1 = flip(mix_q0, "dp", 1)
    mix_q2 = flip(mix_q0, "dp", 2)
    small = jnp.stack(
        [norm1_gain, norm1_bias, qv_bias[0], qv_bias[1], out_bias, norm2_gain, norm2_bias, down_bias]
    )
    small = jnp.concatenate([small, up_bias.reshape(CHAN, width)], axis=0)
    small = jnp.pad(small, ((0, 4), (0, 0)))
    small = jnp.stack([small] + [flip(small, "chan", r) for r in range(1, CHAN)])
    mix_q1, mix_q2, feeding = sync(mix_q1, mix_q2, feeding)
    mix_q3 = flip(mix_q2, "dp", 1)
    vec, up_shift, tok = vectors(info, small)
    mix_q3, x_t, feeding, tok = sync(mix_q3, x_t, feeding, tok)
    mix_far = jnp.concatenate(pick([mix_q0, mix_q1, mix_q2, mix_q3], place), axis=0)
    mixing = [mixing, mix_near, mix_far, flip(mix_far, "chan", 1)]
    feed_q0 = flip(take(feeding, place, D // 2), "chan", 2)

    def message(values, totals):
        edge = lax.dynamic_slice_in_dim(values, (1 - half) * (rows - WIN), WIN, 0)
        high = totals.astype(BF)
        low = (totals - high.astype(F32)).astype(BF)
        rest = jnp.zeros((14, values.shape[1]), BF)
        return flip(jnp.concatenate([edge, high, low, rest], axis=0), "chan", 1)

    normed_one, gate, vals, stacked, totals, qkv_t, tok = project(
        info, x_t, vec, mixing, tokens=[tok]
    )
    cot_pieces = row_pieces(cotangent.T, rows)
    feed_q0, totals, cot_pieces, tok = sync(feed_q0, totals, cot_pieces, tok)
    halo = message(stacked, totals)
    feed_q1 = flip(feed_q0, "dp", 1)
    feed_q2 = flip(feed_q0, "dp", 2)
    cot_t = to_rows(cot_pieces)
    terms, ratio, inverse, mixed, residual, normed_two, out_w, tok = mix(
        info, pair_bias, stacked, halo, totals, gate, x_t, vec, mixing, tokens=[tok]
    )
    feed_q1, feed_q2, cot_t, tok = sync(feed_q1, feed_q2, cot_t, tok)
    feed_q3 = flip(feed_q2, "dp", 1)

    total, into, ups_1, grad_1, cot, tok = feed(
        info, normed_two, cot_t, up_shift[1:2], feed_near, tokens=[tok]
    )
    got_1 = flip(grad_1, "chan", 1)
    feed_q3, tok = sync(feed_q3, tok)
    feed_far = jnp.concatenate(pick([feed_q0, feed_q1, feed_q2, feed_q3], place), axis=0)
    feed_both = flip(feed_far, "chan", 1)
    total, into, ups_3, grad_3, tok = feed(
        info, normed_two, cot, up_shift[3:4], feed_both, (total, into), tokens=[tok]
    )
    got_3 = flip(grad_3, "chan", 1)
    total, into, ups_0, near, tok = feed(
        info, normed_two, cot, up_shift[0:1], feeding, (total, into), extra=got_1, tokens=[tok]
    )
    near = near.reshape(2, D, D)
    near_x = scatter_start(near, along)
    layer_t, into, ups_2, far, tok = feed(
        info,
        normed_two,
        cot,
        up_shift[2:3],
        feed_far,
        (total, into),
        (residual, vec),
        got_3,
        tokens=[tok],
    )
    far = far.reshape(2, D, D)
    res_grad, branch, q_grad, grads, grad_totals, cols_two, tok = branch_back(
        info, into, residual, cot, vec, out_w, ratio, inverse, gate, tokens=[tok]
    )
    near_x, tok = sync(near_x, tok)
    near = scatter_end(near, near_x, along)
    near_z = scatter_start(near, across)
    far_x = scatter_start(far, along)
    grad_halo = message(grads, grad_totals)
    k_grad, v_grad, pair_grad, tok = window_back(
        info, terms, grads, grad_halo, grad_totals, stacked, halo, vals, tokens=[tok]
    )
    ups = jnp.concatenate([ups_0, ups_1, ups_2, ups_3], axis=0)
    m_near, m_far, send, tok = mixing_grads(
        info, q_grad, k_grad, v_grad, mixed, normed_one, branch, pair_grad, cols_two, ups, tokens=[tok]
    )
    got = flip(send, "chan", 1)
    input_t, cols_one, tok = input_back(
        q_grad, k_grad, v_grad, qkv_t, x_t, vec, res_grad, tokens=[tok]
    )

    cols_one = cols_one[:2] + flip(cols_one[:2], "chan", 1)
    got, tok = sync(got, tok)

    def with_norm(values, there):
        lines = jnp.where(there, cols_one, 0.0).reshape(6, WIN)
        return values + jnp.pad(lines, ((D, WIN - 6), (2 * WIN, 0)))

    m_far = flip(with_norm(add(m_far, got[1]), me == 2).astype(BF), "chan", 2)
    m_near = with_norm(add(m_near, got[0]), me == 0)
    near_z, far_x, tok = sync(near_z, far_x, tok)
    near = scatter_end(near, near_z, across)
    far = scatter_end(far, far_x, along)
    far_z = scatter_start(far, across)
    layer_parts = pick(split_rows(layer_t, CHAN), me)
    input_parts = pick(split_rows(input_t, CHAN), me)
    layer_near = exchange_near(layer_parts)
    input_near = exchange_near(input_parts)
    far_z, m_near, tok = sync(far_z, m_near, tok)
    f_near = scatter_rest(near, others)
    f_far = scatter_rest(scatter_end(far, far_z, across), others)
    f_y = flip(f_far, "chan", 2)
    m_far, f_y, tok = sync(m_far, f_y, tok)
    f = gather_rest(add(f_near, f_y).astype(BF), others)
    f_z = [flip(f, "dp", k) for k in across]
    m = add(m_near, m_far).astype(BF)[None]
    m_x = scatter_start(m, along)
    m_x, f, layer_near, tok = sync(m_x, f, layer_near, tok)
    m = scatter_end(m, m_x, along)
    layer_far = exchange_far(layer_parts, layer_near)
    *f_z, m, tok = sync(*f_z, m, tok)
    m_z = scatter_start(m, across)
    f = jnp.concatenate(pick([f, *f_z], own_share(across)), axis=1)
    f_x = gather_start(f, along)
    m_z, f_x, layer_far, input_near, f = sync(m_z, f_x, layer_far, input_near, f)
    m = scatter_rest(scatter_end(m, m_z, across), others)
    m = gather_rest(m, others)
    m_z = gather_start(m, across)
    f = gather_end(f, f_x, along).astype(F32)
    layer_out = columns(layer_parts, layer_near, layer_far, me)
    input_far = exchange_far(input_parts, input_near)
    m_z, f, layer_out, input_far = sync(m_z, f, layer_out, input_far)
    m = gather_end(m, m_z, across)
    m_x = gather_start(m, along)
    input_grad = columns(input_parts, input_near, input_far, me)
    m_x, input_grad, f = sync(m_x, input_grad, f)
    m = gather_end(m, m_x, along)[0]
    block = m[D:]
    other = flip(block, "chan", 2)
    qkv_out = jnp.swapaxes(m[: 3 * width].reshape(3, width, D).astype(F32), 1, 2)
    out_out = m[3 * width : D].astype(F32)
    other, qkv_out, out_out, tok = sync(other, qkv_out, out_out, tok)
    pair = jnp.stack([block, other])
    beside = flip(pair, "chan", 1)
    table = jnp.stack(pick([pair[0], beside[0], pair[1], beside[1]], me))
    pair_out, small_out, ups_out, tok = unpack_pairs(info, table, pair_bias, tokens=[tok])
    vector = [small_out[k, :width] for k in range(8)]
    return (
        layer_out,
        input_grad,
        vector[0],
        vector[1],
        qkv_out,
        jnp.stack(vector[6:8]),
        pair_out,
        out_out,
        vector[4],
        vector[2],
        vector[3],
        f[0],
        ups_out.reshape(-1),
        f[1],
        vector[5],
    )


def solution(mesh):
    in_specs = (
        P("dp", "chan"),
        P("chan"),
        P("chan"),
        P(None, None, "chan"),
        P(None, "chan"),
        P(),
        P("chan", None),
        P("chan"),
        P("chan"),
        P("chan"),
        P(None, "chan"),
        P("chan"),
        P("chan", None),
        P("chan"),
        P("dp"),
        P("dp", "chan"),
    )
    out_specs = (
        P("dp", "chan"),
        P("dp", "chan"),
        P("chan"),
        P("chan"),
        P(None, None, "chan"),
        P(None, "chan"),
        P(),
        P("chan", None),
        P("chan"),
        P("chan"),
        P("chan"),
        P(None, "chan"),
        P("chan"),
        P("chan", None),
        P("chan"),
    )
    return jax.shard_map(body, mesh=mesh, in_specs=in_specs, out_specs=out_specs, check_vma=False)
```

time: 1440 us -> 415 us (0.29)
  waiting for transfers between devices: 795 us -> 124 us
  matrix products: 190 us -> 0 us
  local copies, waits for them, and re-layouts: 202 us -> 76 us
  Pallas kernels: 0 us -> 84.8 us
  blocking collectives: 78.4 us -> 0 us
  starting transfers between devices: 0.79 us -> 71.8 us
  other arithmetic: 102 us -> 48.8 us
  loops' own time: 43.1 us -> 0 us
    psum x2 -> x0, waiting for transfers between devices: 332 us -> none  [the longest x1 243 us: body(): lax.psum((norm1_gain_grad, norm1_bias_grad, qkv_weight_grad, qv_bias_grad...]
    reduce_scatter x4 -> x0, waiting for transfers between devices: 286 us -> none  [the longest x2 142 us: fold_rows(): return lax.psum_scatter(values, 'chan', scatter_dimension=1, tiled=True)]
    dot_general x35 -> x0, matrix products: 183 us -> none  [the longest x8 25.7 us: compute(): jnp.einsum('rb,rk->bk', weights_t, grad_ext, preferred_element_type=jnp.f...]
    all_gather x4 -> x0, waiting for transfers between devices: 177 us -> none  [the longest x2 92.8 us: spread_rows(): return lax.all_gather(values, 'chan', axis=1, tiled=True)]
    ppermute x0 -> x37, waiting for transfers between devices: none -> 93.1 us  [flip(): return lax.ppermute(values, axis, [(i, i ^ mask) for i in range(size)])]
    pallas_call x0 -> x12, Pallas kernels: none -> 84.8 us  [call(): return lambda *operands: run(*operands, *tokens)]
    psum x5 -> x0, blocking collectives: 78.4 us -> none  [the longest x1 30.4 us: body(): lax.psum((norm1_gain_grad, norm1_bias_grad, qkv_weight_grad, qv_bias_grad...]
    dynamic_slice x40 -> x7, local copies, waits for them, and re-layouts: 50.8 us -> 7.53 us  [the longest x4 5.56 us: take(): return lax.dynamic_slice_in_dim(values, index * size, size, axis)]
  transfers between devices with their start and end apart: 10 -> 43, of which waited for: 10 -> 19; matrix products, arithmetic and copies ran while one was open for 6% -> 14% of each run, Pallas kernels for 0% -> 20%
where the time goes in v2:
time: 415 us; the launch traced here: 407 us
  waiting for transfers between devices  124 us (30%)
  Pallas kernels  84.8 us (20%)
  local copies, waits for them, and re-layouts  76 us (18%)
  starting transfers between devices  71.8 us (17%)
  other arithmetic  48.8 us (12%)
    ppermute x37, waiting for transfers between devices, flip(): return lax.ppermute(values, axis, [(i, i ^ mask) for i in range(size)])  93.1 us
    pallas_call x12, Pallas kernels, call(): return lambda *operands: run(*operands, *tokens)  84.8 us
    unnamed x177, local copies, waits for them, and re-layouts  54.8 us
    ppermute x37, starting transfers between devices, flip(): return lax.ppermute(values, axis, [(i, i ^ mask) for i in range(size)])  39.5 us
    all_to_all x3, waiting for transfers between devices, scatter_start(): lax.all_to_all(parts, 'dp', 0, 0, axis_index_groups=dp_groups(masks), til...  20.1 us
    all_to_all x3, starting transfers between devices, scatter_start(): lax.all_to_all(parts, 'dp', 0, 0, axis_index_groups=dp_groups(masks), til...  18 us
    all_to_all x1, waiting for transfers between devices, gather_start(): lax.all_to_all(parts, 'dp', 0, 0, axis_index_groups=dp_groups(masks), til...  10.3 us
    all_to_all x2, starting transfers between devices, to_rows(): pieces = lax.all_to_all(pieces, 'chan', 0, 0, tiled=True)  9.26 us
  transfers between devices with their start and end apart: 43, of which 19 were waited for; matrix products, arithmetic and copies ran while one was open for 14% of the time, Pallas kernels for 20%

profile of v2, /device:TPU:1, one launch (start us, length us, event | category | flops | bytes accessed | tf_op | source)
XLA Modules:
  0.0 407.5 jit_solution(10640470213544430777)
XLA Ops:
  1.8 2.1 collective-permute-start
  4.0 2.7 copy.50
  6.7 4.1 collective-permute-done
  10.8 4.8 %all-to-all-start = ((bf16[4,192,1024]{2,1,0:T(8,128)(2,1)}), bf16[4,192,1024]{2,1,0:T(8,128)(2,1)S(1)}, u32[]{:S(2)}, u32[]{:S(2)}) async-start(bf16[4,192,1024]{2,1,0:T(8,128)(2,1)} %bitcast.183), calls=%async_computation | async-start | bytes 3145728 | tf_op jit(solution)/shard_map/all_to_all | solution.py:540
  19.2 1.7 collective-permute-start.5
  21.2 3.6 collective-permute-done.1
  28.9 6.1 %collective-permute-done.5 = bf16[16,192]{1,0:T(8,128)(2,1)S(1)} collective-permute-done((bf16[16,192]{1,0:T(8,128)(2,1)S(1)}, bf16[16,192]{1,0:T(8,128)(2,1)S(1)}, u32[]{:S(2)}, u32[]{:S(2)}) %collective-permute-start.5) | collective-permute-done | bytes 6176 | tf_op jit(solution)/shard_map/ppermute | solution.py:26
  36.2 1.9 broadcast_select_fusion.45
  39.6 1.9 constant_dynamic-slice_fusion.3
  42.2 2.7 copy.49
  45.0 6.9 %shard_map.272 = (bf16[1024,768]{1,0:T(8,128)(2,1)S(1)}, bf16[1024,768]{1,0:T(8,128)(2,1)S(1)}, bf16[1024,768]{1,0:T(8,128)(2,1)S(1)}, bf16[1024,1536]{1,0:T(8,1...) custom-call(s32[3]{0:T(128)S(1)} %pad_add_fusion.refs_0_, ...), custom_call_target="tpu_custom_call" | custom-call | flops 3623878656 | bytes 12079595 | tf_op jit(solution)/shard_map/pallas_call | solution.py:81
  53.0 1.7 copy-done.7
  54.7 1.8 copy-done.50
  58.8 4.5 %all-to-all-start.1 = ((bf16[4,192,1024]{2,1,0:T(8,128)(2,1)}), bf16[4,192,1024]{2,1,0:T(8,128)(2,1)}, u32[]{:S(2)}, u32[]{:S(2)}) async-start(bf16[4,192,1024]{2,1,0:T(8,128)(2,1)} %bitcast.184), calls=%async_computation.1 | async-start | bytes 3145728 | tf_op jit(solution)/shard_map/all_to_all | solution.py:540
  67.8 1.7 copy-done.2
  70.9 1.9 copy-done.8
  72.8 7.0 %shard_map.273 = (bf16[1024,768]{1,0:T(8,128)(2,1)S(1)}, bf16[1024,768]{1,0:T(8,128)(2,1)S(1)}, f32[1024,768]{1,0:T(8,128)S(1)}, bf16[1024,768]{1,0:T(8,128)(2,1...) custom-call(s32[3]{0:T(128)S(1)} %pad_add_fusion.refs_0_, ...), custom_call_target="tpu_custom_call" | custom-call | flops 3623878656 | bytes 12079595 | tf_op jit(solution)/shard_map/pallas_call | solution.py:81
  79.8 1.7 copy-done.10
  92.0 11.0 %shard_map.274 = (f32[1024,768]{1,0:T(8,128)S(1)}, f32[1024,768]{1,0:T(8,128)S(1)}, f32[1,768]{1,0:T(1,128)S(1)}, bf16[1536,768]{1,0:T(8,128)(2,1)}, bf16[1024,7...) custom-call(s32[3]{0:T(128)S(1)} %pad_add_fusion.refs_0_, bf16[1024,768]{1,0:T(8,128)(2,1)S(1)} %copy-done.42, ...), custom_call_target="tpu_custom_call" | custom-call | flops 7247757312 | bytes 24159192 | tf_op jit(solution)/shard_map/pallas_call | solution.py:81
  105.4 2.0 collective-permute-start.15
  108.8 2.8 collective-permute-done.15.refs_4_
  111.5 9.8 %shard_map.275 = (f32[1024,768]{1,0:T(8,128)S(1)}, f32[1024,768]{1,0:T(8,128)S(1)}, f32[1,768]{1,0:T(1,128)S(1)}, bf16[1536,768]{1,0:T(8,128)(2,1)}, f32[8,128]{1,0:T(8,128)S(1)}) custom-call(s32[3]{0:T(128)S(1)} %pad_add_fusion.refs_0_, bf16[1024,768]{1,0:T(8,128)(2,1)S(1)} %copy-done.43, bf16[1024,768]{1,0:T(8,128)(2,1)S(1)} %get-tuple-element.156.refs_2_.refs_3_, ...), custom_call_target="tpu_custom_call" | custom-call | flops 7247757312 | bytes 24159192 | tf_op jit(solution)/shard_map/pallas_call | solution.py:81
  121.3 1.7 copy-done.56
  126.4 1.7 copy-done.28
  129.5 1.9 copy-done.57
  131.4 1.9 copy-done.59
  133.3 10.8 %shard_map.276 = (f32[1024,768]{1,0:T(8,128)S(1)}, f32[1024,768]{1,0:T(8,128)S(1)}, f32[1,768]{1,0:T(1,128)S(1)}, bf16[1536,768]{1,0:T(8,128)(2,1)S(1)}, f32[8,128]{1,0:T(8,128)S(1)}) custom-call(s32[3]{0:T(128)S(1)} %pad_add_fusion.refs_0_, bf16[1024,768]{1,0:T(8,128)(2,1)S(1)} %copy-done.44, bf16[1024,768]{1,0:T(8,128)(2,1)S(1)} %copy-done.21, ...), custom_call_target="tpu_custom_call" | custom-call | flops 7247757312 | bytes 24159192 | tf_op jit(solution)/shard_map/pallas_call | solution.py:81
  147.1 10.7 %shard_map.277 = (bf16[768,1024]{1,0:T(8,128)(2,1)S(1)}, f32[1024,768]{1,0:T(8,128)S(1)}, f32[1,768]{1,0:T(1,128)S(1)}, bf16[1536,768]{1,0:T(8,128)(2,1)S(1)}, f32[8,128]{1,0:T(8,128)S(1)}) custom-call(s32[3]{0:T(128)S(1)} %pad_add_fusion.refs_0_, bf16[1024,768]{1,0:T(8,128)(2,1)S(1)} %copy-done.45, bf16[1024,768]{1,0:T(8,128)(2,1)S(1)} %copy-done.22, ...), custom_call_target="tpu_custom_call" | custom-call | flops 7247757312 | bytes 24159192 | tf_op jit(solution)/shard_map/pallas_call | solution.py:81
  159.2 5.5 %shard_map.278 = (f32[1024,768]{1,0:T(8,128)S(1)}, bf16[1024,768]{1,0:T(8,128)(2,1)S(1)}, bf16[1024,768]{1,0:T(8,128)(2,1)S(1)}, bf16[1024,1536]{1,0:T(8,128)(2,...) custom-call(s32[3]{0:T(128)S(1)} %pad_add_fusion.refs_0_, ...), custom_call_target="tpu_custom_call" | custom-call | flops 1207959552 | bytes 4026531 | tf_op jit(solution)/shard_map/pallas_call | solution.py:81
  164.7 1.7 copy-done.35
  173.1 1.9 add_convert_fusion.2
  176.1 4.4 %all-to-all-start.2 = ((bf16[4,2,96,768]{3,2,1,0:T(8,128)(2,1)}), bf16[4,2,96,768]{3,2,1,0:T(8,128)(2,1)}, u32[]{:S(2)}, u32[]{:S(2)}) async-start(bf16[4,2,96,768]{3,2,1,0:T(8,128)(2,1)} %copy.42), calls=%async_computation.2 | async-start | bytes 2359296 | tf_op jit(solution)/shard_map/all_to_all | solution.py:644
  183.2 1.9 copy-done.9
  185.0 1.9 copy-done.34
  189.8 5.9 %shard_map.279 = (bf16[1024,768]{1,0:T(8,128)(2,1)S(1)}, bf16[1024,768]{1,0:T(8,128)(2,1)S(1)}, bf16[1024,512]{1,0:T(8,128)(2,1)S(1)}, f32[8,128]{1,0:T(8,128)S(1)}) custom-call(s32[3]{0:T(128)S(1)} %pad_add_fusion.refs_0_, bf16[1024,768]{1,0:T(8,128)(2,1)S(1)} %copy-done.40, bf16[1024,1536]{1,0:T(8,128)(2,1)S(1)} %copy-done.34, ...), custom_call_target="tpu_custom_call" | custom-call | flops 4831838208 | bytes 16106127 | tf_op jit(solution)/shard_map/pallas_call | solution.py:81
  195.8 7.0 %shard_map.280 = (bf16[1024,768]{1,0:T(8,128)(2,1)S(1)}, bf16[1024,768]{1,0:T(8,128)(2,1)S(1)}, bf16[2,1024,768]{2,1,0:T(8,128)(2,1)S(1)}, f32[8,128]{1,0:T(8,128)S(1)}) custom-call(s32[3]{0:T(128)S(1)} %pad_add_fusion.refs_0_, bf16[1024,768]{1,0:T(8,128)(2,1)S(1)} %copy-done.47, bf16[1024,768]{1,0:T(8,128)(2,1)S(1)} %get-tuple-element.188.refs_2_.refs_1_, ...), custom_call_target="tpu_custom_call" | custom-call | flops 4831838208 | bytes 16106127 | tf_op jit(solution)/shard_map/pallas_call | solution.py:81
  205.5 6.0 %shard_map.281 = (bf16[768,1024]{1,0:T(8,128)(2,1)S(1)}, f32[8,768]{1,0:T(8,128)S(1)}, f32[8,128]{1,0:T(8,128)S(1)}) custom-call(bf16[1024,768]{1,0:T(8,128)(2,1)S(1)} %copy-done.47, bf16[1024,768]{1,0:T(8,128)(2,1)S(1)} %get-tuple-element.188.refs_2_.refs_1_, bf16[1024,768]{1,0:T(8,128)(2,1)S(1)} %get-tuple-element.189.refs_3_.refs_2_, ...), custom_call_target="tpu_custom_call" | custom-call | flops 43486543872 | bytes 144955152 | tf_op jit(solution)/shard_map/pallas_call | solution.py:81
  214.4 1.9 add_convert_fusion.1
  217.4 4.8 %all-to-all-start.3 = ((bf16[4,2,96,768]{3,2,1,0:T(8,128)(2,1)}), bf16[4,2,96,768]{3,2,1,0:T(8,128)(2,1)S(1)}, u32[]{:S(2)}, u32[]{:S(2)}) async-start(bf16[4,2,96,768]{3,2,1,0:T(8,128)(2,1)} %copy.43), calls=%async_computation.3 | async-start | bytes 2359296 | tf_op jit(solution)/shard_map/all_to_all | solution.py:644
  223.4 5.7 %fusion = (f32[1024,768]{1,0:T(8,128)}, bf16[1024,768]{1,0:T(8,128)(2,1)}) fusion(f32[6,256]{1,0:T(8,128)S(1)} %reshape.140, bf16[1024,768]{1,0:T(8,128)(2,1)} %copy-done.25, bf16[2,1024,768]{2,1,0:T(8,128)(2,1)} %copy-done.63, f32[6,256]{1,0:T(8,128)S(1)} %reshape.138, bf16[1024,768]{1,0:T(8,128)(2,1)} %copy-done.26), kind=kLoop, calls=%fused_computation.1 | loop fusion | flops 7077888 | bytes 11022336 | tf_op jit(solution)/shard_map/add | solution.py:811
  230.4 20.1 %all-to-all-done.3 = bf16[4,2,96,768]{3,2,1,0:T(8,128)(2,1)S(1)} async-done(((bf16[4,2,96,768]{3,2,1,0:T(8,128)(2,1)}), bf16[4,2,96,768]{3,2,1,0:T(8,128)(2,1)S(1)}, u32[]{:S(2)}, u32[]{:S(2)}) %all-to-all-start.3) | async-done | bytes 1179680 | tf_op jit(solution)/shard_map/all_to_all | solution.py:644
  252.2 2.6 select_bitcast_fusion.7
  257.1 8.0 %collective-permute-done.23 = bf16[1024,768]{1,0:T(8,128)(2,1)} collective-permute-done((bf16[1024,768]{1,0:T(8,128)(2,1)}, bf16[1024,768]{1,0:T(8,128)(2,1)}, u32[]{:S(2)}, u32[]{:S(2)}) %collective-permute-start.23) | collective-permute-done | bytes 1572896 | tf_op jit(solution)/shard_map/ppermute | solution.py:26
  265.1 6.2 %collective-permute-done.24 = bf16[2,96,768]{2,1,0:T(8,128)(2,1)S(1)} collective-permute-done((bf16[2,96,768]{2,1,0:T(8,128)(2,1)S(1)}, bf16[2,96,768]{2,1,0:T(8,128)(2,1)S(1)}, u32[]{:S(2)}, u32[]{:S(2)}) %collective-permute-start.24) | collective-permute-done | bytes 294944 | tf_op jit(solution)/shard_map/ppermute | solution.py:26
  271.3 1.9 add_convert_fusion
  276.0 1.7 collective-permute-start.25
  277.7 2.1 collective-permute-start.26
  279.9 12.6 %collective-permute-done.28 = bf16[1,512,768]{2,1,0:T(8,128)(2,1)} collective-permute-done((bf16[1,512,768]{2,1,0:T(8,128)(2,1)}, bf16[1,512,768]{2,1,0:T(8,128)(2,1)}, u32[]{:S(2)}, u32[]{:S(2)}) %collective-permute-start.28) | collective-permute-done | bytes 786464 | tf_op jit(solution)/shard_map/ppermute | solution.py:26
  292.4 2.4 fusion.3
  294.9 3.3 collective-permute-done.27
  300.7 8.8 %all-to-all-start.4 = ((bf16[4,1,128,768]{3,2,1,0:T(8,128)(2,1)}), bf16[4,1,128,768]{3,2,1,0:T(8,128)(2,1)}, u32[]{:S(2)}, u32[]{:S(2)}) async-start(bf16[4,1,128,768]{3,2,1,0:T(8,128)(2,1)} %bitcast.190), calls=%async_computation.4 | async-start | bytes 1572864 | tf_op jit(solution)/shard_map/all_to_all | solution.py:644
  309.5 2.5 select_bitcast_fusion.4
  312.9 3.2 collective-permute-start.32
  318.4 17.6 %collective-permute-done.31 = bf16[2,192,1024]{2,1,0:T(8,128)(2,1)} collective-permute-done((bf16[2,192,1024]{2,1,0:T(8,128)(2,1)}, bf16[2,192,1024]{2,1,0:T(8,128)(2,1)}, u32[]{:S(2)}, u32[]{:S(2)}) %collective-permute-start.31) | collective-permute-done | bytes 786464 | tf_op jit(solution)/shard_map/ppermute | solution.py:26
  337.1 1.9 pad_maximum_fusion.9
  342.6 5.1 %all-to-all-start.5 = ((bf16[4,1,128,768]{3,2,1,0:T(8,128)(2,1)}), bf16[4,1,128,768]{3,2,1,0:T(8,128)(2,1)}, u32[]{:S(2)}, u32[]{:S(2)}) async-start(bf16[4,1,128,768]{3,2,1,0:T(8,128)(2,1)} %broadcast_in_dim.16), calls=%async_computation.5 | async-start | bytes 1572864 | tf_op jit(solution)/shard_map/all_to_all | solution.py:662
  349.2 2.5 maximum_convert_fusion
  354.3 2.8 collective-permute-done.33
  357.1 10.3 %all-to-all-done.5 = bf16[4,1,128,768]{3,2,1,0:T(8,128)(2,1)} async-done(((bf16[4,1,128,768]{3,2,1,0:T(8,128)(2,1)}), bf16[4,1,128,768]{3,2,1,0:T(8,128)(2,1)}, u32[]{:S(2)}, u32[]{:S(2)}) %all-to-all-start.5) | async-done | bytes 786464 | tf_op jit(solution)/shard_map/all_to_all | solution.py:662
  370.4 14.8 %collective-permute-done.34 = bf16[1,512,768]{2,1,0:T(8,128)(2,1)S(1)} collective-permute-done((bf16[1,512,768]{2,1,0:T(8,128)(2,1)}, bf16[1,512,768]{2,1,0:T(8,128)(2,1)S(1)}, u32[]{:S(2)}, u32[]{:S(2)}) %collective-permute-start.34) | collective-permute-done | bytes 786464 | tf_op jit(solution)/shard_map/ppermute | solution.py:26
  388.9 6.7 %collective-permute-done.35 = bf16[256,768]{1,0:T(8,128)(2,1)S(1)} collective-permute-done((bf16[256,768]{1,0:T(8,128)(2,1)S(1)}, bf16[256,768]{1,0:T(8,128)(2,1)S(1)}, u32[]{:S(2)}, u32[]{:S(2)}) %collective-permute-start.35) | collective-permute-done | bytes 393248 | tf_op jit(solution)/shard_map/ppermute | solution.py:26
  395.7 3.4 collective-permute-start.36
  399.1 2.5 slice_bitcast_fusion
  401.9 3.5 shard_map.282
  (291 shorter events, 97.0 us)
Async XLA Ops:
  1.8 9.0 %collective-permute-start = (bf16[192,768]{1,0:T(8,128)(2,1)S(1)}, bf16[192,768]{1,0:T(8,128)(2,1)}, u32[]{:S(2)}, u32[]{:S(2)}) collective-permute-start(bf16[192,768]{1,0:T(8,128)(2,1)S(1)} %fusion.7), channel_id=1, source_target_pairs={{0,2},{1,3},{2,0},{3,1},{4,6},{5,7},{6,4},{7,5},{8,10},{9,11},{10,... | collective-permute-start | bytes 884744 | tf_op jit(solution)/shard_map/ppermute | solution.py:26
  6.7 9.0 %copy-start.84 = (bf16[192]{0:T(256)(128)(2,1)S(1)}, bf16[192]{0:T(256)(128)(2,1)}, u32[]{:S(2)}) copy-start(bf16[192]{0:T(256)(128)(2,1)} %param.29) | copy-start | bytes 1156
  6.7 9.0 %copy-start.78 = (bf16[2,192]{1,0:T(2,128)(2,1)S(1)}, bf16[2,192]{1,0:T(2,128)(2,1)}, u32[]{:S(2)}) copy-start(bf16[2,192]{1,0:T(2,128)(2,1)} %param.20) | copy-start | bytes 2308
  6.7 14.3 %copy-start.72 = (bf16[768,768]{1,0:T(8,128)(2,1)S(1)}, bf16[768,768]{1,0:T(8,128)(2,1)}, u32[]{:S(2)}) copy-start(bf16[768,768]{1,0:T(8,128)(2,1)} %param.26) | copy-start | bytes 3538948
  10.8 25.4 %all-to-all-start = ((bf16[4,192,1024]{2,1,0:T(8,128)(2,1)}), bf16[4,192,1024]{2,1,0:T(8,128)(2,1)S(1)}, u32[]{:S(2)}, u32[]{:S(2)}) async-start(bf16[4,192,1024]{2,1,0:T(8,128)(2,1)} %bitcast.183), calls=%async_computation | async-start | bytes 3145728 | tf_op jit(solution)/shard_map/all_to_all | solution.py:540
  15.8 9.0 %collective-permute-start.1 = (bf16[192,768]{1,0:T(8,128)(2,1)}, bf16[192,768]{1,0:T(8,128)(2,1)S(1)}, u32[]{:S(2)}, u32[]{:S(2)}) collective-permute-start(bf16[192,768]{1,0:T(8,128)(2,1)} %collective-permute-done), channel_id=1, source_target_pairs={{0,4},{4,0},{8,12},{12,8},{16,20},{20,16},{24,28},{28,24},{1,5},{5... | collective-permute-start | bytes 884744 | tf_op jit(solution)/shard_map/ppermute | solution.py:26
  17.3 8.6 %collective-permute-start.2 = (bf16[192,768]{1,0:T(8,128)(2,1)}, bf16[192,768]{1,0:T(8,128)(2,1)}, u32[]{:S(2)}, u32[]{:S(2)}) collective-permute-start(bf16[192,768]{1,0:T(8,128)(2,1)} %collective-permute-done), channel_id=1, source_target_pairs={{0,8},{4,12},{8,0},{12,4},{16,24},{20,28},{24,16},{28,20},{1,9},{5... | collective-permute-start | bytes 884744 | tf_op jit(solution)/shard_map/ppermute | solution.py:26
  18.6 10.3 %collective-permute-start.4 = (bf16[16,192]{1,0:T(8,128)(2,1)S(1)}, bf16[16,192]{1,0:T(8,128)(2,1)S(1)}, u32[]{:S(2)}, u32[]{:S(2)}) collective-permute-start(bf16[16,192]{1,0:T(8,128)(2,1)S(1)} %get-tuple-element.306), channel_id=1, source_target_pairs={{0,1},{1,0},{2,3},{3,2},{4,5},{5,4},{6,7},{7,6},{8,9},{9,8},{10,11... | collective-permute-start | bytes 18440 | tf_op jit(solution)/shard_map/ppermute | solution.py:26
  19.2 15.8 %collective-permute-start.5 = (bf16[16,192]{1,0:T(8,128)(2,1)S(1)}, bf16[16,192]{1,0:T(8,128)(2,1)S(1)}, u32[]{:S(2)}, u32[]{:S(2)}) collective-permute-start(bf16[16,192]{1,0:T(8,128)(2,1)S(1)} %get-tuple-element.306), channel_id=1, source_target_pairs={{0,2},{1,3},{2,0},{3,1},{4,6},{5,7},{6,4},{7,5},{8,10},{9,11},{10,... | collective-permute-start | bytes 18440 | tf_op jit(solution)/shard_map/ppermute | solution.py:26
  20.9 14.6 %collective-permute-start.6 = (bf16[16,192]{1,0:T(8,128)(2,1)S(1)}, bf16[16,192]{1,0:T(8,128)(2,1)S(1)}, u32[]{:S(2)}, u32[]{:S(2)}) collective-permute-start(bf16[16,192]{1,0:T(8,128)(2,1)S(1)} %get-tuple-element.306), channel_id=1, source_target_pairs={{0,3},{1,2},{2,1},{3,0},{4,7},{5,6},{6,5},{7,4},{8,11},{9,10},{10,... | collective-permute-start | bytes 18440 | tf_op jit(solution)/shard_map/ppermute | solution.py:26
  25.9 10.3 %collective-permute-start.3 = (bf16[192,768]{1,0:T(8,128)(2,1)}, bf16[192,768]{1,0:T(8,128)(2,1)}, u32[]{:S(2)}, u32[]{:S(2)}) collective-permute-start(bf16[192,768]{1,0:T(8,128)(2,1)} %collective-permute-done.2), channel_id=1, source_target_pairs={{0,4},{4,0},{8,12},{12,8},{16,20},{20,16},{24,28},{28,24},{1,5},{5... | collective-permute-start | bytes 884744 | tf_op jit(solution)/shard_map/ppermute | solution.py:26
  26.4 18.6 %collective-permute-start.7 = (bf16[768,768]{1,0:T(8,128)(2,1)S(1)}, bf16[768,768]{1,0:T(8,128)(2,1)}, u32[]{:S(2)}, u32[]{:S(2)}) collective-permute-start(bf16[768,768]{1,0:T(8,128)(2,1)S(1)} %pad_maximum_fusion.2.refs_3_.refs_8_), channel_id=1, source_target_pairs={{0,1},{1,0},{2,3},{3,2},{4,5},{5,4},{6,7},{7,6},{8,9},{9,8},{10,11... | collective-permute-start | bytes 3538952 | tf_op jit(solution)/shard_map/ppermute | solution.py:26
  39.2 5.8 %collective-permute-start.8 = (bf16[768,768]{1,0:T(8,128)(2,1)}, bf16[768,768]{1,0:T(8,128)(2,1)}, u32[]{:S(2)}, u32[]{:S(2)}) collective-permute-start(bf16[768,768]{1,0:T(8,128)(2,1)} %pad_maximum_fusion.3.refs_5_.refs_10_), channel_id=1, source_target_pairs={{0,1},{1,0},{2,3},{3,2},{4,5},{5,4},{6,7},{7,6},{8,9},{9,8},{10,11... | collective-permute-start | bytes 3538952 | tf_op jit(solution)/shard_map/ppermute | solution.py:26
  41.5 17.3 %collective-permute-start.9 = (bf16[384,768]{1,0:T(8,128)(2,1)}, bf16[384,768]{1,0:T(8,128)(2,1)}, u32[]{:S(2)}, u32[]{:S(2)}) collective-permute-start(bf16[384,768]{1,0:T(8,128)(2,1)} %constant_dynamic-slice_fusion.3), channel_id=1, source_target_pairs={{0,2},{1,3},{2,0},{3,1},{4,6},{5,7},{6,4},{7,5},{8,10},{9,11},{10,... | collective-permute-start | bytes 1769480 | tf_op jit(solution)/shard_map/ppermute | solution.py:26
  41.6 49.0 %collective-permute-start.13 = (bf16[1536,768]{1,0:T(8,128)(2,1)}, bf16[1536,768]{1,0:T(8,128)(2,1)}, u32[]{:S(2)}, u32[]{:S(2)}) collective-permute-start(bf16[1536,768]{1,0:T(8,128)(2,1)} %copy-done.27), channel_id=1, source_target_pairs={{0,1},{1,0},{2,3},{3,2},{4,5},{5,4},{6,7},{7,6},{8,9},{9,8},{10,11... | collective-permute-start | bytes 7077896 | tf_op jit(solution)/shard_map/ppermute | solution.py:26
  58.8 30.8 %all-to-all-start.1 = ((bf16[4,192,1024]{2,1,0:T(8,128)(2,1)}), bf16[4,192,1024]{2,1,0:T(8,128)(2,1)}, u32[]{:S(2)}, u32[]{:S(2)}) async-start(bf16[4,192,1024]{2,1,0:T(8,128)(2,1)} %bitcast.184), calls=%async_computation.1 | async-start | bytes 3145728 | tf_op jit(solution)/shard_map/all_to_all | solution.py:540
  65.0 2.8 collective-permute-start.10
  65.0 23.8 %collective-permute-start.11 = (bf16[384,768]{1,0:T(8,128)(2,1)}, bf16[384,768]{1,0:T(8,128)(2,1)S(1)}, u32[]{:S(2)}, u32[]{:S(2)}) collective-permute-start(bf16[384,768]{1,0:T(8,128)(2,1)} %collective-permute-done.9), channel_id=1, source_target_pairs={{0,4},{4,0},{8,12},{12,8},{16,20},{20,16},{24,28},{28,24},{1,5},{5... | collective-permute-start | bytes 1769480 | tf_op jit(solution)/shard_map/ppermute | solution.py:26
  66.4 23.2 %collective-permute-start.12 = (bf16[384,768]{1,0:T(8,128)(2,1)}, bf16[384,768]{1,0:T(8,128)(2,1)}, u32[]{:S(2)}, u32[]{:S(2)}) collective-permute-start(bf16[384,768]{1,0:T(8,128)(2,1)} %collective-permute-done.9), channel_id=1, source_target_pairs={{0,8},{4,12},{8,0},{12,4},{16,24},{20,28},{24,16},{28,20},{1,9},{5... | collective-permute-start | bytes 1769480 | tf_op jit(solution)/shard_map/ppermute | solution.py:26
  67.8 12.0 %copy-start.31 = (bf16[272,1536]{1,0:T(8,128)(2,1)}, bf16[272,1536]{1,0:T(8,128)(2,1)S(1)}, u32[]{:S(2)}) copy-start(bf16[272,1536]{1,0:T(8,128)(2,1)S(1)} %collective-permute-done.10.refs_3_.refs_6_) | copy-start | bytes 2506756
  89.7 14.0 %collective-permute-start.14 = (bf16[384,768]{1,0:T(8,128)(2,1)}, bf16[384,768]{1,0:T(8,128)(2,1)S(1)}, u32[]{:S(2)}, u32[]{:S(2)}) collective-permute-start(bf16[384,768]{1,0:T(8,128)(2,1)} %collective-permute-done.12), channel_id=1, source_target_pairs={{0,4},{4,0},{8,12},{12,8},{16,20},{20,16},{24,28},{28,24},{1,5},{5... | collective-permute-start | bytes 1769480 | tf_op jit(solution)/shard_map/ppermute | solution.py:26
  92.0 11.7 %copy-start.75 = (bf16[384,768]{1,0:T(8,128)(2,1)S(1)}, bf16[384,768]{1,0:T(8,128)(2,1)}, u32[]{:S(2)}) copy-start(bf16[384,768]{1,0:T(8,128)(2,1)} %copy-done.74) | copy-start | bytes 1769476
  105.4 6.1 %collective-permute-start.15 = (bf16[1536,768]{1,0:T(8,128)(2,1)S(1)}, bf16[1536,768]{1,0:T(8,128)(2,1)S(1)}, u32[]{:S(2)}, u32[]{:S(2)}) collective-permute-start(bf16[1536,768]{1,0:T(8,128)(2,1)S(1)} %pad_maximum_fusion.refs_4_), channel_id=1, source_target_pairs={{0,1},{1,0},{2,3},{3,2},{4,5},{5,4},{6,7},{7,6},{8,9},{9,8},{10,11... | collective-permute-start | bytes 7077896 | tf_op jit(solution)/shard_map/ppermute | solution.py:26
  108.7 16.3 %collective-permute-start.16 = (bf16[1536,768]{1,0:T(8,128)(2,1)}, bf16[1536,768]{1,0:T(8,128)(2,1)}, u32[]{:S(2)}, u32[]{:S(2)}) collective-permute-start(bf16[1536,768]{1,0:T(8,128)(2,1)} %get-tuple-element.166), channel_id=1, source_target_pairs={{0,1},{1,0},{2,3},{3,2},{4,5},{5,4},{6,7},{7,6},{8,9},{9,8},{10,11... | collective-permute-start | bytes 7077896 | tf_op jit(solution)/shard_map/ppermute | solution.py:26
  124.6 21.6 %collective-permute-start.18 = (bf16[1536,768]{1,0:T(8,128)(2,1)}, bf16[1536,768]{1,0:T(8,128)(2,1)}, u32[]{:S(2)}, u32[]{:S(2)}) collective-permute-start(bf16[1536,768]{1,0:T(8,128)(2,1)} %get-tuple-element.172), channel_id=1, source_target_pairs={{0,1},{1,0},{2,3},{3,2},{4,5},{5,4},{6,7},{7,6},{8,9},{9,8},{10,11... | collective-permute-start | bytes 7077896 | tf_op jit(solution)/shard_map/ppermute | solution.py:26
  133.3 13.0 %copy-start.13 = (f32[1024,768]{1,0:T(8,128)S(1)}, f32[1024,768]{1,0:T(8,128)}, u32[]{:S(2)}) copy-start(f32[1024,768]{1,0:T(8,128)} %copy-done.12) | copy-start | bytes 9437188
  133.3 13.0 %copy-start.22 = (bf16[1024,768]{1,0:T(8,128)(2,1)S(1)}, bf16[1024,768]{1,0:T(8,128)(2,1)}, u32[]{:S(2)}) copy-start(bf16[1024,768]{1,0:T(8,128)(2,1)} %copy-done.20) | copy-start | bytes 4718596
  133.3 13.0 %copy-start.45 = (bf16[1024,768]{1,0:T(8,128)(2,1)S(1)}, bf16[1024,768]{1,0:T(8,128)(2,1)}, u32[]{:S(2)}) copy-start(bf16[1024,768]{1,0:T(8,128)(2,1)} %copy-done.41) | copy-start | bytes 4718596
  145.3 27.8 %collective-permute-start.17 = (bf16[2,384,768]{2,1,0:T(8,128)(2,1)}, bf16[2,384,768]{2,1,0:T(8,128)(2,1)}, u32[]{:S(2)}, u32[]{:S(2)}) collective-permute-start(bf16[2,384,768]{2,1,0:T(8,128)(2,1)} %constant_dynamic-slice_fusion.2), channel_id=1, source_target_pairs={{0,4},{4,0},{8,12},{12,8},{16,20},{20,16},{24,28},{28,24},{1,5},{5... | collective-permute-start | bytes 3538952 | tf_op jit(solution)/shard_map/ppermute | solution.py:26
  147.1 12.1 %copy-start.3 = (bf16[1024,768]{1,0:T(8,128)(2,1)S(1)}, bf16[1024,768]{1,0:T(8,128)(2,1)}, u32[]{:S(2)}) copy-start(bf16[1024,768]{1,0:T(8,128)(2,1)} %copy-done.1) | copy-start | bytes 4718596
  147.1 12.1 %copy-start.11 = (f32[1024,768]{1,0:T(8,128)S(1)}, f32[1024,768]{1,0:T(8,128)}, u32[]{:S(2)}) copy-start(f32[1024,768]{1,0:T(8,128)} %copy-done.10) | copy-start | bytes 9437188
  147.1 12.1 %copy-start.19 = (bf16[1024,768]{1,0:T(8,128)(2,1)S(1)}, bf16[1024,768]{1,0:T(8,128)(2,1)}, u32[]{:S(2)}) copy-start(bf16[1024,768]{1,0:T(8,128)(2,1)} %copy-done.18) | copy-start | bytes 4718596
  147.1 12.1 %copy-start.30 = (bf16[768,768]{1,0:T(8,128)(2,1)S(1)}, bf16[768,768]{1,0:T(8,128)(2,1)}, u32[]{:S(2)}) copy-start(bf16[768,768]{1,0:T(8,128)(2,1)} %copy-done.29) | copy-start | bytes 3538948
  171.6 11.5 %collective-permute-start.20 = (bf16[272,1536]{1,0:T(8,128)(2,1)}, bf16[272,1536]{1,0:T(8,128)(2,1)S(1)}, u32[]{:S(2)}, u32[]{:S(2)}) collective-permute-start(bf16[272,1536]{1,0:T(8,128)(2,1)} %maximum_maximum_fusion.1), channel_id=1, source_target_pairs={{0,1},{1,0},{2,3},{3,2},{4,5},{5,4},{6,7},{7,6},{8,9},{9,8},{10,11... | collective-permute-start | bytes 2506760 | tf_op jit(solution)/shard_map/ppermute | solution.py:26
  176.1 38.3 %all-to-all-start.2 = ((bf16[4,2,96,768]{3,2,1,0:T(8,128)(2,1)}), bf16[4,2,96,768]{3,2,1,0:T(8,128)(2,1)}, u32[]{:S(2)}, u32[]{:S(2)}) async-start(bf16[4,2,96,768]{3,2,1,0:T(8,128)(2,1)} %copy.42), calls=%async_computation.2 | async-start | bytes 2359296 | tf_op jit(solution)/shard_map/all_to_all | solution.py:644
  181.9 32.4 %collective-permute-start.19 = (bf16[2,384,768]{2,1,0:T(8,128)(2,1)S(1)}, bf16[2,384,768]{2,1,0:T(8,128)(2,1)}, u32[]{:S(2)}, u32[]{:S(2)}) collective-permute-start(bf16[2,384,768]{2,1,0:T(8,128)(2,1)S(1)} %constant_dynamic-slice_fusion.1), channel_id=1, source_target_pairs={{0,4},{4,0},{8,12},{12,8},{16,20},{20,16},{24,28},{28,24},{1,5},{5... | collective-permute-start | bytes 3538952 | tf_op jit(solution)/shard_map/ppermute | solution.py:26
  195.7 9.7 %copy-start.6 = (bf16[4,192,1024]{2,1,0:T(8,128)(2,1)S(1)}, bf16[4,192,1024]{2,1,0:T(8,128)(2,1)}, u32[]{:S(2)}) copy-start(bf16[4,192,1024]{2,1,0:T(8,128)(2,1)} %copy-done.4) | copy-start | bytes 4718596
  195.8 9.7 %copy-start.36 = (f32[1024,768]{1,0:T(8,128)S(1)}, f32[1024,768]{1,0:T(8,128)}, u32[]{:S(2)}) copy-start(f32[1024,768]{1,0:T(8,128)} %copy-done.35) | copy-start | bytes 9437188
  195.8 9.7 %copy-start.51 = (bf16[3,768,768]{2,1,0:T(8,128)(2,1)S(1)}, bf16[3,768,768]{2,1,0:T(8,128)(2,1)}, u32[]{:S(2)}) copy-start(bf16[3,768,768]{2,1,0:T(8,128)(2,1)} %copy-done.50) | copy-start | bytes 10616836
  204.0 8.7 %collective-permute-start.21 = (bf16[2,1024,768]{2,1,0:T(8,128)(2,1)S(1)}, bf16[2,1024,768]{2,1,0:T(8,128)(2,1)S(1)}, u32[]{:S(2)}, u32[]{:S(2)}) collective-permute-start(bf16[2,1024,768]{2,1,0:T(8,128)(2,1)S(1)} %get-tuple-element.200), channel_id=1, source_target_pairs={{0,1},{1,0},{2,3},{3,2},{4,5},{5,4},{6,7},{7,6},{8,9},{9,8},{10,11... | collective-permute-start | bytes 9437192 | tf_op jit(solution)/shard_map/ppermute | solution.py:26
  217.4 33.2 %all-to-all-start.3 = ((bf16[4,2,96,768]{3,2,1,0:T(8,128)(2,1)}), bf16[4,2,96,768]{3,2,1,0:T(8,128)(2,1)S(1)}, u32[]{:S(2)}, u32[]{:S(2)}) async-start(bf16[4,2,96,768]{3,2,1,0:T(8,128)(2,1)} %copy.43), calls=%async_computation.3 | async-start | bytes 2359296 | tf_op jit(solution)/shard_map/all_to_all | solution.py:644
  222.2 1.2 collective-permute-start.22
  229.1 36.0 %collective-permute-start.23 = (bf16[1024,768]{1,0:T(8,128)(2,1)}, bf16[1024,768]{1,0:T(8,128)(2,1)}, u32[]{:S(2)}, u32[]{:S(2)}) collective-permute-start(bf16[1024,768]{1,0:T(8,128)(2,1)} %get-tuple-element.258), channel_id=1, source_target_pairs={{0,2},{1,3},{2,0},{3,1},{4,6},{5,7},{6,4},{7,5},{8,10},{9,11},{10,... | collective-permute-start | bytes 4718600 | tf_op jit(solution)/shard_map/ppermute | solution.py:26
  250.7 20.6 %collective-permute-start.24 = (bf16[2,96,768]{2,1,0:T(8,128)(2,1)S(1)}, bf16[2,96,768]{2,1,0:T(8,128)(2,1)S(1)}, u32[]{:S(2)}, u32[]{:S(2)}) collective-permute-start(bf16[2,96,768]{2,1,0:T(8,128)(2,1)S(1)} %fusion.6), channel_id=1, source_target_pairs={{0,2},{1,3},{2,0},{3,1},{4,6},{5,7},{6,4},{7,5},{8,10},{9,11},{10,... | collective-permute-start | bytes 884744 | tf_op jit(solution)/shard_map/ppermute | solution.py:26
  252.2 19.1 %copy-start.60 = (f32[1024,768]{1,0:T(8,128)S(1)}, f32[1024,768]{1,0:T(8,128)}, u32[]{:S(2)}) copy-start(f32[1024,768]{1,0:T(8,128)} %get-tuple-element.216) | copy-start | bytes 9437188
  255.7 24.2 %collective-permute-start.29 = (bf16[2,192,1024]{2,1,0:T(8,128)(2,1)}, bf16[2,192,1024]{2,1,0:T(8,128)(2,1)S(1)}, u32[]{:S(2)}, u32[]{:S(2)}) collective-permute-start(bf16[2,192,1024]{2,1,0:T(8,128)(2,1)} %pad_maximum_fusion.6), channel_id=1, source_target_pairs={{0,1},{1,0},{2,3},{3,2},{4,5},{5,4},{6,7},{7,6},{8,9},{9,8},{10,11... | collective-permute-start | bytes 2359304 | tf_op jit(solution)/shard_map/ppermute | solution.py:26
  274.2 18.2 %collective-permute-start.28 = (bf16[1,512,768]{2,1,0:T(8,128)(2,1)}, bf16[1,512,768]{2,1,0:T(8,128)(2,1)}, u32[]{:S(2)}, u32[]{:S(2)}) collective-permute-start(bf16[1,512,768]{2,1,0:T(8,128)(2,1)} %dynamic-slice_bitcast_fusion), channel_id=1, source_target_pairs={{0,4},{4,0},{8,12},{12,8},{16,20},{20,16},{24,28},{28,24},{1,5},{5... | collective-permute-start | bytes 2359304 | tf_op jit(solution)/shard_map/ppermute | solution.py:26
  276.0 18.9 %collective-permute-start.25 = (bf16[2,96,768]{2,1,0:T(8,128)(2,1)S(1)}, bf16[2,96,768]{2,1,0:T(8,128)(2,1)}, u32[]{:S(2)}, u32[]{:S(2)}) collective-permute-start(bf16[2,96,768]{2,1,0:T(8,128)(2,1)S(1)} %fusion.4), channel_id=1, source_target_pairs={{0,8},{4,12},{8,0},{12,4},{16,24},{20,28},{24,16},{28,20},{1,9},{5... | collective-permute-start | bytes 884744 | tf_op jit(solution)/shard_map/ppermute | solution.py:26
  277.7 17.2 %collective-permute-start.26 = (bf16[2,96,768]{2,1,0:T(8,128)(2,1)S(1)}, bf16[2,96,768]{2,1,0:T(8,128)(2,1)}, u32[]{:S(2)}, u32[]{:S(2)}) collective-permute-start(bf16[2,96,768]{2,1,0:T(8,128)(2,1)S(1)} %fusion.4), channel_id=1, source_target_pairs={{0,16},{4,20},{8,24},{12,28},{16,0},{20,4},{24,8},{28,12},{1,17},{... | collective-permute-start | bytes 884744 | tf_op jit(solution)/shard_map/ppermute | solution.py:26
  279.8 18.4 %collective-permute-start.27 = (bf16[2,96,768]{2,1,0:T(8,128)(2,1)S(1)}, bf16[2,96,768]{2,1,0:T(8,128)(2,1)}, u32[]{:S(2)}, u32[]{:S(2)}) collective-permute-start(bf16[2,96,768]{2,1,0:T(8,128)(2,1)S(1)} %fusion.4), channel_id=1, source_target_pairs={{0,24},{4,28},{8,16},{12,20},{16,8},{20,12},{24,0},{28,4},{1,25},{... | collective-permute-start | bytes 884744 | tf_op jit(solution)/shard_map/ppermute | solution.py:26
  279.8 19.5 %copy-start.64 = (bf16[2,192,1024]{2,1,0:T(8,128)(2,1)}, bf16[2,192,1024]{2,1,0:T(8,128)(2,1)S(1)}, u32[]{:S(2)}) copy-start(bf16[2,192,1024]{2,1,0:T(8,128)(2,1)S(1)} %collective-permute-done.29) | copy-start | bytes 2359300
  299.5 36.5 %collective-permute-start.30 = (bf16[2,384,768]{2,1,0:T(8,128)(2,1)S(1)}, bf16[2,384,768]{2,1,0:T(8,128)(2,1)}, u32[]{:S(2)}, u32[]{:S(2)}) collective-permute-start(bf16[2,384,768]{2,1,0:T(8,128)(2,1)S(1)} %pad_maximum_fusion.4), channel_id=1, source_target_pairs={{0,4},{4,0},{8,12},{12,8},{16,20},{20,16},{24,28},{28,24},{1,5},{5... | collective-permute-start | bytes 3538952 | tf_op jit(solution)/shard_map/ppermute | solution.py:26
  300.7 35.4 %all-to-all-start.4 = ((bf16[4,1,128,768]{3,2,1,0:T(8,128)(2,1)}), bf16[4,1,128,768]{3,2,1,0:T(8,128)(2,1)}, u32[]{:S(2)}, u32[]{:S(2)}) async-start(bf16[4,1,128,768]{3,2,1,0:T(8,128)(2,1)} %bitcast.190), calls=%async_computation.4 | async-start | bytes 1572864 | tf_op jit(solution)/shard_map/all_to_all | solution.py:644
  312.9 5.5 %collective-permute-start.32 = (bf16[2,192,1024]{2,1,0:T(8,128)(2,1)}, bf16[2,192,1024]{2,1,0:T(8,128)(2,1)}, u32[]{:S(2)}, u32[]{:S(2)}) collective-permute-start(bf16[2,192,1024]{2,1,0:T(8,128)(2,1)} %pad_maximum_fusion.8), channel_id=1, source_target_pairs={{0,1},{1,0},{2,3},{3,2},{4,5},{5,4},{6,7},{7,6},{8,9},{9,8},{10,11... | collective-permute-start | bytes 2359304 | tf_op jit(solution)/shard_map/ppermute | solution.py:26
  317.0 19.0 %collective-permute-start.31 = (bf16[2,192,1024]{2,1,0:T(8,128)(2,1)}, bf16[2,192,1024]{2,1,0:T(8,128)(2,1)}, u32[]{:S(2)}, u32[]{:S(2)}) collective-permute-start(bf16[2,192,1024]{2,1,0:T(8,128)(2,1)} %pad_maximum_fusion.7), channel_id=1, source_target_pairs={{0,2},{1,3},{2,0},{3,1},{4,6},{5,7},{6,4},{7,5},{8,10},{9,11},{10,... | collective-permute-start | bytes 2359304 | tf_op jit(solution)/shard_map/ppermute | solution.py:26
  339.0 18.1 %collective-permute-start.33 = (bf16[2,192,1024]{2,1,0:T(8,128)(2,1)}, bf16[2,192,1024]{2,1,0:T(8,128)(2,1)}, u32[]{:S(2)}, u32[]{:S(2)}) collective-permute-start(bf16[2,192,1024]{2,1,0:T(8,128)(2,1)} %pad_maximum_fusion.9), channel_id=1, source_target_pairs={{0,2},{1,3},{2,0},{3,1},{4,6},{5,7},{6,4},{7,5},{8,10},{9,11},{10,... | collective-permute-start | bytes 2359304 | tf_op jit(solution)/shard_map/ppermute | solution.py:26
  342.6 24.8 %all-to-all-start.5 = ((bf16[4,1,128,768]{3,2,1,0:T(8,128)(2,1)}), bf16[4,1,128,768]{3,2,1,0:T(8,128)(2,1)}, u32[]{:S(2)}, u32[]{:S(2)}) async-start(bf16[4,1,128,768]{3,2,1,0:T(8,128)(2,1)} %broadcast_in_dim.16), calls=%async_computation.5 | async-start | bytes 1572864 | tf_op jit(solution)/shard_map/all_to_all | solution.py:662
  353.0 14.7 %copy-start.69 = (bf16[192,1024]{1,0:T(8,128)(2,1)S(1)}, bf16[192,1024]{1,0:T(8,128)(2,1)}, u32[]{:S(2)}) copy-start(bf16[192,1024]{1,0:T(8,128)(2,1)} %get-tuple-element.250) | copy-start | bytes 1179652
  353.0 14.7 %copy-start.70 = (bf16[192,1024]{1,0:T(8,128)(2,1)S(1)}, bf16[192,1024]{1,0:T(8,128)(2,1)}, u32[]{:S(2)}) copy-start(bf16[192,1024]{1,0:T(8,128)(2,1)} %get-tuple-element.251) | copy-start | bytes 1179652
  367.4 17.8 %collective-permute-start.34 = (bf16[1,512,768]{2,1,0:T(8,128)(2,1)}, bf16[1,512,768]{2,1,0:T(8,128)(2,1)S(1)}, u32[]{:S(2)}, u32[]{:S(2)}) collective-permute-start(bf16[1,512,768]{2,1,0:T(8,128)(2,1)} %bitcast.41), channel_id=1, source_target_pairs={{0,4},{4,0},{8,12},{12,8},{16,20},{20,16},{24,28},{28,24},{1,5},{5... | collective-permute-start | bytes 2359304 | tf_op jit(solution)/shard_map/ppermute | solution.py:26
  369.1 30.0 %slice-start = ((s8[4718592]{0:T(1024)(128)(4,1)}), s8[4194304]{0:T(1024)(128)(4,1)S(1)}, s32[]{:S(2)}) async-start(s8[4718592]{0:T(1024)(128)(4,1)} %bitcast.181), calls=%async_computation.6 | async-start | bytes 8388608
  386.5 12.5 %slice-start.1 = ((s8[4718592]{0:T(1024)(128)(4,1)}), s8[524288]{0:T(1024)(128)(4,1)S(1)}, s32[]{:S(2)}) async-start(s8[4718592]{0:T(1024)(128)(4,1)} %bitcast.181), calls=%async_computation.7 | async-start | bytes 1048576
  387.4 8.2 %collective-permute-start.35 = (bf16[256,768]{1,0:T(8,128)(2,1)S(1)}, bf16[256,768]{1,0:T(8,128)(2,1)S(1)}, u32[]{:S(2)}, u32[]{:S(2)}) collective-permute-start(bf16[256,768]{1,0:T(8,128)(2,1)S(1)} %get-tuple-element.292), channel_id=1, source_target_pairs={{0,2},{1,3},{2,0},{3,1},{4,6},{5,7},{6,4},{7,5},{8,10},{9,11},{10,... | collective-permute-start | bytes 1179656 | tf_op jit(solution)/shard_map/ppermute | solution.py:26
  395.7 5.9 %collective-permute-start.36 = (bf16[2,256,768]{2,1,0:T(8,128)(2,1)S(1)}, bf16[2,256,768]{2,1,0:T(8,128)(2,1)S(1)}, u32[]{:S(2)}, u32[]{:S(2)}) collective-permute-start(bf16[2,256,768]{2,1,0:T(8,128)(2,1)S(1)} %pad_maximum_fusion.10), channel_id=1, source_target_pairs={{0,1},{1,0},{2,3},{3,2},{4,5},{5,4},{6,7},{7,6},{8,9},{9,8},{10,11... | collective-permute-start | bytes 2359304 | tf_op jit(solution)/shard_map/ppermute | solution.py:26
  (68 other events, 227.8 us)

commit v3 on v2

--- a/solution.py
+++ b/solution.py
@@ -19,6 +19,7 @@
 MIB = 1024 * 1024
 RB = 512
 INPUT_COST = 72
+WINDOW_COST = 1000
 
 
 def flip(values, axis, mask):
@@ -425,9 +426,11 @@
     keys = data[:, D:].astype(F32)
     vg_ref[...] = (carried_grad * keys).astype(BF)
     kg_ref[...] = ((exp_grad + carried_grad * v_ref[...].astype(F32)) * keys).astype(BF)
-    pair_ref[:, :WIN] = mm_t(own, data).astype(BF)
+    r = info[2] ^ step
+    slot = (r % 2) * 2 + r // 2
+    pair_ref[slot, :, :WIN] = mm_t(own, data).astype(BF)
     side = jnp.where(before, mm_t(own, left), 0.0) + jnp.where(after_own, mm_t(own, right), 0.0)
-    pair_ref[:, WIN:] = side.astype(BF)
+    pair_ref[slot, :, WIN:] = side.astype(BF)
 
 
 def window_back(info, terms, grads, grad_message, grad_totals, stacked, message, vals, tokens=()):
@@ -436,20 +439,20 @@
         window_kernel,
         rows // WIN,
         [None, whole, whole, whole, whole, whole, whole, rows_of(WIN)],
-        [rows_of(WIN)] * 3,
-        [shape_of((rows, D), BF), shape_of((rows, D), BF), shape_of((rows, 2 * WIN), BF)],
-        flops=8 * rows * D * 3 * WIN,
+        [rows_of(WIN), rows_of(WIN), whole],
+        [shape_of((rows, D), BF)] * 2 + [shape_of((rows // WIN, WIN, 2 * WIN), BF)],
+        flops=WINDOW_COST,
         tokens=tokens,
     )(info, terms, grads, grad_message, grad_totals, stacked, message, vals)
 
 
 def mixing_grads_kernel(
-    step, count, info, q_ref, k_ref, v_ref, m_ref, n_ref, b_ref, pair_ref, two_ref, ups_ref,
+    step, count, info, q_ref, k_ref, v_ref, m_ref, n_ref, b_ref, two_ref, ups_ref,
     keep_near, keep_far, send_ref, pack_ref,
 ):
     half, me = info[1], info[2]
+    keep_refs = (keep_near, keep_far)
     width = D // CHAN
-    keep_refs = (keep_near, keep_far)
     products = [t_mm(ref[...], n_ref[...]).astype(BF) for ref in (q_ref, k_ref, v_ref)]
     products.append(t_mm(m_ref[...], b_ref[...]).astype(BF))
 
@@ -479,53 +482,46 @@
         pack_ref[pl.ds(8 + (me ^ r), 1)] = ups_ref[r : r + 1]
     pack_ref[12:16] = jnp.zeros((4, D), F32)
 
-    for r in range(CHAN):
-        target = keep_refs[r // 2] if r % 2 == 0 else send_ref.at[r // 2]
-        block = me ^ r
-        rows = slice(D, D + WIN)
-        target[rows, : 2 * WIN] = pair_ref[pl.ds(pl.multiple_of(block * WIN, WIN), WIN)]
-        lines = [pack_ref[pl.ds(3 * block + i, 1)] for i in range(3)]
-        lines = [line[:, t * WIN : (t + 1) * WIN] for line in lines for t in range(3)]
-        lines = jnp.concatenate(lines + [jnp.zeros((WIN - 9, WIN), F32)], axis=0)
-        target[rows, 2 * WIN :] = lines.astype(BF)
-
-
-def mixing_grads(info, q_grad, k_grad, v_grad, mixed, normed, branch, pair_grad, two, ups, tokens=()):
+
+def mixing_grads(info, q_grad, k_grad, v_grad, mixed, normed, branch, two, ups, tokens=()):
     rows = normed.shape[0]
     return call(
         mixing_grads_kernel,
         1,
-        [None] + [whole] * 9,
-        [whole] * 3,
-        [shape_of((D + WIN, D), BF)] * 2 + [shape_of((2, D + WIN, D), BF)],
-        scratch=[pltpu.VMEM((16, D), F32)],
+        [None] + [whole] * 8,
+        [whole] * 4,
+        [shape_of((D, D), BF)] * 2 + [shape_of((2, D, D), BF), shape_of((16, D), F32)],
         flops=8 * rows * D * D,
         mem=18,
         tokens=tokens,
-    )(info, q_grad, k_grad, v_grad, mixed, normed, branch, pair_grad, two, ups)
-
-
-def input_kernel(step, count, q_ref, k_ref, v_ref, w_ref, x_ref, vec, resg_ref, out_ref, cols_ref):
+    )(info, q_grad, k_grad, v_grad, mixed, normed, branch, two, ups)
+
+
+def input_kernel(
+    step, count, q_ref, k_ref, v_ref, w_ref, x_ref, vec, resg_ref, pack_ref, out_ref, cols_ref
+):
     upstream = mm(q_ref[...], w_ref[0]) + mm(k_ref[...], w_ref[1]) + mm(v_ref[...], w_ref[2])
     centred, inv_scale = normalize(x_ref[...].astype(F32).T)
     grad = resg_ref[...] + norm_back(upstream, centred, inv_scale, vec[0:1])
     out_ref[...] = grad.T.astype(BF)
-    cols = [col_sum(upstream * centred), col_sum(upstream), jnp.zeros((6, D), F32)]
-    add_into(cols_ref, step, jnp.concatenate(cols, axis=0))
-
-
-def input_back(q_grad, k_grad, v_grad, weights, x_t, vec, res_grad, tokens=()):
+    if step == 0:
+        cols_ref[...] = pack_ref[...]
+    cols_ref[0:1] += col_sum(upstream * centred)
+    cols_ref[1:2] += col_sum(upstream)
+
+
+def input_back(q_grad, k_grad, v_grad, weights, x_t, vec, res_grad, pack, tokens=()):
     rows = res_grad.shape[0]
     wide = rows_of(RB)
     return call(
         input_kernel,
         rows // RB,
-        [wide, wide, wide, whole, cols_of(RB), whole, wide],
+        [wide, wide, wide, whole, cols_of(RB), whole, wide, whole],
         [cols_of(RB), whole],
-        [shape_of((D, rows), BF), shape_of((8, D), F32)],
+        [shape_of((D, rows), BF), shape_of((16, D), F32)],
         flops=INPUT_COST * rows * D * D,
         tokens=tokens,
-    )(q_grad, k_grad, v_grad, weights, x_t, vec, res_grad)
+    )(q_grad, k_grad, v_grad, weights, x_t, vec, res_grad, pack)
 
 
 def sync(*arrays):
@@ -562,11 +558,11 @@
     return lax.dynamic_slice_in_dim(values, index * size, size, axis)
 
 
-def unpack_kernel(step, count, info, packed_ref, pair_ref, out_ref, small_ref, *vectors):
+def unpack_kernel(step, count, info, packed_ref, pair_ref, out_ref, small_ref, ups_ref):
     before, after_own = side_masks()
     grow = [jnp.exp(pair_cols(pair_ref, step, count, k).astype(F32)) for k in (-1, 0, 1)]
-    own = packed_ref[step, :, :WIN].astype(F32)
-    side = packed_ref[step, :, WIN : 2 * WIN].astype(F32)
+    own = packed_ref[step, :WIN, :WIN].astype(F32)
+    side = packed_ref[step, :WIN, WIN:].astype(F32)
     squares = [jnp.zeros((WIN, WIN), F32)] * count
     squares[step] = own * grow[1]
     squares[(step - 1) % count] = jnp.where(before, side * grow[0], 0.0)
@@ -575,14 +571,10 @@
         out_ref[:, k * WIN : (k + 1) * WIN] = squares[k]
     if step == count - 1:
         me, width = info[2], D // CHAN
-        lines = []
+        every = 0.0
         for b in range(CHAN):
-            part = packed_ref[b, :16, 2 * WIN :].astype(F32)
-            for i in range(3):
-                lines.append(
-                    jnp.concatenate([part[3 * i + t : 3 * i + t + 1] for t in range(3)], axis=1)
-                )
-        every = jnp.concatenate(lines, axis=0)
+            part = packed_ref[b, WIN : WIN + 32].astype(F32)
+            every = every + jnp.concatenate([part[:16], part[16:, :WIN]], axis=1)
         mine = every[:8, :width]
         for k in range(1, CHAN):
             mine = jnp.where(me == k, every[:8, k * width : (k + 1) * width], mine)
@@ -591,7 +583,7 @@
             ups = jnp.where(me == k, every[8 + k : 9 + k], ups)
         small_ref[:, :width] = mine
         small_ref[:, width:] = jnp.zeros((8, D - width), F32)
-        vectors[0][...] = ups
+        ups_ref[...] = ups
 
 
 def unpack_pairs(info, packed, pair_bias, tokens=()):
@@ -668,6 +660,23 @@
         pieces = [jnp.where(own == 1, got, values), jnp.where(own == 1, values, got)]
         return jnp.concatenate(pieces, axis=1)
     return got.swapaxes(0, 1).reshape(values.shape[0], -1, values.shape[2])
+
+
+def scatter_all(values):
+    parts = values.reshape(lax.axis_size("dp"), -1, values.shape[1])
+    return lax.all_to_all(parts, "dp", 0, 0, tiled=True)
+
+
+def sum_all(got):
+    total = got[0].astype(F32)
+    for k in range(1, got.shape[0]):
+        total = total + got[k].astype(F32)
+    return total.astype(BF)
+
+
+def gather_all(values):
+    parts = jnp.broadcast_to(values[None], (lax.axis_size("dp"), *values.shape))
+    return lax.all_to_all(parts, "dp", 0, 0, tiled=True)
 
 
 def scatter_rest(values, stages):
@@ -783,79 +792,86 @@
         tokens=[tok],
     )
     far = far.reshape(2, D, D)
+    far_u, far_d = far[:1], far[1:]
+    far_uy = flip(far_u, "chan", 2)
+    far_dx = scatter_start(far_d, along)
     res_grad, branch, q_grad, grads, grad_totals, cols_two, tok = branch_back(
         info, into, residual, cot, vec, out_w, ratio, inverse, gate, tokens=[tok]
     )
-    near_x, tok = sync(near_x, tok)
-    near = scatter_end(near, near_x, along)
-    near_z = scatter_start(near, across)
-    far_x = scatter_start(far, along)
     grad_halo = message(grads, grad_totals)
     k_grad, v_grad, pair_grad, tok = window_back(
         info, terms, grads, grad_halo, grad_totals, stacked, halo, vals, tokens=[tok]
     )
+    t_got = flip(pair_grad[2:], "chan", 1)
     ups = jnp.concatenate([ups_0, ups_1, ups_2, ups_3], axis=0)
-    m_near, m_far, send, tok = mixing_grads(
-        info, q_grad, k_grad, v_grad, mixed, normed_one, branch, pair_grad, cols_two, ups, tokens=[tok]
+    m_near, m_far, send, pack, tok = mixing_grads(
+        info, q_grad, k_grad, v_grad, mixed, normed_one, branch, cols_two, ups, tokens=[tok]
     )
     got = flip(send, "chan", 1)
-    input_t, cols_one, tok = input_back(
-        q_grad, k_grad, v_grad, qkv_t, x_t, vec, res_grad, tokens=[tok]
-    )
-
-    cols_one = cols_one[:2] + flip(cols_one[:2], "chan", 1)
+    near_x, far_uy, far_dx, t_got, tok = sync(near_x, far_uy, far_dx, t_got, tok)
+    t = add(pair_grad[:2], t_got).astype(BF)
+    t_near, t_far = t[:1], flip(t[1:], "chan", 2)
+    near = scatter_end(near, near_x, along)
+    far_dy = flip(scatter_end(far_d, far_dx, along), "chan", 2)
+    far_ux = scatter_start(far_uy, along)
+    input_t, pack, tok = input_back(
+        q_grad, k_grad, v_grad, qkv_t, x_t, vec, res_grad, pack, tokens=[tok]
+    )
+
     got, tok = sync(got, tok)
-
-    def with_norm(values, there):
-        lines = jnp.where(there, cols_one, 0.0).reshape(6, WIN)
-        return values + jnp.pad(lines, ((D, WIN - 6), (2 * WIN, 0)))
-
-    m_far = flip(with_norm(add(m_far, got[1]), me == 2).astype(BF), "chan", 2)
-    m_near = with_norm(add(m_near, got[0]), me == 0)
-    near_z, far_x, tok = sync(near_z, far_x, tok)
-    near = scatter_end(near, near_z, across)
-    far = scatter_end(far, far_x, along)
-    far_z = scatter_start(far, across)
+    m_far = add(m_far, got[1]).astype(BF)
+    far_ux, far_dy, m_far, t_far, tok = sync(far_ux, far_dy, m_far, t_far, tok)
+    m_far = flip(m_far, "chan", 2)
+    f_u = add(near[:1], scatter_end(far_uy, far_ux, along)).astype(BF)
+    f_d = add(near[1:], far_dy).astype(BF)
+    f = jnp.concatenate([f_u, f_d], axis=0)
+    f_z = scatter_start(f, across)
+    m_near = add(m_near, got[0]).astype(BF)
+    half_cols = 2 * WIN
+    rest = jnp.pad(pack[:, half_cols:], ((0, 0), (0, half_cols - WIN)))
+    pack = jnp.pad(jnp.concatenate([pack[:, :half_cols], rest], axis=0), ((0, 96), (0, 0)))
+    t = jnp.concatenate([add(t_near, t_far)[0].astype(BF), pack.astype(BF)], axis=0)
+    t_all = scatter_all(t)
     layer_parts = pick(split_rows(layer_t, CHAN), me)
     input_parts = pick(split_rows(input_t, CHAN), me)
     layer_near = exchange_near(layer_parts)
     input_near = exchange_near(input_parts)
-    far_z, m_near, tok = sync(far_z, m_near, tok)
-    f_near = scatter_rest(near, others)
-    f_far = scatter_rest(scatter_end(far, far_z, across), others)
-    f_y = flip(f_far, "chan", 2)
-    m_far, f_y, tok = sync(m_far, f_y, tok)
-    f = gather_rest(add(f_near, f_y).astype(BF), others)
-    f_z = [flip(f, "dp", k) for k in across]
+    m_far, f_z, layer_near, tok = sync(m_far, f_z, layer_near, tok)
     m = add(m_near, m_far).astype(BF)[None]
     m_x = scatter_start(m, along)
-    m_x, f, layer_near, tok = sync(m_x, f, layer_near, tok)
+    f = gather_rest(scatter_rest(scatter_end(f, f_z, across), others), others)
+    f_z = [flip(f, "dp", k) for k in across]
+    layer_far = exchange_far(layer_parts, layer_near)
+    m_x, t_all, f, tok = sync(m_x, t_all, f, tok)
     m = scatter_end(m, m_x, along)
-    layer_far = exchange_far(layer_parts, layer_near)
-    *f_z, m, tok = sync(*f_z, m, tok)
     m_z = scatter_start(m, across)
+    t = sum_all(t_all)
+    *f_z, layer_far, m = sync(*f_z, layer_far, m)
     f = jnp.concatenate(pick([f, *f_z], own_share(across)), axis=1)
     f_x = gather_start(f, along)
-    m_z, f_x, layer_far, input_near, f = sync(m_z, f_x, layer_far, input_near, f)
-    m = scatter_rest(scatter_end(m, m_z, across), others)
-    m = gather_rest(m, others)
+    m_z, t, input_near, f = sync(m_z, t, input_near, f)
+    m = gather_rest(scatter_rest(scatter_end(m, m_z, across), others), others)
     m_z = gather_start(m, across)
-    f = gather_end(f, f_x, along).astype(F32)
     layer_out = columns(layer_parts, layer_near, layer_far, me)
     input_far = exchange_far(input_parts, input_near)
-    m_z, f, layer_out, input_far = sync(m_z, f, layer_out, input_far)
+    f_x, m, t, layer_out = sync(f_x, m, t, layer_out)
+    t_all = gather_all(t)
+    f_u = gather_end(f[:1], f_x[:1], along)[0].astype(F32)
+    f_d = gather_end(f[1:], f_x[1:], along)[0].astype(F32)
+    m_z, f_u, f_d, tok = sync(m_z, f_u, f_d, tok)
     m = gather_end(m, m_z, across)
     m_x = gather_start(m, along)
+    t_all, input_far, tok = sync(t_all, input_far, tok)
+    t = t_all.reshape(-1, half_cols)
+    t_y = flip(t, "chan", 2)
     input_grad = columns(input_parts, input_near, input_far, me)
-    m_x, input_grad, f = sync(m_x, input_grad, f)
+    m_x, t_y, input_grad = sync(m_x, t_y, input_grad)
+    pair = jnp.stack([t, t_y])
+    beside = flip(pair, "chan", 1)
     m = gather_end(m, m_x, along)[0]
-    block = m[D:]
-    other = flip(block, "chan", 2)
     qkv_out = jnp.swapaxes(m[: 3 * width].reshape(3, width, D).astype(F32), 1, 2)
-    out_out = m[3 * width : D].astype(F32)
-    other, qkv_out, out_out, tok = sync(other, qkv_out, out_out, tok)
-    pair = jnp.stack([block, other])
-    beside = flip(pair, "chan", 1)
+    out_out = m[3 * width :].astype(F32)
+    beside, qkv_out, out_out, tok = sync(beside, qkv_out, out_out, tok)
     table = jnp.stack(pick([pair[0], beside[0], pair[1], beside[1]], me))
     pair_out, small_out, ups_out, tok = unpack_pairs(info, table, pair_bias, tokens=[tok])
     vector = [small_out[k, :width] for k in range(8)]
@@ -871,9 +887,9 @@
         vector[4],
         vector[2],
         vector[3],
-        f[0],
+        f_u,
         ups_out.reshape(-1),
-        f[1],
+        f_d,
         vector[5],
     )
 

time: 415 us -> 369 us (0.89)
  waiting for transfers between devices: 124 us -> 91.8 us
  other arithmetic: 48.8 us -> 39.3 us
  local copies, waits for them, and re-layouts: 76 us -> 69.2 us
    ppermute x37 -> x40, waiting for transfers between devices: 93.1 us -> 42.9 us  [flip(): return lax.ppermute(values, axis, [(i, i ^ mask) for i in range(size)])]
    all_to_all x3 -> x2, waiting for transfers between devices: 20.1 us -> 38.6 us  [scatter_start(): lax.all_to_all(parts, 'dp', 0, 0, axis_index_groups=dp_groups(masks), til...]
    all_to_all x3 -> x2, starting transfers between devices: 18 us -> 8.62 us  [scatter_start(): lax.all_to_all(parts, 'dp', 0, 0, axis_index_groups=dp_groups(masks), til...]
    all_to_all x0 -> x2, starting transfers between devices: none -> 8.63 us  [the longest x1 4.97 us: gather_all(): return lax.all_to_all(parts, 'dp', 0, 0, tiled=True)]
    add x1 -> x0, other arithmetic: 5.67 us -> none  [with_norm(): return values + jnp.pad(lines, ((D, WIN - 6), (2 * WIN, 0)))]
    unnamed x177 -> x181, local copies, waits for them, and re-layouts: 54.8 us -> 49.8 us
    another operation x4, other arithmetic: 7.94 us -> 3.17 us  [exchange_far(): return flip(jnp.stack([pieces[2], near[1]]), 'chan', 2)]
    ppermute x37 -> x40, starting transfers between devices: 39.5 us -> 40.9 us  [flip(): return lax.ppermute(values, axis, [(i, i ^ mask) for i in range(size)])]
  transfers between devices with their start and end apart: 43 -> 47, of which waited for: 19 -> 16; matrix products, arithmetic and copies ran while one was open for 14% -> 14% of each run, Pallas kernels for 20% -> 23%
where the time goes in v3:
time: 369 us; the launch traced here: 362 us
  waiting for transfers between devices  91.8 us (25%)
  Pallas kernels  87.1 us (24%)
  starting transfers between devices  71.7 us (19%)
  local copies, waits for them, and re-layouts  69.2 us (19%)
  other arithmetic  39.3 us (11%)
    pallas_call x12, Pallas kernels, call(): return lambda *operands: run(*operands, *tokens)  87.1 us
    unnamed x181, local copies, waits for them, and re-layouts  49.8 us
    ppermute x40, waiting for transfers between devices, flip(): return lax.ppermute(values, axis, [(i, i ^ mask) for i in range(size)])  42.9 us
    ppermute x40, starting transfers between devices, flip(): return lax.ppermute(values, axis, [(i, i ^ mask) for i in range(size)])  40.9 us
    all_to_all x2, waiting for transfers between devices, scatter_start(): lax.all_to_all(parts, 'dp', 0, 0, axis_index_groups=dp_groups(masks), til...  38.6 us
    all_to_all x2, starting transfers between devices, to_rows(): pieces = lax.all_to_all(pieces, 'chan', 0, 0, tiled=True)  9.77 us
    all_to_all x2, starting transfers between devices, scatter_start(): lax.all_to_all(parts, 'dp', 0, 0, axis_index_groups=dp_groups(masks), til...  8.62 us
    all_to_all x1, waiting for transfers between devices, gather_start(): lax.all_to_all(parts, 'dp', 0, 0, axis_index_groups=dp_groups(masks), til...  7.69 us
  transfers between devices with their start and end apart: 47, of which 16 were waited for; matrix products, arithmetic and copies ran while one was open for 14% of the time, Pallas kernels for 23%

profile of v3, /device:TPU:1, one launch (start us, length us, event | category | flops | bytes accessed | tf_op | source)
XLA Modules:
  0.0 361.7 jit_solution(1250146594335333972)
XLA Ops:
  1.8 2.1 collective-permute-start
  4.0 2.7 copy.44
  6.7 4.0 %collective-permute-done = bf16[192,768]{1,0:T(8,128)(2,1)S(1)} collective-permute-done((bf16[192,768]{1,0:T(8,128)(2,1)S(1)}, bf16[192,768]{1,0:T(8,128)(2,1)S(1)}, u32[]{:S(2)}, u32[]{:S(2)}) %collective-permute-start) | collective-permute-done | bytes 294944 | tf_op jit(solution)/shard_map/ppermute | solution.py:27
  10.8 4.9 %all-to-all-start = ((bf16[4,192,1024]{2,1,0:T(8,128)(2,1)}), bf16[4,192,1024]{2,1,0:T(8,128)(2,1)S(1)}, u32[]{:S(2)}, u32[]{:S(2)}) async-start(bf16[4,192,1024]{2,1,0:T(8,128)(2,1)} %bitcast.176), calls=%async_computation | async-start | bytes 3145728 | tf_op jit(solution)/shard_map/all_to_all | solution.py:536
  15.9 1.5 collective-permute-start.1
  19.3 1.7 collective-permute-start.5
  21.3 3.4 collective-permute-done.1
  28.8 6.3 %collective-permute-done.5 = bf16[16,192]{1,0:T(8,128)(2,1)S(1)} collective-permute-done((bf16[16,192]{1,0:T(8,128)(2,1)S(1)}, bf16[16,192]{1,0:T(8,128)(2,1)S(1)}, u32[]{:S(2)}, u32[]{:S(2)}) %collective-permute-start.5) | collective-permute-done | bytes 6176 | tf_op jit(solution)/shard_map/ppermute | solution.py:27
  36.3 1.8 broadcast_select_fusion.35
  39.6 1.9 constant_dynamic-slice_fusion.3
  42.2 2.7 copy.43
  47.7 7.0 %shard_map.272 = (bf16[1024,768]{1,0:T(8,128)(2,1)S(1)}, bf16[1024,768]{1,0:T(8,128)(2,1)S(1)}, bf16[1024,768]{1,0:T(8,128)(2,1)S(1)}, bf16[1024,1536]{1,0:T(8,1...) custom-call(s32[3]{0:T(128)S(1)} %pad_add_fusion.refs_0_, ...), custom_call_target="tpu_custom_call" | custom-call | flops 3623878656 | bytes 12079595 | tf_op jit(solution)/shard_map/pallas_call | solution.py:82
  57.0 1.8 copy-done.54
  60.1 4.9 %all-to-all-start.1 = ((bf16[4,192,1024]{2,1,0:T(8,128)(2,1)}), bf16[4,192,1024]{2,1,0:T(8,128)(2,1)}, u32[]{:S(2)}, u32[]{:S(2)}) async-start(bf16[4,192,1024]{2,1,0:T(8,128)(2,1)} %bitcast.183), calls=%async_computation.1 | async-start | bytes 3145728 | tf_op jit(solution)/shard_map/all_to_all | solution.py:536
  68.1 1.7 copy-done.3
  72.4 7.3 %shard_map.273 = (bf16[1024,768]{1,0:T(8,128)(2,1)S(1)}, bf16[1024,768]{1,0:T(8,128)(2,1)S(1)}, f32[1024,768]{1,0:T(8,128)S(1)}, bf16[1024,768]{1,0:T(8,128)(2,1...) custom-call(s32[3]{0:T(128)S(1)} %pad_add_fusion.refs_0_, ...), custom_call_target="tpu_custom_call" | custom-call | flops 3623878656 | bytes 12079595 | tf_op jit(solution)/shard_map/pallas_call | solution.py:82
  79.8 1.7 copy-done.16
  81.4 1.7 copy-done.18
  92.0 11.0 %shard_map.274 = (f32[1024,768]{1,0:T(8,128)S(1)}, f32[1024,768]{1,0:T(8,128)S(1)}, f32[1,768]{1,0:T(1,128)S(1)}, bf16[1536,768]{1,0:T(8,128)(2,1)}, bf16[1024,7...) custom-call(s32[3]{0:T(128)S(1)} %pad_add_fusion.refs_0_, bf16[1024,768]{1,0:T(8,128)(2,1)S(1)} %copy-done.46, ...), custom_call_target="tpu_custom_call" | custom-call | flops 7247757312 | bytes 24159192 | tf_op jit(solution)/shard_map/pallas_call | solution.py:82
  105.3 2.0 collective-permute-start.15
  108.6 2.8 collective-permute-done.15.refs_4_
  111.4 9.7 %shard_map.275 = (f32[1024,768]{1,0:T(8,128)S(1)}, f32[1024,768]{1,0:T(8,128)S(1)}, f32[1,768]{1,0:T(1,128)S(1)}, bf16[1536,768]{1,0:T(8,128)(2,1)}, f32[8,128]{1,0:T(8,128)S(1)}) custom-call(s32[3]{0:T(128)S(1)} %pad_add_fusion.refs_0_, bf16[1024,768]{1,0:T(8,128)(2,1)S(1)} %copy-done.47, bf16[1024,768]{1,0:T(8,128)(2,1)S(1)} %get-tuple-element.164.refs_2_.refs_3_, ...), custom_call_target="tpu_custom_call" | custom-call | flops 7247757312 | bytes 24159192 | tf_op jit(solution)/shard_map/pallas_call | solution.py:82
  121.1 1.6 copy-done.58
  122.8 1.7 copy-done.60
  126.2 1.7 copy-done.36
  129.3 1.9 copy-done.59
  131.2 1.9 copy-done.61
  133.1 10.8 %shard_map.276 = (f32[1024,768]{1,0:T(8,128)S(1)}, f32[1024,768]{1,0:T(8,128)S(1)}, f32[1,768]{1,0:T(1,128)S(1)}, bf16[1536,768]{1,0:T(8,128)(2,1)S(1)}, f32[8,128]{1,0:T(8,128)S(1)}) custom-call(s32[3]{0:T(128)S(1)} %pad_add_fusion.refs_0_, bf16[1024,768]{1,0:T(8,128)(2,1)S(1)} %copy-done.48, bf16[1024,768]{1,0:T(8,128)(2,1)S(1)} %copy-done.27, ...), custom_call_target="tpu_custom_call" | custom-call | flops 7247757312 | bytes 24159192 | tf_op jit(solution)/shard_map/pallas_call | solution.py:82
  146.9 10.8 %shard_map.277 = (bf16[768,1024]{1,0:T(8,128)(2,1)S(1)}, f32[1024,768]{1,0:T(8,128)S(1)}, f32[1,768]{1,0:T(1,128)S(1)}, bf16[1536,768]{1,0:T(8,128)(2,1)S(1)}, f32[8,128]{1,0:T(8,128)S(1)}) custom-call(s32[3]{0:T(128)S(1)} %pad_add_fusion.refs_0_, bf16[1024,768]{1,0:T(8,128)(2,1)S(1)} %copy-done.49, bf16[1024,768]{1,0:T(8,128)(2,1)S(1)} %copy-done.28, ...), custom_call_target="tpu_custom_call" | custom-call | flops 7247757312 | bytes 24159192 | tf_op jit(solution)/shard_map/pallas_call | solution.py:82
  157.7 6.1 %shard_map.278 = (f32[1024,768]{1,0:T(8,128)S(1)}, bf16[1024,768]{1,0:T(8,128)(2,1)S(1)}, bf16[1024,768]{1,0:T(8,128)(2,1)S(1)}, bf16[1024,1536]{1,0:T(8,128)(2,...) custom-call(s32[3]{0:T(128)S(1)} %pad_add_fusion.refs_0_, ...), custom_call_target="tpu_custom_call" | custom-call | flops 1207959552 | bytes 4026531 | tf_op jit(solution)/shard_map/pallas_call | solution.py:82
  163.8 1.7 copy-done.41
  171.1 1.7 collective-permute-start.19
  174.3 1.9 copy-done.10
  180.2 7.0 %shard_map.279 = (bf16[1024,768]{1,0:T(8,128)(2,1)S(1)}, bf16[1024,768]{1,0:T(8,128)(2,1)S(1)}, bf16[4,256,512]{2,1,0:T(8,128)(2,1)S(1)}, f32[8,128]{1,0:T(8,128)S(1)}) custom-call(s32[3]{0:T(128)S(1)} %pad_add_fusion.refs_0_, bf16[1024,768]{1,0:T(8,128)(2,1)S(1)} %copy-done.34, bf16[1024,1536]{1,0:T(8,128)(2,1)S(1)} %copy-done.10, ...), custom_call_target="tpu_custom_call" | custom-call | flops 1000 | bytes 3 | tf_op jit(solution)/shard_map/pallas_call | solution.py:82
  188.3 6.9 %shard_map.280 = (bf16[768,768]{1,0:T(8,128)(2,1)S(1)}, bf16[768,768]{1,0:T(8,128)(2,1)S(1)}, bf16[2,768,768]{2,1,0:T(8,128)(2,1)S(1)}, f32[16,768]{1,0:T(8,128)S(1)}, f32[8,128]{1,0:T(8,128)S(1)}) custom-call(s32[3]{0:T(128)S(1)} %pad_add_fusion.refs_0_, bf16[1024,768]{1,0:T(8,128)(2,1)S(1)} %copy-done.51, ...), custom_call_target="tpu_custom_call" | custom-call | flops 4831838208 | bytes 16106127 | tf_op jit(solution)/shard_map/pallas_call | solution.py:82
  195.4 3.7 %collective-permute-done.19 = bf16[1,768,768]{2,1,0:T(8,128)(2,1)} collective-permute-done((bf16[1,768,768]{2,1,0:T(8,128)(2,1)}, bf16[1,768,768]{2,1,0:T(8,128)(2,1)}, u32[]{:S(2)}, u32[]{:S(2)}) %collective-permute-start.19) | collective-permute-done | bytes 1179680 | tf_op jit(solution)/shard_map/ppermute | solution.py:27
  204.1 6.2 %shard_map.281 = (bf16[768,1024]{1,0:T(8,128)(2,1)S(1)}, f32[16,768]{1,0:T(8,128)S(1)}, f32[8,128]{1,0:T(8,128)S(1)}) custom-call(bf16[1024,768]{1,0:T(8,128)(2,1)S(1)} %copy-done.51, bf16[1024,768]{1,0:T(8,128)(2,1)S(1)} %get-tuple-element.195.refs_2_.refs_1_, bf16[1024,768]{1,0:T(8,128)(2,1)S(1)} %get-tuple-element.196.refs_3_.refs_2_, ...), custom_call_target="tpu_custom_call" | custom-call | flops 43486543872 | bytes 144955152 | tf_op jit(solution)/shard_map/pallas_call | solution.py:82
  210.4 1.6 add_convert_fusion.1
  211.9 1.6 fusion.1
  213.7 5.0 %collective-permute-done.24 = bf16[1,384,768]{2,1,0:T(8,128)(2,1)S(1)} collective-permute-done((bf16[1,384,768]{2,1,0:T(8,128)(2,1)S(1)}, bf16[1,384,768]{2,1,0:T(8,128)(2,1)S(1)}, u32[]{:S(2)}, u32[]{:S(2)}) %collective-permute-start.24) | collective-permute-done | bytes 589856 | tf_op jit(solution)/shard_map/ppermute | solution.py:27
  221.4 4.4 %all-to-all-start.2 = ((bf16[4,2,96,768]{3,2,1,0:T(8,128)(2,1)}), bf16[4,2,96,768]{3,2,1,0:T(8,128)(2,1)}, u32[]{:S(2)}, u32[]{:S(2)}) async-start(bf16[4,2,96,768]{3,2,1,0:T(8,128)(2,1)} %bitcast.184), calls=%async_computation.2 | async-start | bytes 2359296 | tf_op jit(solution)/shard_map/all_to_all | solution.py:636
  229.0 2.4 collective-permute-start.28
  232.2 21.7 %all-to-all-done.2 = bf16[4,2,96,768]{3,2,1,0:T(8,128)(2,1)} async-done(((bf16[4,2,96,768]{3,2,1,0:T(8,128)(2,1)}), bf16[4,2,96,768]{3,2,1,0:T(8,128)(2,1)}, u32[]{:S(2)}, u32[]{:S(2)}) %all-to-all-start.2) | async-done | bytes 1179680 | tf_op jit(solution)/shard_map/all_to_all | solution.py:636
  254.0 3.7 %all-to-all-start.3 = ((bf16[8,48,512]{2,1,0:T(8,128)(2,1)}), bf16[8,48,512]{2,1,0:T(8,128)(2,1)S(1)}, u32[]{:S(2)}, u32[]{:S(2)}) async-start(bf16[8,48,512]{2,1,0:T(8,128)(2,1)} %bitcast.195), calls=%async_computation.3 | async-start | bytes 786432 | tf_op jit(solution)/shard_map/all_to_all | solution.py:667
  257.7 2.0 add_convert_fusion
  266.0 1.5 fusion.8
  268.8 2.1 collective-permute-start.30
  271.1 6.0 %collective-permute-done.33 = bf16[1,384,768]{2,1,0:T(8,128)(2,1)} collective-permute-done((bf16[1,384,768]{2,1,0:T(8,128)(2,1)}, bf16[1,384,768]{2,1,0:T(8,128)(2,1)}, u32[]{:S(2)}, u32[]{:S(2)}) %collective-permute-start.33) | collective-permute-done | bytes 589856 | tf_op jit(solution)/shard_map/ppermute | solution.py:27
  277.2 2.0 fusion.4
  279.2 4.2 %all-to-all-start.4 = ((bf16[4,1,96,768]{3,2,1,0:T(8,128)(2,1)}), bf16[4,1,96,768]{3,2,1,0:T(8,128)(2,1)S(1)}, u32[]{:S(2)}, u32[]{:S(2)}) async-start(bf16[4,1,96,768]{3,2,1,0:T(8,128)(2,1)} %bitcast.33), calls=%async_computation.4 | async-start | bytes 1179648 | tf_op jit(solution)/shard_map/all_to_all | solution.py:636
  284.4 1.5 collective-permute-start.35
  285.9 2.5 collective-permute-done.31
  290.1 16.9 %all-to-all-done.4 = bf16[4,1,96,768]{3,2,1,0:T(8,128)(2,1)S(1)} async-done(((bf16[4,1,96,768]{3,2,1,0:T(8,128)(2,1)}), bf16[4,1,96,768]{3,2,1,0:T(8,128)(2,1)S(1)}, u32[]{:S(2)}, u32[]{:S(2)}) %all-to-all-start.4) | async-done | bytes 589856 | tf_op jit(solution)/shard_map/all_to_all | solution.py:636
  307.9 3.8 %all-to-all-start.5 = ((bf16[4,1,96,768]{3,2,1,0:T(8,128)(2,1)}), bf16[4,1,96,768]{3,2,1,0:T(8,128)(2,1)S(1)}, u32[]{:S(2)}, u32[]{:S(2)}) async-start(bf16[4,1,96,768]{3,2,1,0:T(8,128)(2,1)} %broadcast_in_dim.7), calls=%async_computation.5 | async-start | bytes 1179648 | tf_op jit(solution)/shard_map/all_to_all | solution.py:654
  311.7 1.5 bitcast_select_fusion.15
  316.0 7.7 %all-to-all-done.5 = bf16[4,1,96,768]{3,2,1,0:T(8,128)(2,1)S(1)} async-done(((bf16[4,1,96,768]{3,2,1,0:T(8,128)(2,1)}), bf16[4,1,96,768]{3,2,1,0:T(8,128)(2,1)S(1)}, u32[]{:S(2)}, u32[]{:S(2)}) %all-to-all-start.5) | async-done | bytes 589856 | tf_op jit(solution)/shard_map/all_to_all | solution.py:654
  324.5 5.0 %all-to-all-start.6 = ((bf16[8,48,512]{2,1,0:T(8,128)(2,1)}), bf16[8,48,512]{2,1,0:T(8,128)(2,1)S(1)}, u32[]{:S(2)}, u32[]{:S(2)}) async-start(bf16[8,48,512]{2,1,0:T(8,128)(2,1)} %broadcast_in_dim.8), calls=%async_computation.6 | async-start | bytes 786432 | tf_op jit(solution)/shard_map/all_to_all | solution.py:679
  329.4 1.5 broadcast_select_fusion.3
  330.9 2.5 fusion.2
  333.5 1.5 collective-permute-start.36
  334.9 2.6 all-to-all-done.6
  340.7 6.9 %collective-permute-done.36 = bf16[1,384,768]{2,1,0:T(8,128)(2,1)S(1)} collective-permute-done((bf16[1,384,768]{2,1,0:T(8,128)(2,1)S(1)}, bf16[1,384,768]{2,1,0:T(8,128)(2,1)S(1)}, u32[]{:S(2)}, u32[]{:S(2)}) %collective-permute-start.36) | collective-permute-done | bytes 589856 | tf_op jit(solution)/shard_map/ppermute | solution.py:27
  347.6 4.4 %collective-permute-start.39 = (bf16[2,384,512]{2,1,0:T(8,128)(2,1)S(1)}, bf16[2,384,512]{2,1,0:T(8,128)(2,1)S(1)}, u32[]{:S(2)}, u32[]{:S(2)}) collective-permute-start(bf16[2,384,512]{2,1,0:T(8,128)(2,1)S(1)} %pad_maximum_fusion.11), channel_id=1, source_target_pairs={{0,1},{1,0},{2,3},{3,2},{4,5},{5,4},{6,7},{7,6},{8,9},{9,8},{10,11... | collective-permute-start | bytes 2359304 | tf_op jit(solution)/shard_map/ppermute | solution.py:27
  356.2 3.5 shard_map.282
  (308 shorter events, 88.9 us)
Async XLA Ops:
  1.8 8.9 %collective-permute-start = (bf16[192,768]{1,0:T(8,128)(2,1)S(1)}, bf16[192,768]{1,0:T(8,128)(2,1)S(1)}, u32[]{:S(2)}, u32[]{:S(2)}) collective-permute-start(bf16[192,768]{1,0:T(8,128)(2,1)S(1)} %fusion.9), channel_id=1, source_target_pairs={{0,2},{1,3},{2,0},{3,1},{4,6},{5,7},{6,4},{7,5},{8,10},{9,11},{10,... | collective-permute-start | bytes 884744 | tf_op jit(solution)/shard_map/ppermute | solution.py:27
  10.8 25.5 %all-to-all-start = ((bf16[4,192,1024]{2,1,0:T(8,128)(2,1)}), bf16[4,192,1024]{2,1,0:T(8,128)(2,1)S(1)}, u32[]{:S(2)}, u32[]{:S(2)}) async-start(bf16[4,192,1024]{2,1,0:T(8,128)(2,1)} %bitcast.176), calls=%async_computation | async-start | bytes 3145728 | tf_op jit(solution)/shard_map/all_to_all | solution.py:536
  15.9 8.8 %collective-permute-start.1 = (bf16[192,768]{1,0:T(8,128)(2,1)S(1)}, bf16[192,768]{1,0:T(8,128)(2,1)S(1)}, u32[]{:S(2)}, u32[]{:S(2)}) collective-permute-start(bf16[192,768]{1,0:T(8,128)(2,1)S(1)} %collective-permute-done), channel_id=1, source_target_pairs={{0,4},{4,0},{8,12},{12,8},{16,20},{20,16},{24,28},{28,24},{1,5},{5... | collective-permute-start | bytes 884744 | tf_op jit(solution)/shard_map/ppermute | solution.py:27
  17.4 8.4 %collective-permute-start.2 = (bf16[192,768]{1,0:T(8,128)(2,1)S(1)}, bf16[192,768]{1,0:T(8,128)(2,1)}, u32[]{:S(2)}, u32[]{:S(2)}) collective-permute-start(bf16[192,768]{1,0:T(8,128)(2,1)S(1)} %collective-permute-done), channel_id=1, source_target_pairs={{0,8},{4,12},{8,0},{12,4},{16,24},{20,28},{24,16},{28,20},{1,9},{5... | collective-permute-start | bytes 884744 | tf_op jit(solution)/shard_map/ppermute | solution.py:27
  18.7 10.1 %collective-permute-start.4 = (bf16[16,192]{1,0:T(8,128)(2,1)S(1)}, bf16[16,192]{1,0:T(8,128)(2,1)S(1)}, u32[]{:S(2)}, u32[]{:S(2)}) collective-permute-start(bf16[16,192]{1,0:T(8,128)(2,1)S(1)} %get-tuple-element.320), channel_id=1, source_target_pairs={{0,1},{1,0},{2,3},{3,2},{4,5},{5,4},{6,7},{7,6},{8,9},{9,8},{10,11... | collective-permute-start | bytes 18440 | tf_op jit(solution)/shard_map/ppermute | solution.py:27
  19.3 15.8 %collective-permute-start.5 = (bf16[16,192]{1,0:T(8,128)(2,1)S(1)}, bf16[16,192]{1,0:T(8,128)(2,1)S(1)}, u32[]{:S(2)}, u32[]{:S(2)}) collective-permute-start(bf16[16,192]{1,0:T(8,128)(2,1)S(1)} %get-tuple-element.320), channel_id=1, source_target_pairs={{0,2},{1,3},{2,0},{3,1},{4,6},{5,7},{6,4},{7,5},{8,10},{9,11},{10,... | collective-permute-start | bytes 18440 | tf_op jit(solution)/shard_map/ppermute | solution.py:27
  21.0 14.6 %collective-permute-start.6 = (bf16[16,192]{1,0:T(8,128)(2,1)S(1)}, bf16[16,192]{1,0:T(8,128)(2,1)S(1)}, u32[]{:S(2)}, u32[]{:S(2)}) collective-permute-start(bf16[16,192]{1,0:T(8,128)(2,1)S(1)} %get-tuple-element.320), channel_id=1, source_target_pairs={{0,3},{1,2},{2,1},{3,0},{4,7},{5,6},{6,5},{7,4},{8,11},{9,10},{10,... | collective-permute-start | bytes 18440 | tf_op jit(solution)/shard_map/ppermute | solution.py:27
  24.7 10.9 %copy-start.80 = (bf16[192,768]{1,0:T(8,128)(2,1)}, bf16[192,768]{1,0:T(8,128)(2,1)S(1)}, u32[]{:S(2)}) copy-start(bf16[192,768]{1,0:T(8,128)(2,1)S(1)} %collective-permute-done.1) | copy-start | bytes 884740
  25.8 10.5 %collective-permute-start.3 = (bf16[192,768]{1,0:T(8,128)(2,1)}, bf16[192,768]{1,0:T(8,128)(2,1)}, u32[]{:S(2)}, u32[]{:S(2)}) collective-permute-start(bf16[192,768]{1,0:T(8,128)(2,1)} %collective-permute-done.2), channel_id=1, source_target_pairs={{0,4},{4,0},{8,12},{12,8},{16,20},{20,16},{24,28},{28,24},{1,5},{5... | collective-permute-start | bytes 884744 | tf_op jit(solution)/shard_map/ppermute | solution.py:27
  26.3 13.0 %copy-start.11 = (bf16[768,768]{1,0:T(8,128)(2,1)}, bf16[768,768]{1,0:T(8,128)(2,1)S(1)}, u32[]{:S(2)}) copy-start(bf16[768,768]{1,0:T(8,128)(2,1)S(1)} %pad_maximum_fusion.2.refs_3_.refs_8_) | copy-start | bytes 3538948
  26.3 18.7 %collective-permute-start.7 = (bf16[768,768]{1,0:T(8,128)(2,1)S(1)}, bf16[768,768]{1,0:T(8,128)(2,1)}, u32[]{:S(2)}, u32[]{:S(2)}) collective-permute-start(bf16[768,768]{1,0:T(8,128)(2,1)S(1)} %pad_maximum_fusion.2.refs_3_.refs_8_), channel_id=1, source_target_pairs={{0,1},{1,0},{2,3},{3,2},{4,5},{5,4},{6,7},{7,6},{8,9},{9,8},{10,11... | collective-permute-start | bytes 3538952 | tf_op jit(solution)/shard_map/ppermute | solution.py:27
  39.2 5.8 %collective-permute-start.8 = (bf16[768,768]{1,0:T(8,128)(2,1)}, bf16[768,768]{1,0:T(8,128)(2,1)}, u32[]{:S(2)}, u32[]{:S(2)}) collective-permute-start(bf16[768,768]{1,0:T(8,128)(2,1)} %pad_maximum_fusion.3.refs_5_.refs_10_), channel_id=1, source_target_pairs={{0,1},{1,0},{2,3},{3,2},{4,5},{5,4},{6,7},{7,6},{8,9},{9,8},{10,11... | collective-permute-start | bytes 3538952 | tf_op jit(solution)/shard_map/ppermute | solution.py:27
  41.6 18.5 %collective-permute-start.9 = (bf16[384,768]{1,0:T(8,128)(2,1)}, bf16[384,768]{1,0:T(8,128)(2,1)}, u32[]{:S(2)}, u32[]{:S(2)}) collective-permute-start(bf16[384,768]{1,0:T(8,128)(2,1)} %constant_dynamic-slice_fusion.3), channel_id=1, source_target_pairs={{0,2},{1,3},{2,0},{3,1},{4,6},{5,7},{6,4},{7,5},{8,10},{9,11},{10,... | collective-permute-start | bytes 1769480 | tf_op jit(solution)/shard_map/ppermute | solution.py:27
  41.6 48.9 %collective-permute-start.13 = (bf16[1536,768]{1,0:T(8,128)(2,1)}, bf16[1536,768]{1,0:T(8,128)(2,1)}, u32[]{:S(2)}, u32[]{:S(2)}) collective-permute-start(bf16[1536,768]{1,0:T(8,128)(2,1)} %copy-done.35), channel_id=1, source_target_pairs={{0,1},{1,0},{2,3},{3,2},{4,5},{5,4},{6,7},{7,6},{8,9},{9,8},{10,11... | collective-permute-start | bytes 7077896 | tf_op jit(solution)/shard_map/ppermute | solution.py:27
  60.1 29.6 %all-to-all-start.1 = ((bf16[4,192,1024]{2,1,0:T(8,128)(2,1)}), bf16[4,192,1024]{2,1,0:T(8,128)(2,1)}, u32[]{:S(2)}, u32[]{:S(2)}) async-start(bf16[4,192,1024]{2,1,0:T(8,128)(2,1)} %bitcast.183), calls=%async_computation.1 | async-start | bytes 3145728 | tf_op jit(solution)/shard_map/all_to_all | solution.py:536
  65.3 2.8 collective-permute-start.10
  65.3 23.4 %collective-permute-start.11 = (bf16[384,768]{1,0:T(8,128)(2,1)}, bf16[384,768]{1,0:T(8,128)(2,1)S(1)}, u32[]{:S(2)}, u32[]{:S(2)}) collective-permute-start(bf16[384,768]{1,0:T(8,128)(2,1)} %collective-permute-done.9), channel_id=1, source_target_pairs={{0,4},{4,0},{8,12},{12,8},{16,20},{20,16},{24,28},{28,24},{1,5},{5... | collective-permute-start | bytes 1769480 | tf_op jit(solution)/shard_map/ppermute | solution.py:27
  66.7 22.9 %collective-permute-start.12 = (bf16[384,768]{1,0:T(8,128)(2,1)}, bf16[384,768]{1,0:T(8,128)(2,1)}, u32[]{:S(2)}, u32[]{:S(2)}) collective-permute-start(bf16[384,768]{1,0:T(8,128)(2,1)} %collective-permute-done.9), channel_id=1, source_target_pairs={{0,8},{4,12},{8,0},{12,4},{16,24},{20,28},{24,16},{28,20},{1,9},{5... | collective-permute-start | bytes 1769480 | tf_op jit(solution)/shard_map/ppermute | solution.py:27
  68.0 11.7 %copy-start.14 = (bf16[272,1536]{1,0:T(8,128)(2,1)}, bf16[272,1536]{1,0:T(8,128)(2,1)S(1)}, u32[]{:S(2)}) copy-start(bf16[272,1536]{1,0:T(8,128)(2,1)S(1)} %collective-permute-done.10.refs_3_.refs_6_) | copy-start | bytes 2506756
  89.6 14.0 %collective-permute-start.14 = (bf16[384,768]{1,0:T(8,128)(2,1)}, bf16[384,768]{1,0:T(8,128)(2,1)S(1)}, u32[]{:S(2)}, u32[]{:S(2)}) collective-permute-start(bf16[384,768]{1,0:T(8,128)(2,1)} %collective-permute-done.12), channel_id=1, source_target_pairs={{0,4},{4,0},{8,12},{12,8},{16,20},{20,16},{24,28},{28,24},{1,5},{5... | collective-permute-start | bytes 1769480 | tf_op jit(solution)/shard_map/ppermute | solution.py:27
  92.0 11.7 %copy-start.79 = (bf16[384,768]{1,0:T(8,128)(2,1)S(1)}, bf16[384,768]{1,0:T(8,128)(2,1)}, u32[]{:S(2)}) copy-start(bf16[384,768]{1,0:T(8,128)(2,1)} %copy-done.78) | copy-start | bytes 1769476
  105.3 6.1 %collective-permute-start.15 = (bf16[1536,768]{1,0:T(8,128)(2,1)S(1)}, bf16[1536,768]{1,0:T(8,128)(2,1)S(1)}, u32[]{:S(2)}, u32[]{:S(2)}) collective-permute-start(bf16[1536,768]{1,0:T(8,128)(2,1)S(1)} %pad_maximum_fusion.refs_4_), channel_id=1, source_target_pairs={{0,1},{1,0},{2,3},{3,2},{4,5},{5,4},{6,7},{7,6},{8,9},{9,8},{10,11... | collective-permute-start | bytes 7077896 | tf_op jit(solution)/shard_map/ppermute | solution.py:27
  108.6 16.2 %collective-permute-start.16 = (bf16[1536,768]{1,0:T(8,128)(2,1)}, bf16[1536,768]{1,0:T(8,128)(2,1)}, u32[]{:S(2)}, u32[]{:S(2)}) collective-permute-start(bf16[1536,768]{1,0:T(8,128)(2,1)} %get-tuple-element.174), channel_id=1, source_target_pairs={{0,1},{1,0},{2,3},{3,2},{4,5},{5,4},{6,7},{7,6},{8,9},{9,8},{10,11... | collective-permute-start | bytes 7077896 | tf_op jit(solution)/shard_map/ppermute | solution.py:27
  124.4 21.5 %collective-permute-start.18 = (bf16[1536,768]{1,0:T(8,128)(2,1)}, bf16[1536,768]{1,0:T(8,128)(2,1)}, u32[]{:S(2)}, u32[]{:S(2)}) collective-permute-start(bf16[1536,768]{1,0:T(8,128)(2,1)} %get-tuple-element.180), channel_id=1, source_target_pairs={{0,1},{1,0},{2,3},{3,2},{4,5},{5,4},{6,7},{7,6},{8,9},{9,8},{10,11... | collective-permute-start | bytes 7077896 | tf_op jit(solution)/shard_map/ppermute | solution.py:27
  133.1 12.9 %copy-start.19 = (f32[1024,768]{1,0:T(8,128)S(1)}, f32[1024,768]{1,0:T(8,128)}, u32[]{:S(2)}) copy-start(f32[1024,768]{1,0:T(8,128)} %copy-done.18) | copy-start | bytes 9437188
  133.1 12.9 %copy-start.28 = (bf16[1024,768]{1,0:T(8,128)(2,1)S(1)}, bf16[1024,768]{1,0:T(8,128)(2,1)}, u32[]{:S(2)}) copy-start(bf16[1024,768]{1,0:T(8,128)(2,1)} %copy-done.26) | copy-start | bytes 4718596
  133.1 12.9 %copy-start.49 = (bf16[1024,768]{1,0:T(8,128)(2,1)S(1)}, bf16[1024,768]{1,0:T(8,128)(2,1)}, u32[]{:S(2)}) copy-start(bf16[1024,768]{1,0:T(8,128)(2,1)} %copy-done.45) | copy-start | bytes 4718596
  145.0 50.3 %collective-permute-start.17 = (bf16[2,384,768]{2,1,0:T(8,128)(2,1)}, bf16[2,384,768]{2,1,0:T(8,128)(2,1)}, u32[]{:S(2)}, u32[]{:S(2)}) collective-permute-start(bf16[2,384,768]{2,1,0:T(8,128)(2,1)} %constant_dynamic-slice_fusion.2), channel_id=1, source_target_pairs={{0,4},{4,0},{8,12},{12,8},{16,20},{20,16},{24,28},{28,24},{1,5},{5... | collective-permute-start | bytes 3538952 | tf_op jit(solution)/shard_map/ppermute | solution.py:27
  146.9 10.8 %copy-start.4 = (bf16[1024,768]{1,0:T(8,128)(2,1)S(1)}, bf16[1024,768]{1,0:T(8,128)(2,1)}, u32[]{:S(2)}) copy-start(bf16[1024,768]{1,0:T(8,128)(2,1)} %copy-done.2) | copy-start | bytes 4718596
  146.9 10.8 %copy-start.17 = (f32[1024,768]{1,0:T(8,128)S(1)}, f32[1024,768]{1,0:T(8,128)}, u32[]{:S(2)}) copy-start(f32[1024,768]{1,0:T(8,128)} %copy-done.16) | copy-start | bytes 9437188
  146.9 10.8 %copy-start.25 = (bf16[1024,768]{1,0:T(8,128)(2,1)S(1)}, bf16[1024,768]{1,0:T(8,128)(2,1)}, u32[]{:S(2)}) copy-start(bf16[1024,768]{1,0:T(8,128)(2,1)} %copy-done.24) | copy-start | bytes 4718596
  146.9 10.8 %copy-start.38 = (bf16[768,768]{1,0:T(8,128)(2,1)S(1)}, bf16[768,768]{1,0:T(8,128)(2,1)}, u32[]{:S(2)}) copy-start(bf16[768,768]{1,0:T(8,128)(2,1)} %copy-done.37) | copy-start | bytes 3538948
  169.8 4.5 %collective-permute-start.21 = (bf16[272,1536]{1,0:T(8,128)(2,1)}, bf16[272,1536]{1,0:T(8,128)(2,1)}, u32[]{:S(2)}, u32[]{:S(2)}) collective-permute-start(bf16[272,1536]{1,0:T(8,128)(2,1)} %maximum_maximum_fusion.1), channel_id=1, source_target_pairs={{0,1},{1,0},{2,3},{3,2},{4,5},{5,4},{6,7},{7,6},{8,9},{9,8},{10,11... | collective-permute-start | bytes 2506760 | tf_op jit(solution)/shard_map/ppermute | solution.py:27
  171.1 27.9 %collective-permute-start.19 = (bf16[1,768,768]{2,1,0:T(8,128)(2,1)}, bf16[1,768,768]{2,1,0:T(8,128)(2,1)}, u32[]{:S(2)}, u32[]{:S(2)}) collective-permute-start(bf16[1,768,768]{2,1,0:T(8,128)(2,1)} %get-tuple-element.284), channel_id=1, source_target_pairs={{0,2},{1,3},{2,0},{3,1},{4,6},{5,7},{6,4},{7,5},{8,10},{9,11},{10,... | collective-permute-start | bytes 3538952 | tf_op jit(solution)/shard_map/ppermute | solution.py:27
  173.6 21.7 %collective-permute-start.20 = (bf16[1,384,768]{2,1,0:T(8,128)(2,1)}, bf16[1,384,768]{2,1,0:T(8,128)(2,1)}, u32[]{:S(2)}, u32[]{:S(2)}) collective-permute-start(bf16[1,384,768]{2,1,0:T(8,128)(2,1)} %dynamic-slice_bitcast_fusion.1), channel_id=1, source_target_pairs={{0,4},{4,0},{8,12},{12,8},{16,20},{20,16},{24,28},{28,24},{1,5},{5... | collective-permute-start | bytes 1769480 | tf_op jit(solution)/shard_map/ppermute | solution.py:27
  187.2 11.8 %collective-permute-start.22 = (bf16[2,256,512]{2,1,0:T(8,128)(2,1)S(1)}, bf16[2,256,512]{2,1,0:T(8,128)(2,1)S(1)}, u32[]{:S(2)}, u32[]{:S(2)}) collective-permute-start(bf16[2,256,512]{2,1,0:T(8,128)(2,1)S(1)} %slice.208), channel_id=1, source_target_pairs={{0,1},{1,0},{2,3},{3,2},{4,5},{5,4},{6,7},{7,6},{8,9},{9,8},{10,11... | collective-permute-start | bytes 1572872 | tf_op jit(solution)/shard_map/ppermute | solution.py:27
  188.3 12.2 %copy-start.63 = (bf16[768,768]{1,0:T(8,128)(2,1)S(1)}, bf16[768,768]{1,0:T(8,128)(2,1)}, u32[]{:S(2)}) copy-start(bf16[768,768]{1,0:T(8,128)(2,1)} %copy-done.62) | copy-start | bytes 3538948
  188.3 15.8 %copy-start.55 = (bf16[3,768,768]{2,1,0:T(8,128)(2,1)S(1)}, bf16[3,768,768]{2,1,0:T(8,128)(2,1)}, u32[]{:S(2)}) copy-start(bf16[3,768,768]{2,1,0:T(8,128)(2,1)} %copy-done.54) | copy-start | bytes 10616836
  195.3 16.7 %collective-permute-start.25 = (bf16[2,768,768]{2,1,0:T(8,128)(2,1)S(1)}, bf16[2,768,768]{2,1,0:T(8,128)(2,1)S(1)}, u32[]{:S(2)}, u32[]{:S(2)}) collective-permute-start(bf16[2,768,768]{2,1,0:T(8,128)(2,1)S(1)} %get-tuple-element.210), channel_id=1, source_target_pairs={{0,1},{1,0},{2,3},{3,2},{4,5},{5,4},{6,7},{7,6},{8,9},{9,8},{10,11... | collective-permute-start | bytes 7077896 | tf_op jit(solution)/shard_map/ppermute | solution.py:27
  199.2 14.5 %collective-permute-start.26 = (bf16[1,256,512]{2,1,0:T(8,128)(2,1)S(1)}, bf16[1,256,512]{2,1,0:T(8,128)(2,1)S(1)}, u32[]{:S(2)}, u32[]{:S(2)}) collective-permute-start(bf16[1,256,512]{2,1,0:T(8,128)(2,1)S(1)} %slice.264), channel_id=1, source_target_pairs={{0,2},{1,3},{2,0},{3,1},{4,6},{5,7},{6,4},{7,5},{8,10},{9,11},{10,... | collective-permute-start | bytes 786440 | tf_op jit(solution)/shard_map/ppermute | solution.py:27
  201.9 16.9 %collective-permute-start.24 = (bf16[1,384,768]{2,1,0:T(8,128)(2,1)S(1)}, bf16[1,384,768]{2,1,0:T(8,128)(2,1)S(1)}, u32[]{:S(2)}, u32[]{:S(2)}) collective-permute-start(bf16[1,384,768]{2,1,0:T(8,128)(2,1)S(1)} %fusion.5), channel_id=1, source_target_pairs={{0,2},{1,3},{2,0},{3,1},{4,6},{5,7},{6,4},{7,5},{8,10},{9,11},{10,... | collective-permute-start | bytes 1769480 | tf_op jit(solution)/shard_map/ppermute | solution.py:27
  203.6 15.2 %collective-permute-start.23 = (bf16[1,384,768]{2,1,0:T(8,128)(2,1)S(1)}, bf16[1,384,768]{2,1,0:T(8,128)(2,1)S(1)}, u32[]{:S(2)}, u32[]{:S(2)}) collective-permute-start(bf16[1,384,768]{2,1,0:T(8,128)(2,1)S(1)} %constant_dynamic-slice_fusion), channel_id=1, source_target_pairs={{0,4},{4,0},{8,12},{12,8},{16,20},{20,16},{24,28},{28,24},{1,5},{5... | collective-permute-start | bytes 1769480 | tf_op jit(solution)/shard_map/ppermute | solution.py:27
  221.4 32.5 %all-to-all-start.2 = ((bf16[4,2,96,768]{3,2,1,0:T(8,128)(2,1)}), bf16[4,2,96,768]{3,2,1,0:T(8,128)(2,1)}, u32[]{:S(2)}, u32[]{:S(2)}) async-start(bf16[4,2,96,768]{3,2,1,0:T(8,128)(2,1)} %bitcast.184), calls=%async_computation.2 | async-start | bytes 2359296 | tf_op jit(solution)/shard_map/all_to_all | solution.py:636
  225.9 31.8 %collective-permute-start.27 = (bf16[768,768]{1,0:T(8,128)(2,1)}, bf16[768,768]{1,0:T(8,128)(2,1)}, u32[]{:S(2)}, u32[]{:S(2)}) collective-permute-start(bf16[768,768]{1,0:T(8,128)(2,1)} %fusion.1), channel_id=1, source_target_pairs={{0,2},{1,3},{2,0},{3,1},{4,6},{5,7},{6,4},{7,5},{8,10},{9,11},{10,... | collective-permute-start | bytes 3538952 | tf_op jit(solution)/shard_map/ppermute | solution.py:27
  229.0 28.7 %copy-start.40 = (bf16[768,768]{1,0:T(8,128)(2,1)S(1)}, bf16[768,768]{1,0:T(8,128)(2,1)}, u32[]{:S(2)}) copy-start(bf16[768,768]{1,0:T(8,128)(2,1)} %copy-done.39) | copy-start | bytes 3538948
  229.0 28.7 %collective-permute-start.28 = (bf16[2,192,1024]{2,1,0:T(8,128)(2,1)}, bf16[2,192,1024]{2,1,0:T(8,128)(2,1)}, u32[]{:S(2)}, u32[]{:S(2)}) collective-permute-start(bf16[2,192,1024]{2,1,0:T(8,128)(2,1)} %pad_maximum_fusion.7), channel_id=1, source_target_pairs={{0,1},{1,0},{2,3},{3,2},{4,5},{5,4},{6,7},{7,6},{8,9},{9,8},{10,11... | collective-permute-start | bytes 2359304 | tf_op jit(solution)/shard_map/ppermute | solution.py:27
  254.0 17.2 %all-to-all-start.3 = ((bf16[8,48,512]{2,1,0:T(8,128)(2,1)}), bf16[8,48,512]{2,1,0:T(8,128)(2,1)S(1)}, u32[]{:S(2)}, u32[]{:S(2)}) async-start(bf16[8,48,512]{2,1,0:T(8,128)(2,1)} %bitcast.195), calls=%async_computation.3 | async-start | bytes 786432 | tf_op jit(solution)/shard_map/all_to_all | solution.py:667
  260.6 16.6 %collective-permute-start.33 = (bf16[1,384,768]{2,1,0:T(8,128)(2,1)}, bf16[1,384,768]{2,1,0:T(8,128)(2,1)}, u32[]{:S(2)}, u32[]{:S(2)}) collective-permute-start(bf16[1,384,768]{2,1,0:T(8,128)(2,1)} %dynamic-slice_bitcast_fusion), channel_id=1, source_target_pairs={{0,4},{4,0},{8,12},{12,8},{16,20},{20,16},{24,28},{28,24},{1,5},{5... | collective-permute-start | bytes 1769480 | tf_op jit(solution)/shard_map/ppermute | solution.py:27
  264.0 24.3 %collective-permute-start.32 = (bf16[2,192,1024]{2,1,0:T(8,128)(2,1)}, bf16[2,192,1024]{2,1,0:T(8,128)(2,1)}, u32[]{:S(2)}, u32[]{:S(2)}) collective-permute-start(bf16[2,192,1024]{2,1,0:T(8,128)(2,1)} %pad_maximum_fusion.8), channel_id=1, source_target_pairs={{0,2},{1,3},{2,0},{3,1},{4,6},{5,7},{6,4},{7,5},{8,10},{9,11},{10,... | collective-permute-start | bytes 2359304 | tf_op jit(solution)/shard_map/ppermute | solution.py:27
  266.0 11.1 %copy-start.65 = (bf16[768,768]{1,0:T(8,128)(2,1)S(1)}, bf16[768,768]{1,0:T(8,128)(2,1)}, u32[]{:S(2)}) copy-start(bf16[768,768]{1,0:T(8,128)(2,1)} %copy-done.64) | copy-start | bytes 3538948
  267.5 15.9 %copy-start.71 = (bf16[1,192,1024]{2,1,0:T(8,128)(2,1)S(1)}, bf16[1,192,1024]{2,1,0:T(8,128)(2,1)}, u32[]{:S(2)}) copy-start(bf16[1,192,1024]{2,1,0:T(8,128)(2,1)} %get-tuple-element.294) | copy-start | bytes 1179652
  267.5 18.3 %collective-permute-start.29 = (bf16[2,96,768]{2,1,0:T(8,128)(2,1)S(1)}, bf16[2,96,768]{2,1,0:T(8,128)(2,1)}, u32[]{:S(2)}, u32[]{:S(2)}) collective-permute-start(bf16[2,96,768]{2,1,0:T(8,128)(2,1)S(1)} %fusion.8), channel_id=1, source_target_pairs={{0,8},{4,12},{8,0},{12,4},{16,24},{20,28},{24,16},{28,20},{1,9},{5... | collective-permute-start | bytes 884744 | tf_op jit(solution)/shard_map/ppermute | solution.py:27
  268.8 17.1 %collective-permute-start.30 = (bf16[2,96,768]{2,1,0:T(8,128)(2,1)S(1)}, bf16[2,96,768]{2,1,0:T(8,128)(2,1)}, u32[]{:S(2)}, u32[]{:S(2)}) collective-permute-start(bf16[2,96,768]{2,1,0:T(8,128)(2,1)S(1)} %fusion.8), channel_id=1, source_target_pairs={{0,16},{4,20},{8,24},{12,28},{16,0},{20,4},{24,8},{28,12},{1,17},{... | collective-permute-start | bytes 884744 | tf_op jit(solution)/shard_map/ppermute | solution.py:27
  270.9 17.4 %collective-permute-start.31 = (bf16[2,96,768]{2,1,0:T(8,128)(2,1)S(1)}, bf16[2,96,768]{2,1,0:T(8,128)(2,1)}, u32[]{:S(2)}, u32[]{:S(2)}) collective-permute-start(bf16[2,96,768]{2,1,0:T(8,128)(2,1)S(1)} %fusion.8), channel_id=1, source_target_pairs={{0,24},{4,28},{8,16},{12,20},{16,8},{20,12},{24,0},{28,4},{1,25},{... | collective-permute-start | bytes 884744 | tf_op jit(solution)/shard_map/ppermute | solution.py:27
  279.2 27.8 %all-to-all-start.4 = ((bf16[4,1,96,768]{3,2,1,0:T(8,128)(2,1)}), bf16[4,1,96,768]{3,2,1,0:T(8,128)(2,1)S(1)}, u32[]{:S(2)}, u32[]{:S(2)}) async-start(bf16[4,1,96,768]{3,2,1,0:T(8,128)(2,1)} %bitcast.33), calls=%async_computation.4 | async-start | bytes 1179648 | tf_op jit(solution)/shard_map/all_to_all | solution.py:636
  284.4 5.7 %collective-permute-start.35 = (bf16[2,192,1024]{2,1,0:T(8,128)(2,1)}, bf16[2,192,1024]{2,1,0:T(8,128)(2,1)}, u32[]{:S(2)}, u32[]{:S(2)}) collective-permute-start(bf16[2,192,1024]{2,1,0:T(8,128)(2,1)} %pad_maximum_fusion.9), channel_id=1, source_target_pairs={{0,1},{1,0},{2,3},{3,2},{4,5},{5,4},{6,7},{7,6},{8,9},{9,8},{10,11... | collective-permute-start | bytes 2359304 | tf_op jit(solution)/shard_map/ppermute | solution.py:27
  289.7 22.0 %copy-start.74 = (bf16[192,1024]{1,0:T(8,128)(2,1)S(1)}, bf16[192,1024]{1,0:T(8,128)(2,1)}, u32[]{:S(2)}) copy-start(bf16[192,1024]{1,0:T(8,128)(2,1)} %get-tuple-element.269) | copy-start | bytes 1179652
  289.7 26.3 %collective-permute-start.34 = (bf16[2,384,768]{2,1,0:T(8,128)(2,1)S(1)}, bf16[2,384,768]{2,1,0:T(8,128)(2,1)}, u32[]{:S(2)}, u32[]{:S(2)}) collective-permute-start(bf16[2,384,768]{2,1,0:T(8,128)(2,1)S(1)} %pad_maximum_fusion.5), channel_id=1, source_target_pairs={{0,4},{4,0},{8,12},{12,8},{16,20},{20,16},{24,28},{28,24},{1,5},{5... | collective-permute-start | bytes 3538952 | tf_op jit(solution)/shard_map/ppermute | solution.py:27
  307.9 15.8 %all-to-all-start.5 = ((bf16[4,1,96,768]{3,2,1,0:T(8,128)(2,1)}), bf16[4,1,96,768]{3,2,1,0:T(8,128)(2,1)S(1)}, u32[]{:S(2)}, u32[]{:S(2)}) async-start(bf16[4,1,96,768]{3,2,1,0:T(8,128)(2,1)} %broadcast_in_dim.7), calls=%async_computation.5 | async-start | bytes 1179648 | tf_op jit(solution)/shard_map/all_to_all | solution.py:654
  314.3 20.6 %collective-permute-start.37 = (bf16[2,192,1024]{2,1,0:T(8,128)(2,1)S(1)}, bf16[2,192,1024]{2,1,0:T(8,128)(2,1)}, u32[]{:S(2)}, u32[]{:S(2)}) collective-permute-start(bf16[2,192,1024]{2,1,0:T(8,128)(2,1)S(1)} %pad_maximum_fusion.10), channel_id=1, source_target_pairs={{0,2},{1,3},{2,0},{3,1},{4,6},{5,7},{6,4},{7,5},{8,10},{9,11},{10,... | collective-permute-start | bytes 2359304 | tf_op jit(solution)/shard_map/ppermute | solution.py:27
  324.5 13.1 %all-to-all-start.6 = ((bf16[8,48,512]{2,1,0:T(8,128)(2,1)}), bf16[8,48,512]{2,1,0:T(8,128)(2,1)S(1)}, u32[]{:S(2)}, u32[]{:S(2)}) async-start(bf16[8,48,512]{2,1,0:T(8,128)(2,1)} %broadcast_in_dim.8), calls=%async_computation.6 | async-start | bytes 786432 | tf_op jit(solution)/shard_map/all_to_all | solution.py:679
  333.5 14.1 %collective-permute-start.36 = (bf16[1,384,768]{2,1,0:T(8,128)(2,1)S(1)}, bf16[1,384,768]{2,1,0:T(8,128)(2,1)S(1)}, u32[]{:S(2)}, u32[]{:S(2)}) collective-permute-start(bf16[1,384,768]{2,1,0:T(8,128)(2,1)S(1)} %bitcast.191), channel_id=1, source_target_pairs={{0,4},{4,0},{8,12},{12,8},{16,20},{20,16},{24,28},{28,24},{1,5},{5... | collective-permute-start | bytes 1769480 | tf_op jit(solution)/shard_map/ppermute | solution.py:27
  337.5 10.0 %collective-permute-start.38 = (bf16[384,512]{1,0:T(8,128)(2,1)S(1)}, bf16[384,512]{1,0:T(8,128)(2,1)S(1)}, u32[]{:S(2)}, u32[]{:S(2)}) collective-permute-start(bf16[384,512]{1,0:T(8,128)(2,1)S(1)} %bitcast.189), channel_id=1, source_target_pairs={{0,2},{1,3},{2,0},{3,1},{4,6},{5,7},{6,4},{7,5},{8,10},{9,11},{10,... | collective-permute-start | bytes 1179656 | tf_op jit(solution)/shard_map/ppermute | solution.py:27
  347.6 6.8 %collective-permute-start.39 = (bf16[2,384,512]{2,1,0:T(8,128)(2,1)S(1)}, bf16[2,384,512]{2,1,0:T(8,128)(2,1)S(1)}, u32[]{:S(2)}, u32[]{:S(2)}) collective-permute-start(bf16[2,384,512]{2,1,0:T(8,128)(2,1)S(1)} %pad_maximum_fusion.11), channel_id=1, source_target_pairs={{0,1},{1,0},{2,3},{3,2},{4,5},{5,4},{6,7},{7,6},{8,9},{9,8},{10,11... | collective-permute-start | bytes 2359304 | tf_op jit(solution)/shard_map/ppermute | solution.py:27
  (73 other events, 252.7 us)

commit v4 on v3

--- a/solution.py
+++ b/solution.py
@@ -19,6 +19,7 @@
 MIB = 1024 * 1024
 RB = 512
 INPUT_COST = 72
+CUT = 512
 WINDOW_COST = 1000
 
 
@@ -775,29 +776,36 @@
         info, normed_two, cot, up_shift[3:4], feed_both, (total, into), tokens=[tok]
     )
     got_3 = flip(grad_3, "chan", 1)
-    total, into, ups_0, near, tok = feed(
-        info, normed_two, cot, up_shift[0:1], feeding, (total, into), extra=got_1, tokens=[tok]
-    )
-    near = near.reshape(2, D, D)
-    near_x = scatter_start(near, along)
-    layer_t, into, ups_2, far, tok = feed(
+    total, into, ups_2, grad_2, tok = feed(
+        info, normed_two, cot, up_shift[2:3], feed_far, (total, into), tokens=[tok]
+    )
+    far_p = add(grad_2[:CUT], got_3[:CUT]).astype(BF)
+    far_q = add(grad_2[CUT:], got_3[CUT:]).astype(BF)[None]
+    far_py = flip(far_p, "chan", 2)
+    far_qx = scatter_start(far_q, along)
+    layer_t, into, ups_0, near, tok = feed(
         info,
         normed_two,
         cot,
-        up_shift[2:3],
-        feed_far,
+        up_shift[0:1],
+        feeding,
         (total, into),
         (residual, vec),
-        got_3,
+        got_1,
         tokens=[tok],
     )
-    far = far.reshape(2, D, D)
-    far_u, far_d = far[:1], far[1:]
-    far_uy = flip(far_u, "chan", 2)
-    far_dx = scatter_start(far_d, along)
+    own = own_share(along)
+    rest_rows = D - CUT // 2
+    near_qx = flip(
+        lax.dynamic_slice_in_dim(near, CUT + (1 - own) * rest_rows, rest_rows, 0), "dp", along[0]
+    )
     res_grad, branch, q_grad, grads, grad_totals, cols_two, tok = branch_back(
         info, into, residual, cot, vec, out_w, ratio, inverse, gate, tokens=[tok]
     )
+    far_py, far_qx, grad_totals, tok = sync(far_py, far_qx, grad_totals, tok)
+    sum_p = add(near[:CUT], far_py).astype(BF)[None]
+    sum_px = scatter_start(sum_p, along)
+    far_qy = flip(scatter_end(far_q, far_qx, along), "chan", 2)
     grad_halo = message(grads, grad_totals)
     k_grad, v_grad, pair_grad, tok = window_back(
         info, terms, grads, grad_halo, grad_totals, stacked, halo, vals, tokens=[tok]
@@ -808,24 +816,30 @@
         info, q_grad, k_grad, v_grad, mixed, normed_one, branch, cols_two, ups, tokens=[tok]
     )
     got = flip(send, "chan", 1)
-    near_x, far_uy, far_dx, t_got, tok = sync(near_x, far_uy, far_dx, t_got, tok)
+    t_got, tok = sync(t_got, tok)
     t = add(pair_grad[:2], t_got).astype(BF)
     t_near, t_far = t[:1], flip(t[1:], "chan", 2)
-    near = scatter_end(near, near_x, along)
-    far_dy = flip(scatter_end(far_d, far_dx, along), "chan", 2)
-    far_ux = scatter_start(far_uy, along)
     input_t, pack, tok = input_back(
         q_grad, k_grad, v_grad, qkv_t, x_t, vec, res_grad, pack, tokens=[tok]
     )
 
     got, tok = sync(got, tok)
     m_far = add(m_far, got[1]).astype(BF)
-    far_ux, far_dy, m_far, t_far, tok = sync(far_ux, far_dy, m_far, t_far, tok)
+    near_qx, sum_px, far_qy, m_far, t_far, tok = sync(near_qx, sum_px, far_qy, m_far, t_far, tok)
     m_far = flip(m_far, "chan", 2)
-    f_u = add(near[:1], scatter_end(far_uy, far_ux, along)).astype(BF)
-    f_d = add(near[1:], far_dy).astype(BF)
-    f = jnp.concatenate([f_u, f_d], axis=0)
-    f_z = scatter_start(f, across)
+    near_q = lax.dynamic_slice_in_dim(near, CUT + own * rest_rows, rest_rows, 0)
+    f_q = (add(near_q, near_qx) + far_qy[0].astype(F32)).astype(BF)
+    f = jnp.concatenate([scatter_end(sum_p, sum_px, along)[0], f_q], axis=0)
+    f_z = lax.all_to_all(
+        jnp.concatenate(
+            [f[: CUT // 2].reshape(4, -1, D), f[CUT // 2 :].reshape(4, -1, D)], axis=1
+        ),
+        "dp",
+        0,
+        0,
+        axis_index_groups=dp_groups(across),
+        tiled=True,
+    )
     m_near = add(m_near, got[0]).astype(BF)
     half_cols = 2 * WIN
     rest = jnp.pad(pack[:, half_cols:], ((0, 0), (0, half_cols - WIN)))
@@ -839,7 +853,10 @@
     m_far, f_z, layer_near, tok = sync(m_far, f_z, layer_near, tok)
     m = add(m_near, m_far).astype(BF)[None]
     m_x = scatter_start(m, along)
-    f = gather_rest(scatter_rest(scatter_end(f, f_z, across), others), others)
+    f = sum_all(f_z)[None]
+    cut = CUT // 8
+    f_p, f_q = [gather_rest(scatter_rest(v, others), others) for v in (f[:, :cut], f[:, cut:])]
+    f = jnp.concatenate([f_p, f_q], axis=1)[0]
     f_z = [flip(f, "dp", k) for k in across]
     layer_far = exchange_far(layer_parts, layer_near)
     m_x, t_all, f, tok = sync(m_x, t_all, f, tok)
@@ -847,8 +864,9 @@
     m_z = scatter_start(m, across)
     t = sum_all(t_all)
     *f_z, layer_far, m = sync(*f_z, layer_far, m)
-    f = jnp.concatenate(pick([f, *f_z], own_share(across)), axis=1)
-    f_x = gather_start(f, along)
+    pieces = pick([f, *f_z], own_share(across))
+    f = jnp.concatenate([p[:cut] for p in pieces] + [p[cut:] for p in pieces], axis=0)
+    f_x = flip(f, "dp", along[0])
     m_z, t, input_near, f = sync(m_z, t, input_near, f)
     m = gather_rest(scatter_rest(scatter_end(m, m_z, across), others), others)
     m_z = gather_start(m, across)
@@ -856,8 +874,12 @@
     input_far = exchange_far(input_parts, input_near)
     f_x, m, t, layer_out = sync(f_x, m, t, layer_out)
     t_all = gather_all(t)
-    f_u = gather_end(f[:1], f_x[:1], along)[0].astype(F32)
-    f_d = gather_end(f[1:], f_x[1:], along)[0].astype(F32)
+    low, high = jnp.where(own == 1, f_x, f), jnp.where(own == 1, f, f_x)
+    half_cut = CUT // 2
+    f_u = jnp.concatenate(
+        [low[:half_cut], high[:half_cut], low[half_cut : half_cut + D - CUT]], axis=0
+    ).astype(F32)
+    f_d = jnp.concatenate([low[half_cut + D - CUT :], high[half_cut:]], axis=0).astype(F32)
     m_z, f_u, f_d, tok = sync(m_z, f_u, f_d, tok)
     m = gather_end(m, m_z, across)
     m_x = gather_start(m, along)

time: 369 us -> 362 us (0.981)
  waiting for transfers between devices: 91.8 us -> 75 us
  starting transfers between devices: 71.7 us -> 79 us
  other arithmetic: 39.3 us -> 45.4 us
    all_to_all x2 -> x1, waiting for transfers between devices: 38.6 us -> 11.5 us  [scatter_start(): lax.all_to_all(parts, 'dp', 0, 0, axis_index_groups=dp_groups(masks), til...]
    all_to_all x0 -> x1, waiting for transfers between devices: none -> 22.1 us  [body(): lax.all_to_all(jnp.concatenate([f[:CUT // 2].reshape(4, -1, D), f[CUT //...]
    ppermute x40, waiting for transfers between devices: 42.9 us -> 33.5 us  [flip(): return lax.ppermute(values, axis, [(i, i ^ mask) for i in range(size)])]
    all_to_all x1, starting transfers between devices: 4.97 us -> 10.8 us  [gather_all(): return lax.all_to_all(parts, 'dp', 0, 0, tiled=True)]
    convert_element_type x2 -> x5, other arithmetic: 4 us -> 9.37 us  [the longest x1 2.55 us: body(): f_u = jnp.concatenate([low[:half_cut], high[:half_cut], low[half_cut:half...]
    all_to_all x2 -> x1, starting transfers between devices: 8.62 us -> 3.9 us  [scatter_start(): lax.all_to_all(parts, 'dp', 0, 0, axis_index_groups=dp_groups(masks), til...]
    all_to_all x0 -> x1, starting transfers between devices: none -> 4.7 us  [body(): lax.all_to_all(jnp.concatenate([f[:CUT // 2].reshape(4, -1, D), f[CUT //...]
    dynamic_slice x5 -> x4, local copies, waits for them, and re-layouts: 5.84 us -> 2.05 us  [take(): return lax.dynamic_slice_in_dim(values, index * size, size, axis)]
  transfers between devices with their start and end apart: 47 -> 47, of which waited for: 16 -> 14; matrix products, arithmetic and copies ran while one was open for 14% -> 16% of each run, Pallas kernels for 23% -> 20%
where the time goes in v4:
time: 362 us; the launch traced here: 355 us
  Pallas kernels  85.2 us (24%)
  starting transfers between devices  79 us (22%)
  waiting for transfers between devices  75 us (21%)
  local copies, waits for them, and re-layouts  67.4 us (19%)
  other arithmetic  45.4 us (13%)
    pallas_call x12, Pallas kernels, call(): return lambda *operands: run(*operands, *tokens)  85.2 us
    unnamed x192, local copies, waits for them, and re-layouts  51.9 us
    ppermute x40, starting transfers between devices, flip(): return lax.ppermute(values, axis, [(i, i ^ mask) for i in range(size)])  42.6 us
    ppermute x40, waiting for transfers between devices, flip(): return lax.ppermute(values, axis, [(i, i ^ mask) for i in range(size)])  33.5 us
    all_to_all x1, waiting for transfers between devices, body(): lax.all_to_all(jnp.concatenate([f[:CUT // 2].reshape(4, -1, D), f[CUT //...  22.1 us
    all_to_all x1, waiting for transfers between devices, scatter_start(): lax.all_to_all(parts, 'dp', 0, 0, axis_index_groups=dp_groups(masks), til...  11.5 us
    all_to_all x1, starting transfers between devices, gather_all(): return lax.all_to_all(parts, 'dp', 0, 0, tiled=True)  10.8 us
    all_to_all x2, starting transfers between devices, to_rows(): pieces = lax.all_to_all(pieces, 'chan', 0, 0, tiled=True)  9.42 us
  transfers between devices with their start and end apart: 47, of which 14 were waited for; matrix products, arithmetic and copies ran while one was open for 16% of the time, Pallas kernels for 20%

profile of v4, /device:TPU:1, one launch (start us, length us, event | category | flops | bytes accessed | tf_op | source)
XLA Modules:
  0.0 354.8 jit_solution(4779532794872616454)
XLA Ops:
  1.8 2.1 collective-permute-start
  4.0 2.7 copy.41
  6.7 4.0 %collective-permute-done = bf16[192,768]{1,0:T(8,128)(2,1)S(1)} collective-permute-done((bf16[192,768]{1,0:T(8,128)(2,1)S(1)}, bf16[192,768]{1,0:T(8,128)(2,1)S(1)}, u32[]{:S(2)}, u32[]{:S(2)}) %collective-permute-start) | collective-permute-done | bytes 294944 | tf_op jit(solution)/shard_map/ppermute | solution.py:28
  10.8 4.9 %all-to-all-start = ((bf16[4,192,1024]{2,1,0:T(8,128)(2,1)}), bf16[4,192,1024]{2,1,0:T(8,128)(2,1)S(1)}, u32[]{:S(2)}, u32[]{:S(2)}) async-start(bf16[4,192,1024]{2,1,0:T(8,128)(2,1)} %bitcast.170), calls=%async_computation | async-start | bytes 3145728 | tf_op jit(solution)/shard_map/all_to_all | solution.py:537
  15.9 1.5 collective-permute-start.1
  19.3 1.7 collective-permute-start.5
  21.3 3.4 collective-permute-done.1
  28.8 6.3 %collective-permute-done.5 = bf16[16,192]{1,0:T(8,128)(2,1)S(1)} collective-permute-done((bf16[16,192]{1,0:T(8,128)(2,1)S(1)}, bf16[16,192]{1,0:T(8,128)(2,1)S(1)}, u32[]{:S(2)}, u32[]{:S(2)}) %collective-permute-start.5) | collective-permute-done | bytes 6176 | tf_op jit(solution)/shard_map/ppermute | solution.py:28
  36.3 1.8 broadcast_select_fusion.33
  39.7 1.9 constant_dynamic-slice_fusion.2
  42.3 2.7 copy.40
  47.7 7.0 %shard_map.272 = (bf16[1024,768]{1,0:T(8,128)(2,1)S(1)}, bf16[1024,768]{1,0:T(8,128)(2,1)S(1)}, bf16[1024,768]{1,0:T(8,128)(2,1)S(1)}, bf16[1024,1536]{1,0:T(8,1...) custom-call(s32[3]{0:T(128)S(1)} %pad_add_fusion.refs_0_, ...), custom_call_target="tpu_custom_call" | custom-call | flops 3623878656 | bytes 12079595 | tf_op jit(solution)/shard_map/pallas_call | solution.py:83
  57.1 1.8 copy-done.53
  60.1 4.5 %all-to-all-start.1 = ((bf16[4,192,1024]{2,1,0:T(8,128)(2,1)}), bf16[4,192,1024]{2,1,0:T(8,128)(2,1)}, u32[]{:S(2)}, u32[]{:S(2)}) async-start(bf16[4,192,1024]{2,1,0:T(8,128)(2,1)} %bitcast.174), calls=%async_computation.1 | async-start | bytes 3145728 | tf_op jit(solution)/shard_map/all_to_all | solution.py:537
  67.8 1.7 copy-done.3
  72.1 7.3 %shard_map.273 = (bf16[1024,768]{1,0:T(8,128)(2,1)S(1)}, bf16[1024,768]{1,0:T(8,128)(2,1)S(1)}, f32[1024,768]{1,0:T(8,128)S(1)}, bf16[1024,768]{1,0:T(8,128)(2,1...) custom-call(s32[3]{0:T(128)S(1)} %pad_add_fusion.refs_0_, ...), custom_call_target="tpu_custom_call" | custom-call | flops 3623878656 | bytes 12079595 | tf_op jit(solution)/shard_map/pallas_call | solution.py:83
  79.5 1.7 copy-done.16
  81.1 1.7 copy-done.18
  91.7 11.1 %shard_map.274 = (f32[1024,768]{1,0:T(8,128)S(1)}, f32[1024,768]{1,0:T(8,128)S(1)}, f32[1,768]{1,0:T(1,128)S(1)}, bf16[1536,768]{1,0:T(8,128)(2,1)}, bf16[1024,7...) custom-call(s32[3]{0:T(128)S(1)} %pad_add_fusion.refs_0_, bf16[1024,768]{1,0:T(8,128)(2,1)S(1)} %copy-done.47, ...), custom_call_target="tpu_custom_call" | custom-call | flops 7247757312 | bytes 24159192 | tf_op jit(solution)/shard_map/pallas_call | solution.py:83
  103.4 1.4 broadcast_select_fusion.11
  105.0 2.0 collective-permute-start.15
  108.3 2.8 collective-permute-done.15.refs_4_
  111.1 9.6 %shard_map.275 = (f32[1024,768]{1,0:T(8,128)S(1)}, f32[1024,768]{1,0:T(8,128)S(1)}, f32[1,768]{1,0:T(1,128)S(1)}, bf16[1536,768]{1,0:T(8,128)(2,1)}, f32[8,128]{1,0:T(8,128)S(1)}) custom-call(s32[3]{0:T(128)S(1)} %pad_add_fusion.refs_0_, bf16[1024,768]{1,0:T(8,128)(2,1)S(1)} %copy-done.48, bf16[1024,768]{1,0:T(8,128)(2,1)S(1)} %get-tuple-element.166.refs_2_.refs_3_, ...), custom_call_target="tpu_custom_call" | custom-call | flops 7247757312 | bytes 24159192 | tf_op jit(solution)/shard_map/pallas_call | solution.py:83
  120.7 1.6 copy-done.57
  122.4 1.7 copy-done.59
  124.6 1.7 copy-done.21
  129.0 1.9 copy-done.58
  130.9 1.9 copy-done.60
  132.8 9.6 %shard_map.276 = (f32[1024,768]{1,0:T(8,128)S(1)}, f32[1024,768]{1,0:T(8,128)S(1)}, f32[1,768]{1,0:T(1,128)S(1)}, bf16[1536,768]{1,0:T(8,128)(2,1)S(1)}, f32[8,128]{1,0:T(8,128)S(1)}) custom-call(s32[3]{0:T(128)S(1)} %pad_add_fusion.refs_0_, bf16[1024,768]{1,0:T(8,128)(2,1)S(1)} %copy-done.49, bf16[1024,768]{1,0:T(8,128)(2,1)S(1)} %copy-done.26, ...), custom_call_target="tpu_custom_call" | custom-call | flops 7247757312 | bytes 24159192 | tf_op jit(solution)/shard_map/pallas_call | solution.py:83
  142.5 2.0 add_convert_fusion
  145.6 1.8 add_convert_fusion.3
  147.4 1.7 collective-permute-start.19
  149.2 10.8 %shard_map.277 = (bf16[768,1024]{1,0:T(8,128)(2,1)S(1)}, f32[1024,768]{1,0:T(8,128)S(1)}, f32[1,768]{1,0:T(1,128)S(1)}, bf16[1536,768]{1,0:T(8,128)(2,1)S(1)}, f32[8,128]{1,0:T(8,128)S(1)}) custom-call(s32[3]{0:T(128)S(1)} %pad_add_fusion.refs_0_, bf16[1024,768]{1,0:T(8,128)(2,1)S(1)} %copy-done.50, bf16[1024,768]{1,0:T(8,128)(2,1)S(1)} %copy-done.27, ...), custom_call_target="tpu_custom_call" | custom-call | flops 7247757312 | bytes 24159192 | tf_op jit(solution)/shard_map/pallas_call | solution.py:83
  161.4 5.8 %shard_map.278 = (f32[1024,768]{1,0:T(8,128)S(1)}, bf16[1024,768]{1,0:T(8,128)(2,1)S(1)}, bf16[1024,768]{1,0:T(8,128)(2,1)S(1)}, bf16[1024,1536]{1,0:T(8,128)(2,...) custom-call(s32[3]{0:T(128)S(1)} %pad_add_fusion.refs_0_, ...), custom_call_target="tpu_custom_call" | custom-call | flops 1207959552 | bytes 4026531 | tf_op jit(solution)/shard_map/pallas_call | solution.py:83
  167.3 1.7 copy-done.40
  176.4 1.7 fusion.3
  178.2 1.6 add_convert_fusion.2
  181.3 6.7 %shard_map.279 = (bf16[1024,768]{1,0:T(8,128)(2,1)S(1)}, bf16[1024,768]{1,0:T(8,128)(2,1)S(1)}, bf16[4,256,512]{2,1,0:T(8,128)(2,1)S(1)}, f32[8,128]{1,0:T(8,128)S(1)}) custom-call(s32[3]{0:T(128)S(1)} %pad_add_fusion.refs_0_, bf16[1024,768]{1,0:T(8,128)(2,1)S(1)} %copy-done.33, bf16[1024,1536]{1,0:T(8,128)(2,1)S(1)} %copy-done.10, ...), custom_call_target="tpu_custom_call" | custom-call | flops 1000 | bytes 3 | tf_op jit(solution)/shard_map/pallas_call | solution.py:83
  189.4 6.9 %shard_map.280 = (bf16[768,768]{1,0:T(8,128)(2,1)S(1)}, bf16[768,768]{1,0:T(8,128)(2,1)S(1)}, bf16[2,768,768]{2,1,0:T(8,128)(2,1)S(1)}, f32[16,768]{1,0:T(8,128)S(1)}, f32[8,128]{1,0:T(8,128)S(1)}) custom-call(s32[3]{0:T(128)S(1)} %pad_add_fusion.refs_0_, bf16[1024,768]{1,0:T(8,128)(2,1)S(1)} %copy-done.45, ...), custom_call_target="tpu_custom_call" | custom-call | flops 4831838208 | bytes 16106127 | tf_op jit(solution)/shard_map/pallas_call | solution.py:83
  197.1 1.4 collective-permute-start.26
  198.6 6.1 %shard_map.281 = (bf16[768,1024]{1,0:T(8,128)(2,1)S(1)}, f32[16,768]{1,0:T(8,128)S(1)}, f32[8,128]{1,0:T(8,128)S(1)}) custom-call(bf16[1024,768]{1,0:T(8,128)(2,1)S(1)} %copy-done.45, bf16[1024,768]{1,0:T(8,128)(2,1)S(1)} %get-tuple-element.200.refs_2_.refs_1_, bf16[1024,768]{1,0:T(8,128)(2,1)S(1)} %get-tuple-element.201.refs_3_.refs_2_, ...), custom_call_target="tpu_custom_call" | custom-call | flops 43486543872 | bytes 144955152 | tf_op jit(solution)/shard_map/pallas_call | solution.py:83
  204.7 1.5 fusion.1
  209.2 4.7 %all-to-all-start.2 = ((bf16[4,192,768]{2,1,0:T(8,128)(2,1)}), bf16[4,192,768]{2,1,0:T(8,128)(2,1)}, u32[]{:S(2)}, u32[]{:S(2)}) async-start(bf16[4,192,768]{2,1,0:T(8,128)(2,1)} %pad_maximum_fusion.4), calls=%async_computation.2 | async-start | bytes 2359296 | tf_op jit(solution)/shard_map/all_to_all | solution.py:833
  220.0 22.1 %all-to-all-done.2 = bf16[4,192,768]{2,1,0:T(8,128)(2,1)} async-done(((bf16[4,192,768]{2,1,0:T(8,128)(2,1)}), bf16[4,192,768]{2,1,0:T(8,128)(2,1)}, u32[]{:S(2)}, u32[]{:S(2)}) %all-to-all-start.2) | async-done | bytes 1179680 | tf_op jit(solution)/shard_map/all_to_all | solution.py:833
  242.1 3.7 %all-to-all-start.3 = ((bf16[8,48,512]{2,1,0:T(8,128)(2,1)}), bf16[8,48,512]{2,1,0:T(8,128)(2,1)S(1)}, u32[]{:S(2)}, u32[]{:S(2)}) async-start(bf16[8,48,512]{2,1,0:T(8,128)(2,1)} %bitcast.186), calls=%async_computation.3 | async-start | bytes 786432 | tf_op jit(solution)/shard_map/all_to_all | solution.py:668
  245.8 2.0 add_convert_fusion.1
  248.0 1.5 collective-permute-start.33
  253.5 1.5 fusion.8
  256.3 2.1 collective-permute-start.30
  259.6 6.4 %collective-permute-done.33 = bf16[1,384,768]{2,1,0:T(8,128)(2,1)S(1)} collective-permute-done((bf16[1,384,768]{2,1,0:T(8,128)(2,1)S(1)}, bf16[1,384,768]{2,1,0:T(8,128)(2,1)S(1)}, u32[]{:S(2)}, u32[]{:S(2)}) %collective-permute-start.33) | collective-permute-done | bytes 589856 | tf_op jit(solution)/shard_map/ppermute | solution.py:28
  267.6 2.0 fusion.4
  269.6 3.9 %all-to-all-start.4 = ((bf16[4,1,96,768]{3,2,1,0:T(8,128)(2,1)}), bf16[4,1,96,768]{3,2,1,0:T(8,128)(2,1)S(1)}, u32[]{:S(2)}, u32[]{:S(2)}) async-start(bf16[4,1,96,768]{3,2,1,0:T(8,128)(2,1)} %bitcast.34), calls=%async_computation.4 | async-start | bytes 1179648 | tf_op jit(solution)/shard_map/all_to_all | solution.py:637
  273.5 2.4 collective-permute-done.31
  283.0 11.5 %all-to-all-done.4 = bf16[4,1,96,768]{3,2,1,0:T(8,128)(2,1)S(1)} async-done(((bf16[4,1,96,768]{3,2,1,0:T(8,128)(2,1)}), bf16[4,1,96,768]{3,2,1,0:T(8,128)(2,1)S(1)}, u32[]{:S(2)}, u32[]{:S(2)}) %all-to-all-start.4) | async-done | bytes 589856 | tf_op jit(solution)/shard_map/all_to_all | solution.py:637
  295.5 3.9 %all-to-all-start.5 = ((bf16[4,1,96,768]{3,2,1,0:T(8,128)(2,1)}), bf16[4,1,96,768]{3,2,1,0:T(8,128)(2,1)S(1)}, u32[]{:S(2)}, u32[]{:S(2)}) async-start(bf16[4,1,96,768]{3,2,1,0:T(8,128)(2,1)} %broadcast_in_dim.7), calls=%async_computation.5 | async-start | bytes 1179648 | tf_op jit(solution)/shard_map/all_to_all | solution.py:655
  303.5 5.7 %all-to-all-done.5 = bf16[4,1,96,768]{3,2,1,0:T(8,128)(2,1)S(1)} async-done(((bf16[4,1,96,768]{3,2,1,0:T(8,128)(2,1)}), bf16[4,1,96,768]{3,2,1,0:T(8,128)(2,1)S(1)}, u32[]{:S(2)}, u32[]{:S(2)}) %all-to-all-start.5) | async-done | bytes 589856 | tf_op jit(solution)/shard_map/all_to_all | solution.py:655
  310.0 10.8 %all-to-all-start.6 = ((bf16[8,48,512]{2,1,0:T(8,128)(2,1)}), bf16[8,48,512]{2,1,0:T(8,128)(2,1)S(1)}, u32[]{:S(2)}, u32[]{:S(2)}) async-start(bf16[8,48,512]{2,1,0:T(8,128)(2,1)} %broadcast_in_dim.8), calls=%async_computation.6 | async-start | bytes 786432 | tf_op jit(solution)/shard_map/all_to_all | solution.py:680
  320.8 1.8 broadcast_select_fusion
  322.8 2.5 maximum_convert_fusion
  325.4 1.5 collective-permute-start.36
  326.8 2.1 all-to-all-done.6
  332.0 6.0 %collective-permute-done.36 = bf16[1,384,768]{2,1,0:T(8,128)(2,1)S(1)} collective-permute-done((bf16[1,384,768]{2,1,0:T(8,128)(2,1)S(1)}, bf16[1,384,768]{2,1,0:T(8,128)(2,1)S(1)}, u32[]{:S(2)}, u32[]{:S(2)}) %collective-permute-start.36) | collective-permute-done | bytes 589856 | tf_op jit(solution)/shard_map/ppermute | solution.py:28
  338.1 6.9 %collective-permute-start.39 = (bf16[2,384,512]{2,1,0:T(8,128)(2,1)S(1)}, bf16[2,384,512]{2,1,0:T(8,128)(2,1)S(1)}, u32[]{:S(2)}, u32[]{:S(2)}) collective-permute-start(bf16[2,384,512]{2,1,0:T(8,128)(2,1)S(1)} %pad_maximum_fusion.10), channel_id=1, source_target_pairs={{0,1},{1,0},{2,3},{3,2},{4,5},{5,4},{6,7},{7,6},{8,9},{9,8},{10,11... | collective-permute-start | bytes 2359304 | tf_op jit(solution)/shard_map/ppermute | solution.py:28
  349.1 3.5 shard_map.282
  (323 shorter events, 89.5 us)
Async XLA Ops:
  1.8 8.9 %collective-permute-start = (bf16[192,768]{1,0:T(8,128)(2,1)S(1)}, bf16[192,768]{1,0:T(8,128)(2,1)S(1)}, u32[]{:S(2)}, u32[]{:S(2)}) collective-permute-start(bf16[192,768]{1,0:T(8,128)(2,1)S(1)} %fusion.9), channel_id=1, source_target_pairs={{0,2},{1,3},{2,0},{3,1},{4,6},{5,7},{6,4},{7,5},{8,10},{9,11},{10,... | collective-permute-start | bytes 884744 | tf_op jit(solution)/shard_map/ppermute | solution.py:28
  10.8 10.3 %copy-start.74 = (bf16[768,768]{1,0:T(8,128)(2,1)S(1)}, bf16[768,768]{1,0:T(8,128)(2,1)}, u32[]{:S(2)}) copy-start(bf16[768,768]{1,0:T(8,128)(2,1)} %param.26) | copy-start | bytes 3538948
  10.8 25.5 %all-to-all-start = ((bf16[4,192,1024]{2,1,0:T(8,128)(2,1)}), bf16[4,192,1024]{2,1,0:T(8,128)(2,1)S(1)}, u32[]{:S(2)}, u32[]{:S(2)}) async-start(bf16[4,192,1024]{2,1,0:T(8,128)(2,1)} %bitcast.170), calls=%async_computation | async-start | bytes 3145728 | tf_op jit(solution)/shard_map/all_to_all | solution.py:537
  15.9 8.8 %collective-permute-start.1 = (bf16[192,768]{1,0:T(8,128)(2,1)S(1)}, bf16[192,768]{1,0:T(8,128)(2,1)S(1)}, u32[]{:S(2)}, u32[]{:S(2)}) collective-permute-start(bf16[192,768]{1,0:T(8,128)(2,1)S(1)} %collective-permute-done), channel_id=1, source_target_pairs={{0,4},{4,0},{8,12},{12,8},{16,20},{20,16},{24,28},{28,24},{1,5},{5... | collective-permute-start | bytes 884744 | tf_op jit(solution)/shard_map/ppermute | solution.py:28
  17.4 8.4 %collective-permute-start.2 = (bf16[192,768]{1,0:T(8,128)(2,1)S(1)}, bf16[192,768]{1,0:T(8,128)(2,1)}, u32[]{:S(2)}, u32[]{:S(2)}) collective-permute-start(bf16[192,768]{1,0:T(8,128)(2,1)S(1)} %collective-permute-done), channel_id=1, source_target_pairs={{0,8},{4,12},{8,0},{12,4},{16,24},{20,28},{24,16},{28,20},{1,9},{5... | collective-permute-start | bytes 884744 | tf_op jit(solution)/shard_map/ppermute | solution.py:28
  18.7 10.1 %collective-permute-start.4 = (bf16[16,192]{1,0:T(8,128)(2,1)S(1)}, bf16[16,192]{1,0:T(8,128)(2,1)S(1)}, u32[]{:S(2)}, u32[]{:S(2)}) collective-permute-start(bf16[16,192]{1,0:T(8,128)(2,1)S(1)} %get-tuple-element.321), channel_id=1, source_target_pairs={{0,1},{1,0},{2,3},{3,2},{4,5},{5,4},{6,7},{7,6},{8,9},{9,8},{10,11... | collective-permute-start | bytes 18440 | tf_op jit(solution)/shard_map/ppermute | solution.py:28
  19.3 15.8 %collective-permute-start.5 = (bf16[16,192]{1,0:T(8,128)(2,1)S(1)}, bf16[16,192]{1,0:T(8,128)(2,1)S(1)}, u32[]{:S(2)}, u32[]{:S(2)}) collective-permute-start(bf16[16,192]{1,0:T(8,128)(2,1)S(1)} %get-tuple-element.321), channel_id=1, source_target_pairs={{0,2},{1,3},{2,0},{3,1},{4,6},{5,7},{6,4},{7,5},{8,10},{9,11},{10,... | collective-permute-start | bytes 18440 | tf_op jit(solution)/shard_map/ppermute | solution.py:28
  21.0 14.6 %collective-permute-start.6 = (bf16[16,192]{1,0:T(8,128)(2,1)S(1)}, bf16[16,192]{1,0:T(8,128)(2,1)S(1)}, u32[]{:S(2)}, u32[]{:S(2)}) collective-permute-start(bf16[16,192]{1,0:T(8,128)(2,1)S(1)} %get-tuple-element.321), channel_id=1, source_target_pairs={{0,3},{1,2},{2,1},{3,0},{4,7},{5,6},{6,5},{7,4},{8,11},{9,10},{10,... | collective-permute-start | bytes 18440 | tf_op jit(solution)/shard_map/ppermute | solution.py:28
  24.7 10.9 %copy-start.81 = (bf16[192,768]{1,0:T(8,128)(2,1)}, bf16[192,768]{1,0:T(8,128)(2,1)S(1)}, u32[]{:S(2)}) copy-start(bf16[192,768]{1,0:T(8,128)(2,1)S(1)} %collective-permute-done.1) | copy-start | bytes 884740
  25.8 10.5 %collective-permute-start.3 = (bf16[192,768]{1,0:T(8,128)(2,1)}, bf16[192,768]{1,0:T(8,128)(2,1)}, u32[]{:S(2)}, u32[]{:S(2)}) collective-permute-start(bf16[192,768]{1,0:T(8,128)(2,1)} %collective-permute-done.2), channel_id=1, source_target_pairs={{0,4},{4,0},{8,12},{12,8},{16,20},{20,16},{24,28},{28,24},{1,5},{5... | collective-permute-start | bytes 884744 | tf_op jit(solution)/shard_map/ppermute | solution.py:28
  26.3 13.0 %copy-start.11 = (bf16[768,768]{1,0:T(8,128)(2,1)}, bf16[768,768]{1,0:T(8,128)(2,1)S(1)}, u32[]{:S(2)}) copy-start(bf16[768,768]{1,0:T(8,128)(2,1)S(1)} %pad_maximum_fusion.2.refs_3_.refs_8_) | copy-start | bytes 3538948
  26.3 18.8 %collective-permute-start.7 = (bf16[768,768]{1,0:T(8,128)(2,1)S(1)}, bf16[768,768]{1,0:T(8,128)(2,1)}, u32[]{:S(2)}, u32[]{:S(2)}) collective-permute-start(bf16[768,768]{1,0:T(8,128)(2,1)S(1)} %pad_maximum_fusion.2.refs_3_.refs_8_), channel_id=1, source_target_pairs={{0,1},{1,0},{2,3},{3,2},{4,5},{5,4},{6,7},{7,6},{8,9},{9,8},{10,11... | collective-permute-start | bytes 3538952 | tf_op jit(solution)/shard_map/ppermute | solution.py:28
  39.3 5.8 %collective-permute-start.8 = (bf16[768,768]{1,0:T(8,128)(2,1)}, bf16[768,768]{1,0:T(8,128)(2,1)}, u32[]{:S(2)}, u32[]{:S(2)}) collective-permute-start(bf16[768,768]{1,0:T(8,128)(2,1)} %pad_maximum_fusion.3.refs_5_.refs_10_), channel_id=1, source_target_pairs={{0,1},{1,0},{2,3},{3,2},{4,5},{5,4},{6,7},{7,6},{8,9},{9,8},{10,11... | collective-permute-start | bytes 3538952 | tf_op jit(solution)/shard_map/ppermute | solution.py:28
  41.6 18.5 %collective-permute-start.9 = (bf16[384,768]{1,0:T(8,128)(2,1)}, bf16[384,768]{1,0:T(8,128)(2,1)}, u32[]{:S(2)}, u32[]{:S(2)}) collective-permute-start(bf16[384,768]{1,0:T(8,128)(2,1)} %constant_dynamic-slice_fusion.2), channel_id=1, source_target_pairs={{0,2},{1,3},{2,0},{3,1},{4,6},{5,7},{6,4},{7,5},{8,10},{9,11},{10,... | collective-permute-start | bytes 1769480 | tf_op jit(solution)/shard_map/ppermute | solution.py:28
  41.7 48.6 %collective-permute-start.13 = (bf16[1536,768]{1,0:T(8,128)(2,1)}, bf16[1536,768]{1,0:T(8,128)(2,1)}, u32[]{:S(2)}, u32[]{:S(2)}) collective-permute-start(bf16[1536,768]{1,0:T(8,128)(2,1)} %copy-done.34), channel_id=1, source_target_pairs={{0,1},{1,0},{2,3},{3,2},{4,5},{5,4},{6,7},{7,6},{8,9},{9,8},{10,11... | collective-permute-start | bytes 7077896 | tf_op jit(solution)/shard_map/ppermute | solution.py:28
  60.1 29.2 %all-to-all-start.1 = ((bf16[4,192,1024]{2,1,0:T(8,128)(2,1)}), bf16[4,192,1024]{2,1,0:T(8,128)(2,1)}, u32[]{:S(2)}, u32[]{:S(2)}) async-start(bf16[4,192,1024]{2,1,0:T(8,128)(2,1)} %bitcast.174), calls=%async_computation.1 | async-start | bytes 3145728 | tf_op jit(solution)/shard_map/all_to_all | solution.py:537
  64.9 2.8 collective-permute-start.10
  65.0 23.5 %collective-permute-start.11 = (bf16[384,768]{1,0:T(8,128)(2,1)}, bf16[384,768]{1,0:T(8,128)(2,1)S(1)}, u32[]{:S(2)}, u32[]{:S(2)}) collective-permute-start(bf16[384,768]{1,0:T(8,128)(2,1)} %collective-permute-done.9), channel_id=1, source_target_pairs={{0,4},{4,0},{8,12},{12,8},{16,20},{20,16},{24,28},{28,24},{1,5},{5... | collective-permute-start | bytes 1769480 | tf_op jit(solution)/shard_map/ppermute | solution.py:28
  66.4 22.9 %collective-permute-start.12 = (bf16[384,768]{1,0:T(8,128)(2,1)}, bf16[384,768]{1,0:T(8,128)(2,1)}, u32[]{:S(2)}, u32[]{:S(2)}) collective-permute-start(bf16[384,768]{1,0:T(8,128)(2,1)} %collective-permute-done.9), channel_id=1, source_target_pairs={{0,8},{4,12},{8,0},{12,4},{16,24},{20,28},{24,16},{28,20},{1,9},{5... | collective-permute-start | bytes 1769480 | tf_op jit(solution)/shard_map/ppermute | solution.py:28
  67.7 11.7 %copy-start.14 = (bf16[272,1536]{1,0:T(8,128)(2,1)}, bf16[272,1536]{1,0:T(8,128)(2,1)S(1)}, u32[]{:S(2)}) copy-start(bf16[272,1536]{1,0:T(8,128)(2,1)S(1)} %collective-permute-done.10.refs_3_.refs_6_) | copy-start | bytes 2506756
  89.3 14.0 %collective-permute-start.14 = (bf16[384,768]{1,0:T(8,128)(2,1)}, bf16[384,768]{1,0:T(8,128)(2,1)S(1)}, u32[]{:S(2)}, u32[]{:S(2)}) collective-permute-start(bf16[384,768]{1,0:T(8,128)(2,1)} %collective-permute-done.12), channel_id=1, source_target_pairs={{0,4},{4,0},{8,12},{12,8},{16,20},{20,16},{24,28},{28,24},{1,5},{5... | collective-permute-start | bytes 1769480 | tf_op jit(solution)/shard_map/ppermute | solution.py:28
  91.7 11.7 %copy-start.79 = (bf16[384,768]{1,0:T(8,128)(2,1)S(1)}, bf16[384,768]{1,0:T(8,128)(2,1)}, u32[]{:S(2)}) copy-start(bf16[384,768]{1,0:T(8,128)(2,1)} %copy-done.78) | copy-start | bytes 1769476
  102.8 8.4 %copy-start.25 = (bf16[1024,768]{1,0:T(8,128)(2,1)}, bf16[1024,768]{1,0:T(8,128)(2,1)S(1)}, u32[]{:S(2)}) copy-start(bf16[1024,768]{1,0:T(8,128)(2,1)S(1)} %get-tuple-element.166.refs_2_.refs_3_) | copy-start | bytes 4718596
  105.0 6.1 %collective-permute-start.15 = (bf16[1536,768]{1,0:T(8,128)(2,1)S(1)}, bf16[1536,768]{1,0:T(8,128)(2,1)S(1)}, u32[]{:S(2)}, u32[]{:S(2)}) collective-permute-start(bf16[1536,768]{1,0:T(8,128)(2,1)S(1)} %pad_maximum_fusion.refs_4_), channel_id=1, source_target_pairs={{0,1},{1,0},{2,3},{3,2},{4,5},{5,4},{6,7},{7,6},{8,9},{9,8},{10,11... | collective-permute-start | bytes 7077896 | tf_op jit(solution)/shard_map/ppermute | solution.py:28
  124.0 18.4 %collective-permute-start.18 = (bf16[1536,768]{1,0:T(8,128)(2,1)}, bf16[1536,768]{1,0:T(8,128)(2,1)}, u32[]{:S(2)}, u32[]{:S(2)}) collective-permute-start(bf16[1536,768]{1,0:T(8,128)(2,1)} %get-tuple-element.184), channel_id=1, source_target_pairs={{0,1},{1,0},{2,3},{3,2},{4,5},{5,4},{6,7},{7,6},{8,9},{9,8},{10,11... | collective-permute-start | bytes 7077896 | tf_op jit(solution)/shard_map/ppermute | solution.py:28
  124.4 24.7 %collective-permute-start.16 = (bf16[1536,768]{1,0:T(8,128)(2,1)}, bf16[1536,768]{1,0:T(8,128)(2,1)}, u32[]{:S(2)}, u32[]{:S(2)}) collective-permute-start(bf16[1536,768]{1,0:T(8,128)(2,1)} %get-tuple-element.180), channel_id=1, source_target_pairs={{0,1},{1,0},{2,3},{3,2},{4,5},{5,4},{6,7},{7,6},{8,9},{9,8},{10,11... | collective-permute-start | bytes 7077896 | tf_op jit(solution)/shard_map/ppermute | solution.py:28
  144.6 26.7 %collective-permute-start.20 = (bf16[1,512,768]{2,1,0:T(8,128)(2,1)S(1)}, bf16[1,512,768]{2,1,0:T(8,128)(2,1)S(1)}, u32[]{:S(2)}, u32[]{:S(2)}) collective-permute-start(bf16[1,512,768]{2,1,0:T(8,128)(2,1)S(1)} %dynamic-slice_bitcast_fusion), channel_id=1, source_target_pairs={{0,4},{4,0},{8,12},{12,8},{16,20},{20,16},{24,28},{28,24},{1,5},{5... | collective-permute-start | bytes 2359304 | tf_op jit(solution)/shard_map/ppermute | solution.py:28
  147.4 23.9 %collective-permute-start.19 = (bf16[512,768]{1,0:T(8,128)(2,1)S(1)}, bf16[512,768]{1,0:T(8,128)(2,1)S(1)}, u32[]{:S(2)}, u32[]{:S(2)}) collective-permute-start(bf16[512,768]{1,0:T(8,128)(2,1)S(1)} %add_convert_fusion.3), channel_id=1, source_target_pairs={{0,2},{1,3},{2,0},{3,1},{4,6},{5,7},{6,4},{7,5},{8,10},{9,11},{10,... | collective-permute-start | bytes 2359304 | tf_op jit(solution)/shard_map/ppermute | solution.py:28
  149.1 12.3 %copy-start.4 = (bf16[1024,768]{1,0:T(8,128)(2,1)S(1)}, bf16[1024,768]{1,0:T(8,128)(2,1)}, u32[]{:S(2)}) copy-start(bf16[1024,768]{1,0:T(8,128)(2,1)} %copy-done.2) | copy-start | bytes 4718596
  149.1 12.3 %copy-start.17 = (f32[1024,768]{1,0:T(8,128)S(1)}, f32[1024,768]{1,0:T(8,128)}, u32[]{:S(2)}) copy-start(f32[1024,768]{1,0:T(8,128)} %copy-done.16) | copy-start | bytes 9437188
  149.2 12.2 %copy-start.24 = (bf16[1024,768]{1,0:T(8,128)(2,1)S(1)}, bf16[1024,768]{1,0:T(8,128)(2,1)}, u32[]{:S(2)}) copy-start(bf16[1024,768]{1,0:T(8,128)(2,1)} %copy-done.23) | copy-start | bytes 4718596
  149.2 12.2 %copy-start.37 = (bf16[768,768]{1,0:T(8,128)(2,1)S(1)}, bf16[768,768]{1,0:T(8,128)(2,1)}, u32[]{:S(2)}) copy-start(bf16[768,768]{1,0:T(8,128)(2,1)} %copy-done.36) | copy-start | bytes 3538948
  173.6 6.2 %collective-permute-start.23 = (bf16[272,1536]{1,0:T(8,128)(2,1)}, bf16[272,1536]{1,0:T(8,128)(2,1)}, u32[]{:S(2)}, u32[]{:S(2)}) collective-permute-start(bf16[272,1536]{1,0:T(8,128)(2,1)} %maximum_maximum_fusion.1), channel_id=1, source_target_pairs={{0,1},{1,0},{2,3},{3,2},{4,5},{5,4},{6,7},{7,6},{8,9},{9,8},{10,11... | collective-permute-start | bytes 2506760 | tf_op jit(solution)/shard_map/ppermute | solution.py:28
  175.6 30.9 %collective-permute-start.17 = (bf16[512,768]{1,0:T(8,128)(2,1)S(1)}, bf16[512,768]{1,0:T(8,128)(2,1)S(1)}, u32[]{:S(2)}, u32[]{:S(2)}) collective-permute-start(bf16[512,768]{1,0:T(8,128)(2,1)S(1)} %constant_dynamic-slice_fusion.1), channel_id=1, source_target_pairs={{0,4},{4,0},{8,12},{12,8},{16,20},{20,16},{24,28},{28,24},{1,5},{5... | collective-permute-start | bytes 2359304 | tf_op jit(solution)/shard_map/ppermute | solution.py:28
  178.1 28.5 %collective-permute-start.22 = (bf16[1,512,768]{2,1,0:T(8,128)(2,1)S(1)}, bf16[1,512,768]{2,1,0:T(8,128)(2,1)S(1)}, u32[]{:S(2)}, u32[]{:S(2)}) collective-permute-start(bf16[1,512,768]{2,1,0:T(8,128)(2,1)S(1)} %fusion.3), channel_id=1, source_target_pairs={{0,2},{1,3},{2,0},{3,1},{4,6},{5,7},{6,4},{7,5},{8,10},{9,11},{10,... | collective-permute-start | bytes 2359304 | tf_op jit(solution)/shard_map/ppermute | solution.py:28
  181.3 8.0 %copy-start.56 = (bf16[1024,768]{1,0:T(8,128)(2,1)S(1)}, bf16[1024,768]{1,0:T(8,128)(2,1)}, u32[]{:S(2)}) copy-start(bf16[1024,768]{1,0:T(8,128)(2,1)} %copy-done.55) | copy-start | bytes 4718596
  188.1 8.9 %collective-permute-start.25 = (bf16[2,256,512]{2,1,0:T(8,128)(2,1)S(1)}, bf16[2,256,512]{2,1,0:T(8,128)(2,1)S(1)}, u32[]{:S(2)}, u32[]{:S(2)}) collective-permute-start(bf16[2,256,512]{2,1,0:T(8,128)(2,1)S(1)} %slice.239), channel_id=1, source_target_pairs={{0,1},{1,0},{2,3},{3,2},{4,5},{5,4},{6,7},{7,6},{8,9},{9,8},{10,11... | collective-permute-start | bytes 1572872 | tf_op jit(solution)/shard_map/ppermute | solution.py:28
  188.7 17.9 %collective-permute-start.21 = (bf16[1,256,768]{2,1,0:T(8,128)(2,1)S(1)}, bf16[1,256,768]{2,1,0:T(8,128)(2,1)S(1)}, u32[]{:S(2)}, u32[]{:S(2)}) collective-permute-start(bf16[1,256,768]{2,1,0:T(8,128)(2,1)S(1)} %dynamic-slice_bitcast_fusion.2), channel_id=1, source_target_pairs={{0,4},{4,0},{8,12},{12,8},{16,20},{20,16},{24,28},{28,24},{1,5},{5... | collective-permute-start | bytes 1179656 | tf_op jit(solution)/shard_map/ppermute | solution.py:28
  189.4 9.1 %copy-start.41 = (f32[1024,768]{1,0:T(8,128)S(1)}, f32[1024,768]{1,0:T(8,128)}, u32[]{:S(2)}) copy-start(f32[1024,768]{1,0:T(8,128)} %copy-done.40) | copy-start | bytes 9437188
  189.4 9.1 %copy-start.54 = (bf16[3,768,768]{2,1,0:T(8,128)(2,1)S(1)}, bf16[3,768,768]{2,1,0:T(8,128)(2,1)}, u32[]{:S(2)}) copy-start(bf16[3,768,768]{2,1,0:T(8,128)(2,1)} %copy-done.53) | copy-start | bytes 10616836
  196.4 8.3 %collective-permute-start.24 = (bf16[2,768,768]{2,1,0:T(8,128)(2,1)S(1)}, bf16[2,768,768]{2,1,0:T(8,128)(2,1)S(1)}, u32[]{:S(2)}, u32[]{:S(2)}) collective-permute-start(bf16[2,768,768]{2,1,0:T(8,128)(2,1)S(1)} %get-tuple-element.212), channel_id=1, source_target_pairs={{0,1},{1,0},{2,3},{3,2},{4,5},{5,4},{6,7},{7,6},{8,9},{9,8},{10,11... | collective-permute-start | bytes 7077896 | tf_op jit(solution)/shard_map/ppermute | solution.py:28
  197.1 9.4 %collective-permute-start.26 = (bf16[1,256,512]{2,1,0:T(8,128)(2,1)S(1)}, bf16[1,256,512]{2,1,0:T(8,128)(2,1)S(1)}, u32[]{:S(2)}, u32[]{:S(2)}) collective-permute-start(bf16[1,256,512]{2,1,0:T(8,128)(2,1)S(1)} %slice.304), channel_id=1, source_target_pairs={{0,2},{1,3},{2,0},{3,1},{4,6},{5,7},{6,4},{7,5},{8,10},{9,11},{10,... | collective-permute-start | bytes 786440 | tf_op jit(solution)/shard_map/ppermute | solution.py:28
  209.2 32.9 %all-to-all-start.2 = ((bf16[4,192,768]{2,1,0:T(8,128)(2,1)}), bf16[4,192,768]{2,1,0:T(8,128)(2,1)}, u32[]{:S(2)}, u32[]{:S(2)}) async-start(bf16[4,192,768]{2,1,0:T(8,128)(2,1)} %pad_maximum_fusion.4), calls=%async_computation.2 | async-start | bytes 2359296 | tf_op jit(solution)/shard_map/all_to_all | solution.py:833
  213.9 31.9 %collective-permute-start.27 = (bf16[768,768]{1,0:T(8,128)(2,1)}, bf16[768,768]{1,0:T(8,128)(2,1)}, u32[]{:S(2)}, u32[]{:S(2)}) collective-permute-start(bf16[768,768]{1,0:T(8,128)(2,1)} %fusion.1), channel_id=1, source_target_pairs={{0,2},{1,3},{2,0},{3,1},{4,6},{5,7},{6,4},{7,5},{8,10},{9,11},{10,... | collective-permute-start | bytes 3538952 | tf_op jit(solution)/shard_map/ppermute | solution.py:28
  217.1 28.8 %copy-start.39 = (bf16[768,768]{1,0:T(8,128)(2,1)S(1)}, bf16[768,768]{1,0:T(8,128)(2,1)}, u32[]{:S(2)}) copy-start(bf16[768,768]{1,0:T(8,128)(2,1)} %copy-done.38) | copy-start | bytes 3538948
  217.1 28.7 %collective-permute-start.28 = (bf16[2,192,1024]{2,1,0:T(8,128)(2,1)}, bf16[2,192,1024]{2,1,0:T(8,128)(2,1)}, u32[]{:S(2)}, u32[]{:S(2)}) collective-permute-start(bf16[2,192,1024]{2,1,0:T(8,128)(2,1)} %pad_maximum_fusion.6), channel_id=1, source_target_pairs={{0,1},{1,0},{2,3},{3,2},{4,5},{5,4},{6,7},{7,6},{8,9},{9,8},{10,11... | collective-permute-start | bytes 2359304 | tf_op jit(solution)/shard_map/ppermute | solution.py:28
  242.1 25.5 %all-to-all-start.3 = ((bf16[8,48,512]{2,1,0:T(8,128)(2,1)}), bf16[8,48,512]{2,1,0:T(8,128)(2,1)S(1)}, u32[]{:S(2)}, u32[]{:S(2)}) async-start(bf16[8,48,512]{2,1,0:T(8,128)(2,1)} %bitcast.186), calls=%async_computation.3 | async-start | bytes 786432 | tf_op jit(solution)/shard_map/all_to_all | solution.py:668
  248.0 18.0 %collective-permute-start.33 = (bf16[1,384,768]{2,1,0:T(8,128)(2,1)S(1)}, bf16[1,384,768]{2,1,0:T(8,128)(2,1)S(1)}, u32[]{:S(2)}, u32[]{:S(2)}) collective-permute-start(bf16[1,384,768]{2,1,0:T(8,128)(2,1)S(1)} %dynamic-slice_bitcast_fusion.1), channel_id=1, source_target_pairs={{0,4},{4,0},{8,12},{12,8},{16,20},{20,16},{24,28},{28,24},{1,5},{5... | collective-permute-start | bytes 1769480 | tf_op jit(solution)/shard_map/ppermute | solution.py:28
  251.4 24.5 %collective-permute-start.32 = (bf16[2,192,1024]{2,1,0:T(8,128)(2,1)}, bf16[2,192,1024]{2,1,0:T(8,128)(2,1)}, u32[]{:S(2)}, u32[]{:S(2)}) collective-permute-start(bf16[2,192,1024]{2,1,0:T(8,128)(2,1)} %pad_maximum_fusion.7), channel_id=1, source_target_pairs={{0,2},{1,3},{2,0},{3,1},{4,6},{5,7},{6,4},{7,5},{8,10},{9,11},{10,... | collective-permute-start | bytes 2359304 | tf_op jit(solution)/shard_map/ppermute | solution.py:28
  253.5 14.1 %copy-start.63 = (bf16[768,768]{1,0:T(8,128)(2,1)S(1)}, bf16[768,768]{1,0:T(8,128)(2,1)}, u32[]{:S(2)}) copy-start(bf16[768,768]{1,0:T(8,128)(2,1)} %copy-done.62) | copy-start | bytes 3538948
  255.0 18.5 %collective-permute-start.29 = (bf16[192,768]{1,0:T(8,128)(2,1)S(1)}, bf16[192,768]{1,0:T(8,128)(2,1)S(1)}, u32[]{:S(2)}, u32[]{:S(2)}) collective-permute-start(bf16[192,768]{1,0:T(8,128)(2,1)S(1)} %fusion.8), channel_id=1, source_target_pairs={{0,8},{4,12},{8,0},{12,4},{16,24},{20,28},{24,16},{28,20},{1,9},{5... | collective-permute-start | bytes 884744 | tf_op jit(solution)/shard_map/ppermute | solution.py:28
  256.3 17.3 %collective-permute-start.30 = (bf16[192,768]{1,0:T(8,128)(2,1)S(1)}, bf16[192,768]{1,0:T(8,128)(2,1)}, u32[]{:S(2)}, u32[]{:S(2)}) collective-permute-start(bf16[192,768]{1,0:T(8,128)(2,1)S(1)} %fusion.8), channel_id=1, source_target_pairs={{0,16},{4,20},{8,24},{12,28},{16,0},{20,4},{24,8},{28,12},{1,17},{... | collective-permute-start | bytes 884744 | tf_op jit(solution)/shard_map/ppermute | solution.py:28
  258.4 17.5 %collective-permute-start.31 = (bf16[192,768]{1,0:T(8,128)(2,1)S(1)}, bf16[192,768]{1,0:T(8,128)(2,1)}, u32[]{:S(2)}, u32[]{:S(2)}) collective-permute-start(bf16[192,768]{1,0:T(8,128)(2,1)S(1)} %fusion.8), channel_id=1, source_target_pairs={{0,24},{4,28},{8,16},{12,20},{16,8},{20,12},{24,0},{28,4},{1,25},{... | collective-permute-start | bytes 884744 | tf_op jit(solution)/shard_map/ppermute | solution.py:28
  266.8 16.2 %collective-permute-start.35 = (bf16[2,192,1024]{2,1,0:T(8,128)(2,1)}, bf16[2,192,1024]{2,1,0:T(8,128)(2,1)}, u32[]{:S(2)}, u32[]{:S(2)}) collective-permute-start(bf16[2,192,1024]{2,1,0:T(8,128)(2,1)} %pad_maximum_fusion.8), channel_id=1, source_target_pairs={{0,1},{1,0},{2,3},{3,2},{4,5},{5,4},{6,7},{7,6},{8,9},{9,8},{10,11... | collective-permute-start | bytes 2359304 | tf_op jit(solution)/shard_map/ppermute | solution.py:28
  269.6 24.9 %all-to-all-start.4 = ((bf16[4,1,96,768]{3,2,1,0:T(8,128)(2,1)}), bf16[4,1,96,768]{3,2,1,0:T(8,128)(2,1)S(1)}, u32[]{:S(2)}, u32[]{:S(2)}) async-start(bf16[4,1,96,768]{3,2,1,0:T(8,128)(2,1)} %bitcast.34), calls=%async_computation.4 | async-start | bytes 1179648 | tf_op jit(solution)/shard_map/all_to_all | solution.py:637
  282.4 16.9 %copy-start.69 = (bf16[192,1024]{1,0:T(8,128)(2,1)S(1)}, bf16[192,1024]{1,0:T(8,128)(2,1)}, u32[]{:S(2)}) copy-start(bf16[192,1024]{1,0:T(8,128)(2,1)} %get-tuple-element.273) | copy-start | bytes 1179652
  282.4 16.9 %copy-start.70 = (bf16[192,1024]{1,0:T(8,128)(2,1)S(1)}, bf16[192,1024]{1,0:T(8,128)(2,1)}, u32[]{:S(2)}) copy-start(bf16[192,1024]{1,0:T(8,128)(2,1)} %get-tuple-element.274) | copy-start | bytes 1179652
  282.4 21.1 %collective-permute-start.34 = (bf16[768,768]{1,0:T(8,128)(2,1)}, bf16[768,768]{1,0:T(8,128)(2,1)}, u32[]{:S(2)}, u32[]{:S(2)}) collective-permute-start(bf16[768,768]{1,0:T(8,128)(2,1)} %slice_dynamic-update-slice_fusion), channel_id=1, source_target_pairs={{0,4},{4,0},{8,12},{12,8},{16,20},{20,16},{24,28},{28,24},{1,5},{5... | collective-permute-start | bytes 3538952 | tf_op jit(solution)/shard_map/ppermute | solution.py:28
  295.5 13.7 %all-to-all-start.5 = ((bf16[4,1,96,768]{3,2,1,0:T(8,128)(2,1)}), bf16[4,1,96,768]{3,2,1,0:T(8,128)(2,1)S(1)}, u32[]{:S(2)}, u32[]{:S(2)}) async-start(bf16[4,1,96,768]{3,2,1,0:T(8,128)(2,1)} %broadcast_in_dim.7), calls=%async_computation.5 | async-start | bytes 1179648 | tf_op jit(solution)/shard_map/all_to_all | solution.py:655
  303.1 23.7 %collective-permute-start.37 = (bf16[2,192,1024]{2,1,0:T(8,128)(2,1)S(1)}, bf16[2,192,1024]{2,1,0:T(8,128)(2,1)}, u32[]{:S(2)}, u32[]{:S(2)}) collective-permute-start(bf16[2,192,1024]{2,1,0:T(8,128)(2,1)S(1)} %pad_maximum_fusion.9), channel_id=1, source_target_pairs={{0,2},{1,3},{2,0},{3,1},{4,6},{5,7},{6,4},{7,5},{8,10},{9,11},{10,... | collective-permute-start | bytes 2359304 | tf_op jit(solution)/shard_map/ppermute | solution.py:28
  310.0 19.0 %all-to-all-start.6 = ((bf16[8,48,512]{2,1,0:T(8,128)(2,1)}), bf16[8,48,512]{2,1,0:T(8,128)(2,1)S(1)}, u32[]{:S(2)}, u32[]{:S(2)}) async-start(bf16[8,48,512]{2,1,0:T(8,128)(2,1)} %broadcast_in_dim.8), calls=%async_computation.6 | async-start | bytes 786432 | tf_op jit(solution)/shard_map/all_to_all | solution.py:680
  325.4 12.6 %collective-permute-start.36 = (bf16[1,384,768]{2,1,0:T(8,128)(2,1)S(1)}, bf16[1,384,768]{2,1,0:T(8,128)(2,1)S(1)}, u32[]{:S(2)}, u32[]{:S(2)}) collective-permute-start(bf16[1,384,768]{2,1,0:T(8,128)(2,1)S(1)} %bitcast.181), channel_id=1, source_target_pairs={{0,4},{4,0},{8,12},{12,8},{16,20},{20,16},{24,28},{28,24},{1,5},{5... | collective-permute-start | bytes 1769480 | tf_op jit(solution)/shard_map/ppermute | solution.py:28
  329.0 9.0 %collective-permute-start.38 = (bf16[384,512]{1,0:T(8,128)(2,1)S(1)}, bf16[384,512]{1,0:T(8,128)(2,1)S(1)}, u32[]{:S(2)}, u32[]{:S(2)}) collective-permute-start(bf16[384,512]{1,0:T(8,128)(2,1)S(1)} %bitcast.178), channel_id=1, source_target_pairs={{0,2},{1,3},{2,0},{3,1},{4,6},{5,7},{6,4},{7,5},{8,10},{9,11},{10,... | collective-permute-start | bytes 1179656 | tf_op jit(solution)/shard_map/ppermute | solution.py:28
  338.1 9.3 %collective-permute-start.39 = (bf16[2,384,512]{2,1,0:T(8,128)(2,1)S(1)}, bf16[2,384,512]{2,1,0:T(8,128)(2,1)S(1)}, u32[]{:S(2)}, u32[]{:S(2)}) collective-permute-start(bf16[2,384,512]{2,1,0:T(8,128)(2,1)S(1)} %pad_maximum_fusion.10), channel_id=1, source_target_pairs={{0,1},{1,0},{2,3},{3,2},{4,5},{5,4},{6,7},{7,6},{8,9},{9,8},{10,11... | collective-permute-start | bytes 2359304 | tf_op jit(solution)/shard_map/ppermute | solution.py:28
  (75 other events, 235.5 us)
